TPU v7x, 256 devices: a whole 4x4x8 slice. The times are simulated.
256 devices in a mesh: row: 32 (over x, z), col: 8 (over y, core).
Axes of the slice: x: 4, y: 4, z: 8, core: 2. Of those that a mesh axis runs over, the one named last changes fastest.
Arguments:
- panel: float32 [32768, 256], P('row', 'col'), as said below
- trailing: bfloat16 [32768, 16384], P('row', 'col'), may hold values from -6 to 6
Outputs:
- r_factor: float32 [256, 256], replicated
- top_rows: float32 [256, 16384], P(None, 'col')
- updated: bfloat16 [32768, 16384], P('row', 'col')
Inputs may be any that keep to these rules, and one draw needn't show every extreme that they name: The panel has full column rank, its columns of differing scales.
All inputs are finite; a program needn't handle non-finite values.
Results may differ from a plain program's by a relative error of at most 0.0025.
Values sent between devices are 32-bit elements; how exact they have to be, the bound alone decides.
No kernel may reach another device: no remote copies, remote signals or barrier semaphores. Data moves between devices by JAX's collectives and lax.ppermute only.
A program may use at most 64 MiB of HBM per device.

v0:
```python
import jax
import jax.numpy as jnp
from jax import lax
from jax.sharding import PartitionSpec as P


def partner_2(block, axis, apart):
    count = lax.axis_size(axis)
    route = []
    for low in range(count):
        high = low | 1 << apart
        if high != low and high < count:
            route += [(low, high), (high, low)]
    return lax.ppermute(block, axis, route)


def local(panel, trailing):
    highest = lax.Precision.HIGHEST
    whole = lax.all_gather(panel, "col", axis=1, tiled=True)
    local_gram = jnp.dot(whole.T, whole, precision=highest, preferred_element_type=jnp.float32)
    gram_sum = local_gram
    levels = lax.axis_size("row").bit_length() - 1
    for level in range(levels):
        partner = partner_2(gram_sum, "row", level)
        gram_sum = gram_sum + partner
    lower = jnp.linalg.cholesky(gram_sum)
    basis = jax.scipy.linalg.solve_triangular(lower, whole.T, lower=True).T
    top_rows = lax.psum(
        jnp.dot(basis.T, trailing, precision=highest, preferred_element_type=jnp.float32), "row"
    )
    update = jnp.dot(
        basis.astype(jnp.bfloat16),
        top_rows.astype(jnp.bfloat16),
        preferred_element_type=jnp.float32,
    )
    updated = (trailing.astype(jnp.float32) - update).astype(jnp.bfloat16)
    return (lower.T, top_rows, updated)


def solution(mesh):
    return jax.shard_map(
        local,
        mesh=mesh,
        in_specs=(P("row", "col"), P("row", "col")),
        out_specs=(P(), P(None, "col"), P("row", "col")),
        check_vma=False,
    )
```

profile of v0, /device:TPU:1, one launch (start us, length us, event | category | flops | bytes accessed | tf_op | source)
XLA Modules:
  0.0 330.1 jit_solution(2958663262399651897)
XLA Ops:
  7.2 0.7 all-gather.2.cloned.1.call-update
  7.9 32.1 %all-gather.2.cloned.1.call-done = f32[1024,256]{0,1:T(8,128)} async-done(((f32[1024,32]{0,1:T(8,128)}), f32[1024,256]{0,1:T(8,128)}) %all-gather.2.cloned.1.call-update) | async-done | bytes 1048592 | tf_op jit(solution)/shard_map/all_gather | solution.py:19
  40.1 2.6 fusion.17
  42.7 1.4 collective-permute-start
  44.0 6.4 %collective-permute-done = f32[256,256]{0,1:T(8,128)S(1)} collective-permute-done((f32[256,256]{0,1:T(8,128)S(1)}, f32[256,256]{0,1:T(8,128)S(1)}, u32[]{:S(2)}, u32[]{:S(2)}) %collective-permute-start) | collective-permute-done | bytes 262176 | tf_op jit(solution)/shard_map/ppermute | solution.py:14
  50.5 2.3 collective-permute-start.1
  52.8 11.4 %collective-permute-done.1 = f32[256,256]{0,1:T(8,128)S(1)} collective-permute-done((f32[256,256]{0,1:T(8,128)S(1)}, f32[256,256]{0,1:T(8,128)S(1)}, u32[]{:S(2)}, u32[]{:S(2)}) %collective-permute-start.1) | collective-permute-done | bytes 262176 | tf_op jit(solution)/shard_map/ppermute | solution.py:14
  64.3 6.5 %collective-permute-start.2 = (f32[256,256]{0,1:T(8,128)S(1)}, f32[256,256]{0,1:T(8,128)S(1)}, u32[]{:S(2)}, u32[]{:S(2)}) collective-permute-start(f32[256,256]{0,1:T(8,128)S(1)} %add.41), channel_id=1, source_target_pairs={{0,32},{32,0},{8,40},{40,8},{16,48},{48,16},{24,56},{56,24},{64,96... | collective-permute-start | bytes 786440 | tf_op jit(solution)/shard_map/ppermute | solution.py:14
  70.8 8.8 %collective-permute-done.2 = f32[256,256]{0,1:T(8,128)S(1)} collective-permute-done((f32[256,256]{0,1:T(8,128)S(1)}, f32[256,256]{0,1:T(8,128)S(1)}, u32[]{:S(2)}, u32[]{:S(2)}) %collective-permute-start.2) | collective-permute-done | bytes 262176 | tf_op jit(solution)/shard_map/ppermute | solution.py:14
  79.6 1.3 collective-permute-start.3
  81.0 4.0 %collective-permute-done.3 = f32[256,256]{0,1:T(8,128)S(1)} collective-permute-done((f32[256,256]{0,1:T(8,128)S(1)}, f32[256,256]{0,1:T(8,128)S(1)}, u32[]{:S(2)}, u32[]{:S(2)}) %collective-permute-start.3) | collective-permute-done | bytes 262176 | tf_op jit(solution)/shard_map/ppermute | solution.py:14
  85.0 3.0 collective-permute-start.4
  88.0 6.5 %collective-permute-done.4 = f32[256,256]{0,1:T(8,128)S(1)} collective-permute-done((f32[256,256]{0,1:T(8,128)S(1)}, f32[256,256]{0,1:T(8,128)S(1)}, u32[]{:S(2)}, u32[]{:S(2)}) %collective-permute-start.4) | collective-permute-done | bytes 262176 | tf_op jit(solution)/shard_map/ppermute | solution.py:14
  94.6 11.7 %cholesky.50 = f32[128,128]{1,0:T(8,128)S(1)} custom-call(f32[128,128]{1,0:T(8,128)S(1)} %cholesky.118), custom_call_target="Cholesky" | custom-call | tf_op jit(solution)/shard_map/jit(cholesky)/cholesky | solution.py:26
  106.4 9.8 %custom-call.15 = f32[1,128,128]{1,2,0:T(8,128)S(1)} custom-call(f32[1,128,128]{2,1,0:T(8,128)S(1)} %get-tuple-element.29), custom_call_target="InvertDiagBlocksLowerTriangular" | custom-call | tf_op jit(solution)/shard_map/jit(cholesky)/cholesky | solution.py:26
  116.5 0.3 slice_subtract_fusion
  116.7 11.7 %cholesky.105 = f32[128,128]{1,0:T(8,128)S(1)} custom-call(f32[128,128]{1,0:T(8,128)S(1)} %slice_subtract_fusion), custom_call_target="Cholesky" | custom-call | tf_op jit(solution)/shard_map/jit(cholesky)/cholesky | solution.py:26
  128.5 0.6 compare_reduce_fusion
  130.5 4.2 %while.1 = (s32[]{:T(128)}, f32[256,256]{1,0:T(8,128)S(1)}, s32[2,2]{1,0:T(2,128)S(1)}, f32[2,128,128]{2,1,0:T(8,128)S(1)}, s32[]{:T(128)}) while((s32[]{:T(128)}, f32[256,256]{1,0:T(8,128)S(1)}, s32[2,2]{1,0:T(2,128)S(1)}, f32[2,128,128]{2,1,0:T(8,128)S(1)}, s32[]{:T(128)}) %tuple.29), condition=%wide.while_cond, body=%wide.while_body.sunk | while | flops 2 | bytes 131189 | solution.py:27
  130.7 0.6 fusion.26
  131.3 1.4 bitcast_dynamic-update-slice_fusion.2
  132.7 0.6 fusion.26
  133.3 1.4 bitcast_dynamic-update-slice_fusion.2
  134.7 19.7 %custom-call.16 = f32[2,128,128]{1,2,0:T(8,128)S(1)} custom-call(f32[2,128,128]{2,1,0:T(8,128)S(1)} %get-tuple-element.10), custom_call_target="InvertDiagBlocksLowerTriangular" | custom-call | tf_op jit(solution)/shard_map/jit(_solve_triangular)/triangular_solve | solution.py:27
  154.4 0.6 fusion.4
  155.0 0.6 convolution_subtract_fusion
  155.6 0.6 fusion.10
  156.3 6.9 %fusion.2 = f32[256,2048]{1,0:T(8,128)} fusion(bf16[1024,2048]{1,0:T(8,128)(2,1)} %param.3, f32[128,1024]{1,0:T(8,128)S(1)} %fusion.10, f32[128,1024]{1,0:T(8,128)S(1)} %fusion.4), kind=kOutput, calls=%fused_computation.7 | convolution fusion | flops 6442713088 | bytes 7340032 | tf_op jit(solution)/shard_map/dot_general | solution.py:29
  163.2 0.8 copy.8
  164.1 151.6 %all-reduce.3.cloned.1.call-done = f32[256,2048]{1,0:T(8,128)} async-done(((f32[256,2048]{1,0:T(8,128)}), f32[256,2048]{1,0:T(8,128)}) %all-reduce.3.cloned.1.call-update) | async-done | bytes 2097168 | tf_op jit(solution)/shard_map/psum | solution.py:28
  315.6 6.3 %subtract_convert_fusion = bf16[1024,2048]{1,0:T(8,128)(2,1)} fusion(bf16[1024,2048]{1,0:T(8,128)(2,1)} %param.3, f32[256,2048]{1,0:T(8,128)} %all-reduce.3.cloned.1.call-done, f32[128,1024]{1,0:T(8,128)S(1)} %fusion.10, f32[128,1024]{1,0:T(8,128)S(1)} %fusion.4), kind=kOutput, calls=%fused_computation.2 | convolution fusion | flops 1081606144 | bytes 11534336 | tf_op jit(solution)/shard_map/dot_general | solution.py:31
  321.9 1.3 copy.22
  (25 shorter events, 0.9 us)
Async XLA Ops:
  7.2 32.9 %all-gather.2.cloned.1.call-start = ((), (), s32[]{:S(2)}) async-start(), calls=%async_computation | async-start | bytes 1179648 | tf_op jit(solution)/shard_map/all_gather | solution.py:19
  7.9 307.7 %all-reduce.3.cloned.1.call-start = ((), (), s32[]{:S(2)}) async-start(), calls=%async_computation.1 | async-start | bytes 4194304 | tf_op jit(solution)/shard_map/psum | solution.py:28
  42.7 111.7 %copy-start = (f32[1024,256]{0,1:T(8,128)S(1)}, f32[1024,256]{0,1:T(8,128)}, u32[]{:S(2)}) copy-start(f32[1024,256]{0,1:T(8,128)} %all-gather.2.cloned.1.call-done) | copy-start | bytes 3145732
  42.7 7.8 %collective-permute-start = (f32[256,256]{0,1:T(8,128)S(1)}, f32[256,256]{0,1:T(8,128)S(1)}, u32[]{:S(2)}, u32[]{:S(2)}) collective-permute-start(f32[256,256]{0,1:T(8,128)S(1)} %fusion.17), channel_id=1, source_target_pairs={{0,8},{8,0},{16,24},{24,16},{32,40},{40,32},{48,56},{56,48},{64,72... | collective-permute-start | bytes 786440 | tf_op jit(solution)/shard_map/ppermute | solution.py:14
  50.5 13.8 %collective-permute-start.1 = (f32[256,256]{0,1:T(8,128)S(1)}, f32[256,256]{0,1:T(8,128)S(1)}, u32[]{:S(2)}, u32[]{:S(2)}) collective-permute-start(f32[256,256]{0,1:T(8,128)S(1)} %add.40), channel_id=1, source_target_pairs={{0,16},{16,0},{8,24},{24,8},{32,48},{48,32},{40,56},{56,40},{64,80... | collective-permute-start | bytes 786440 | tf_op jit(solution)/shard_map/ppermute | solution.py:14
  64.3 15.3 %collective-permute-start.2 = (f32[256,256]{0,1:T(8,128)S(1)}, f32[256,256]{0,1:T(8,128)S(1)}, u32[]{:S(2)}, u32[]{:S(2)}) collective-permute-start(f32[256,256]{0,1:T(8,128)S(1)} %add.41), channel_id=1, source_target_pairs={{0,32},{32,0},{8,40},{40,8},{16,48},{48,16},{24,56},{56,24},{64,96... | collective-permute-start | bytes 786440 | tf_op jit(solution)/shard_map/ppermute | solution.py:14
  79.6 5.3 %collective-permute-start.3 = (f32[256,256]{0,1:T(8,128)S(1)}, f32[256,256]{0,1:T(8,128)S(1)}, u32[]{:S(2)}, u32[]{:S(2)}) collective-permute-start(f32[256,256]{0,1:T(8,128)S(1)} %add.42), channel_id=1, source_target_pairs={{0,64},{64,0},{8,72},{72,8},{16,80},{80,16},{24,88},{88,24},{32,96... | collective-permute-start | bytes 786440 | tf_op jit(solution)/shard_map/ppermute | solution.py:14
  85.0 9.4 %collective-permute-start.4 = (f32[256,256]{0,1:T(8,128)S(1)}, f32[256,256]{0,1:T(8,128)S(1)}, u32[]{:S(2)}, u32[]{:S(2)}) collective-permute-start(f32[256,256]{0,1:T(8,128)S(1)} %add.43), channel_id=1, source_target_pairs={{0,128},{128,0},{8,136},{136,8},{16,144},{144,16},{24,152},{152,24... | collective-permute-start | bytes 786440 | tf_op jit(solution)/shard_map/ppermute | solution.py:14
  315.6 6.3 %copy-start.1 = (f32[256,2048]{1,0:T(8,128)S(1)}, f32[256,2048]{1,0:T(8,128)}, u32[]{:S(2)}) copy-start(f32[256,2048]{1,0:T(8,128)} %all-reduce.3.cloned.1.call-done) | copy-start | bytes 6291460
Sparse Core Ops, SparseCore 0:
  9.9 30.1 all-gather.1
  163.3 152.2 all-reduce.2
where the time goes:
time: 334 us; the launch traced here: 330 us
  waiting for transfers between devices  221 us (66%)
  other arithmetic  53.9 us (16%)
  matrix products  18.1 us (5%)
  between operations  15.5 us (5%)
  starting transfers between devices  14.6 us (4%)
  local copies, waits for them, and re-layouts  6.34 us (2%)
    psum x1, waiting for transfers between devices, local(): lax.psum(jnp.dot(basis.T, trailing, precision=highest, preferred_element_...  152 us
    ppermute x5, waiting for transfers between devices, partner_2(): return lax.ppermute(block, axis, route)  37.1 us
    another operation x6, other arithmetic, local(): lower = jnp.linalg.cholesky(gram_sum)  34 us
    all_gather x1, waiting for transfers between devices, local(): whole = lax.all_gather(panel, 'col', axis=1, tiled=True)  32.1 us
    another operation x3, other arithmetic, local(): basis = jax.scipy.linalg.solve_triangular(lower, whole.T, lower=True).T  19.7 us
    ppermute x5, starting transfers between devices, partner_2(): return lax.ppermute(block, axis, route)  14.5 us
    dot_general x1, matrix products, local(): jnp.dot(basis.T, trailing, precision=highest, preferred_element_type=jnp....  6.94 us
  transfers between devices with their start and end apart: 7, of which 7 were waited for; matrix products, arithmetic and copies ran while one was open for 0% of the time, Pallas kernels for 0%

commit v1 on v0

v1 whole, which is shorter than its diff:
```python
import jax
import jax.numpy as jnp
from jax import lax
from jax.experimental import pallas as pl
from jax.experimental.pallas import tpu as pltpu
from jax.sharding import PartitionSpec as P

F32 = jnp.float32
BF16 = jnp.bfloat16
HIGHEST = lax.Precision.HIGHEST
NX, NZ = 4, 8
B, ROWS, COLS, HALF = 256, 1024, 2048, 128

X_GROUPS = [[x * NZ + z for x in range(NX)] for z in range(NZ)]
Z_GROUPS = [[x * NZ + z for z in range(NZ)] for x in range(NX)]
Y_GROUPS = [[2 * y + core for y in range(4)] for core in range(2)]
SIBLING = [(c, c ^ 1) for c in range(8)]


def dot(a, b, contract, precision=None):
    return lax.dot_general(a, b, (contract, ((), ())), precision=precision, preferred_element_type=F32)


def product_kernel(core_ref, mine_ref, other_ref, trailing_ref, panel_t_ref, out_ref, parts):
    first = core_ref[0] == 0
    for y in range(4):
        mine, other = mine_ref[y], other_ref[y]
        panel_t_ref[64 * y:64 * y + 32] = jnp.where(first, mine, other)
        panel_t_ref[64 * y + 32:64 * y + 64] = jnp.where(first, other, mine)
    value = panel_t_ref[...]
    high = value.astype(BF16)
    rest = value - high.astype(F32)
    middle = rest.astype(BF16)
    parts[0:B] = high
    parts[B:2 * B] = middle
    parts[2 * B:] = (rest - middle.astype(F32)).astype(BF16)
    half = panel_t_ref[pl.ds(pl.multiple_of(core_ref[0] * HALF, HALF), HALF)]
    out_ref[:, COLS:] = dot(value, half, ((1,), (1,)), HIGHEST)

    @pl.loop(0, COLS // 256)
    def _(tile):
        columns = pl.ds(pl.multiple_of(tile * 256, 256), 256)
        block = trailing_ref[:, columns]
        total = dot(parts[2 * B:], block, ((1,), (0,)))
        total += dot(parts[B:2 * B], block, ((1,), (0,)))
        out_ref[:, columns] = total + dot(parts[0:B], block, ((1,), (0,)))


def eliminate(work, upper, inverse):
    n = HALF
    row = lax.broadcasted_iota(jnp.int32, (n, 1), 0)
    eight = lax.broadcasted_iota(jnp.int32, (8, 1), 0)
    lane = lax.broadcasted_iota(jnp.int32, (n, n), 1)
    inverse[...] = (lane == lax.broadcasted_iota(jnp.int32, (n, n), 0)).astype(F32)

    @pl.loop(0, n // 8)
    def _(block):
        base = pl.multiple_of(block * 8, 8)
        s = work[...]
        m = inverse[...]
        pivots = jnp.zeros((8, 1), F32)
        for k in range(8):
            pivot_s = jnp.sum(jnp.where(row == base + k, s, 0.0), axis=0, keepdims=True)
            pivot_m = jnp.sum(jnp.where(row == base + k, m, 0.0), axis=0, keepdims=True)
            pivot = pivot_s[:, k:k + 1]
            factor = jnp.where(row > base + k, s[:, k:k + 1] / pivot, 0.0)
            s = s - factor * pivot_s
            m = m - factor * pivot_m
            pivots = jnp.where(eight == k, pivot, pivots)
        work[...] = s
        inverse[...] = m
        scale = lax.rsqrt(pivots)
        scale = scale * (1.5 - 0.5 * pivots * scale * scale)
        inverse[pl.ds(base, 8)] = inverse[pl.ds(base, 8)] * scale
        upper[pl.ds(base, 8)] = pltpu.roll(work[pl.ds(base, 8)] * scale, base, 1)
        work[...] = pltpu.roll(work[...], n - 8, 1)

    inv = inverse[...]
    up = upper[...]
    sub = lax.broadcasted_iota(jnp.int32, (n, n), 0)
    upper[...] = jnp.where(lane >= sub, up, 0.0)
    inverse[...] = jnp.where(lane <= sub, inv, 0.0)


def factor_kernel(core_ref, mine_ref, other_ref, panel_t_ref, r_ref, inv_ref, low_ref, work, upper, inverse):
    first = core_ref[0] == 0
    mine, other = mine_ref[...], other_ref[...]
    left = jnp.where(first, mine, other)
    right = jnp.where(first, other, mine)
    work[...] = left[:HALF]
    eliminate(work, upper, inverse)
    r_ref[:HALF, :HALF] = upper[...]
    inv_ref[:HALF, :HALF] = inverse[...]
    inv_ref[:HALF, HALF:] = jnp.zeros((HALF, HALF), F32)
    r_ref[HALF:, :HALF] = jnp.zeros((HALF, HALF), F32)
    cross = dot(inverse[...], right[:HALF], ((1,), (0,)), HIGHEST)
    r_ref[:HALF, HALF:] = cross
    work[...] = right[HALF:] - dot(cross, cross, ((0,), (0,)), HIGHEST)
    eliminate(work, upper, inverse)
    r_ref[HALF:, HALF:] = upper[...]
    inv_ref[HALF:, HALF:] = inverse[...]
    lower = dot(cross, inv_ref[:HALF, :HALF], ((0,), (0,)), HIGHEST)
    inv_ref[HALF:, :HALF] = -dot(inverse[...], lower, ((1,), (0,)), HIGHEST)
    basis = dot(panel_t_ref[...], inv_ref[...], ((0,), (1,)), HIGHEST)
    low_ref[...] = basis.astype(BF16)


def update_kernel(sums_ref, inv_ref, low_ref, trailing_ref, top_ref, updated_ref):
    top = dot(inv_ref[...], sums_ref[...], ((1,), (0,)), HIGHEST)
    top_ref[...] = top
    change = dot(low_ref[...], top.astype(BF16), ((1,), (0,)))
    updated_ref[...] = (trailing_ref[...].astype(F32) - change).astype(BF16)


VMEM = pl.BlockSpec(memory_space=pltpu.VMEM)
SMEM = pl.BlockSpec(memory_space=pltpu.SMEM)


def cost(flops, size):
    return pl.CostEstimate(flops=int(flops), bytes_accessed=int(size), transcendentals=0)


def swap(block, axis, groups):
    return lax.all_to_all(block, axis, 0, 0, tiled=True, axis_index_groups=groups)


def gather(block, axis, groups):
    count = len(groups[0])
    return swap(jnp.concatenate([block] * count, axis=0), axis, groups)


def scatter_sum(block, axis, groups):
    count = len(groups[0])
    received = swap(block, axis, groups)
    return jnp.sum(received.reshape((count, -1) + block.shape[1:]), axis=0)


def local(panel, trailing):
    core = (lax.axis_index("col") % 2).astype(jnp.int32).reshape(1)
    params = pltpu.CompilerParams(vmem_limit_bytes=48 * 2**20)
    with jax.named_scope("gather_panel"):
        mine = gather(panel.T, "col", Y_GROUPS)
        other = lax.ppermute(mine, "col", SIBLING)
    with jax.named_scope("product"):
        panel_t, sums = pl.pallas_call(
            product_kernel,
            out_shape=(jax.ShapeDtypeStruct((B, ROWS), F32), jax.ShapeDtypeStruct((B, COLS + HALF), F32)),
            in_specs=[SMEM, VMEM, VMEM, VMEM],
            out_specs=(VMEM, VMEM),
            scratch_shapes=[pltpu.VMEM((3 * B, ROWS), BF16)],
            compiler_params=params,
            cost_estimate=cost(3.6e9, 8e6),
        )(core, mine.reshape(4, 32, ROWS), other.reshape(4, 32, ROWS), trailing)
    with jax.named_scope("sum_over_x"):
        sums = scatter_sum(sums, "row", X_GROUPS)
    with jax.named_scope("sum_over_z"):
        sums = scatter_sum(sums, "row", Z_GROUPS)
    with jax.named_scope("gather_gram"):
        gram_mine = gather(gather(sums[:, COLS:], "row", Z_GROUPS), "row", X_GROUPS)
        gram_other = lax.ppermute(gram_mine, "col", SIBLING)
    with jax.named_scope("gather_sums"):
        sums = gather(gather(sums[:, :COLS], "row", Z_GROUPS), "row", X_GROUPS)
    with jax.named_scope("factor"):
        r_factor, inverse, low = pl.pallas_call(
            factor_kernel,
            out_shape=(
                jax.ShapeDtypeStruct((B, B), F32),
                jax.ShapeDtypeStruct((B, B), F32),
                jax.ShapeDtypeStruct((ROWS, B), BF16),
            ),
            in_specs=[SMEM, VMEM, VMEM, VMEM],
            out_specs=(VMEM, VMEM, VMEM),
            scratch_shapes=[pltpu.VMEM((HALF, HALF), F32)] * 3,
            compiler_params=params,
            cost_estimate=cost(2e10, 3e6),
        )(core, gram_mine, gram_other, panel_t)
    with jax.named_scope("update"):
        tile = 256
        top, updated = pl.pallas_call(
            update_kernel,
            grid=(COLS // tile,),
            out_shape=(jax.ShapeDtypeStruct((B, COLS), F32), jax.ShapeDtypeStruct((ROWS, COLS), BF16)),
            in_specs=[
                pl.BlockSpec((B, tile), lambda i: (0, i)),
                pl.BlockSpec((B, B), lambda i: (0, 0)),
                pl.BlockSpec((ROWS, B), lambda i: (0, 0)),
                pl.BlockSpec((ROWS, tile), lambda i: (0, i)),
            ],
            out_specs=(
                pl.BlockSpec((B, tile), lambda i: (0, i)),
                pl.BlockSpec((ROWS, tile), lambda i: (0, i)),
            ),
            compiler_params=params,
            cost_estimate=cost(3e9, 12e6),
        )(sums, inverse, low, trailing)
    return r_factor, top, updated


def solution(mesh):
    return jax.shard_map(
        local,
        mesh=mesh,
        in_specs=(P("row", "col"), P("row", "col")),
        out_specs=(P(), P(None, "col"), P("row", "col")),
        check_vma=False,
    )
```

time: 334 us -> 180 us (0.54)
  the two profiles are of different devices: /device:TPU:1 before, /device:TPU:2 now
where the time goes in v1:
time: 180 us; the launch traced here: 179 us
  blocking collectives  70.2 us (39%)
  Pallas kernels  52.6 us (29%)
  waiting for transfers between devices  23 us (13%)
  starting transfers between devices  16.7 us (9%)
  local copies, waits for them, and re-layouts  12 us (7%)
  other arithmetic  3.58 us (2%)
    all_to_all x3, blocking collectives, swap(): lax.all_to_all(block, axis, 0, 0, tiled=True, axis_index_groups=groups)  70.2 us
    pallas_call x1, Pallas kernels, local(): pl.pallas_call(factor_kernel, out_shape=(jax.ShapeDtypeStruct((B, B), F32...  34.1 us
    all_to_all x4, waiting for transfers between devices, swap(): lax.all_to_all(block, axis, 0, 0, tiled=True, axis_index_groups=groups)  21.1 us
    all_to_all x4, starting transfers between devices, swap(): lax.all_to_all(block, axis, 0, 0, tiled=True, axis_index_groups=groups)  16.6 us
    unnamed x18, local copies, waits for them, and re-layouts  10.8 us
    pallas_call x1, Pallas kernels, local(): pl.pallas_call(update_kernel, grid=(COLS // tile,), out_shape=(jax.ShapeD...  10.2 us
    pallas_call x1, Pallas kernels, local(): pl.pallas_call(product_kernel, out_shape=(jax.ShapeDtypeStruct((B, ROWS),...  8.22 us
  transfers between devices with their start and end apart: 6, of which 4 were waited for; matrix products, arithmetic and copies ran while one was open for 3% of the time, Pallas kernels for 19%

profile of v1, /device:TPU:2, one launch (start us, length us, event | category | flops | bytes accessed | tf_op | source)
XLA Modules:
  0.0 178.9 jit_solution(9677028305801669672)
XLA Ops:
  0.6 1.2 pad_maximum_fusion.1
  1.8 13.7 %all_to_all.76.mine_ref = f32[4,32,1024]{2,1,0:T(8,128)S(1)} all-to-all(f32[4,32,1024]{2,1,0:T(8,128)S(1)} %bitcast.24), channel_id=1, replica_groups={{0,2,4,6},{1,3,5,7},{8,10,12,14},{9,11,13,15},{16,18,20,22},{17,19,21,2..., dimensions={0} | all-to-all | bytes 1048576 | tf_op jit(solution)/shard_map/gather_panel/all_to_all | solution.py:124
  15.6 1.9 %collective-permute-done = f32[128,1024]{1,0:T(8,128)S(1)} collective-permute-done((f32[128,1024]{1,0:T(8,128)S(1)}, f32[128,1024]{1,0:T(8,128)S(1)}, u32[]{:S(2)}, u32[]{:S(2)}) %collective-permute-start) | collective-permute-done | bytes 524320 | tf_op jit(solution)/shard_map/gather_panel/ppermute | solution.py:143
  17.5 8.2 %product.1 = (f32[256,1024]{1,0:T(8,128)S(1)}, f32[256,2176]{1,0:T(8,128)S(1)}) custom-call(s32[1]{0:T(128)} %bitcast.core_ref, f32[4,32,1024]{2,1,0:T(8,128)S(1)} %all_to_all.76.mine_ref, f32[4,32,1024]{2,1,0:T(8,128)S(1)} %bitcast.20, bf16[1024,2048]{1,0:T(8,128)(2,1)} %trailing_ref.3), custom_call_target="tpu_custom_call" | custom-call | flops 3600000000 | bytes 8000000 | tf_op jit(solution)/shard_map/product/pallas_call | solution.py:145
  25.7 1.0 copy-done
  26.7 31.2 %all_to_all.77 = f32[4,64,2176]{2,1,0:T(8,128)S(1)} all-to-all(f32[4,64,2176]{2,1,0:T(8,128)S(1)} %bitcast.15), channel_id=1, replica_groups={{0,64,128,192},{8,72,136,200},{16,80,144,208},{24,88,152,216},{32,96,16..., dimensions={0} | all-to-all | bytes 4456448 | tf_op jit(solution)/shard_map/sum_over_x/all_to_all | solution.py:124
  58.0 25.3 %all_to_all.78 = f32[8,8,2176]{2,1,0:T(8,128)S(1)} all-to-all(f32[8,8,2176]{2,1,0:T(8,128)S(1)} %bitcast.22), channel_id=1, replica_groups={{0,8,16,24,32,40,48,56},{64,72,80,88,96,104,112,120},{128,136,144,152,1..., dimensions={0} | all-to-all | bytes 1114112 | tf_op jit(solution)/shard_map/sum_over_z/all_to_all | solution.py:124
  83.4 0.6 constant_dynamic-update-slice_fusion.7
  84.0 0.6 slice_dynamic-update-slice_fusion.6
  84.6 0.6 constant_dynamic-update-slice_fusion.6
  85.2 0.6 constant_dynamic-update-slice_fusion.5
  85.8 0.6 constant_dynamic-update-slice_fusion.4
  87.0 0.6 constant_dynamic-update-slice_fusion.2
  88.7 3.3 %all-to-all-start.3 = ((f32[8,8,128]{2,1,0:T(8,128)}), f32[8,8,128]{2,1,0:T(8,128)S(1)}, u32[]{:S(2)}, u32[]{:S(2)}) async-start(f32[8,8,128]{2,1,0:T(8,128)} %bitcast.7), calls=%async_computation.3 | async-start | bytes 65536 | tf_op jit(solution)/shard_map/gather_gram/all_to_all | solution.py:124
  92.1 0.6 slice_dynamic-update-slice_fusion.5
  92.7 0.6 slice_dynamic-update-slice_fusion.4
  93.4 0.6 slice_dynamic-update-slice_fusion.3
  94.0 0.6 slice_dynamic-update-slice_fusion.2
  94.6 0.6 slice_dynamic-update-slice_fusion.1
  95.3 0.6 slice_dynamic-update-slice_fusion
  95.9 4.1 %all-to-all-done.3 = f32[8,8,128]{2,1,0:T(8,128)S(1)} async-done(((f32[8,8,128]{2,1,0:T(8,128)}), f32[8,8,128]{2,1,0:T(8,128)S(1)}, u32[]{:S(2)}, u32[]{:S(2)}) %all-to-all-start.3) | async-done | bytes 32800 | tf_op jit(solution)/shard_map/gather_gram/all_to_all | solution.py:124
  100.0 0.7 pad_maximum_fusion.2
  100.7 4.8 %all-to-all-start.4 = ((f32[4,64,128]{2,1,0:T(8,128)}), f32[4,64,128]{2,1,0:T(8,128)S(1)}, u32[]{:S(2)}, u32[]{:S(2)}) async-start(f32[4,64,128]{2,1,0:T(8,128)} %bitcast.9), calls=%async_computation.4 | async-start | bytes 262144 | tf_op jit(solution)/shard_map/gather_gram/all_to_all | solution.py:124
  105.5 0.6 slice_dynamic-update-slice_fusion.7
  106.1 3.9 %all-to-all-done.4 = f32[4,64,128]{2,1,0:T(8,128)S(1)} async-done(((f32[4,64,128]{2,1,0:T(8,128)}), f32[4,64,128]{2,1,0:T(8,128)S(1)}, u32[]{:S(2)}, u32[]{:S(2)}) %all-to-all-start.4) | async-done | bytes 131104 | tf_op jit(solution)/shard_map/gather_gram/all_to_all | solution.py:124
  110.0 3.5 %all-to-all-start.5 = ((f32[8,8,2048]{2,1,0:T(8,128)}), f32[8,8,2048]{2,1,0:T(8,128)S(1)}, u32[]{:S(2)}, u32[]{:S(2)}) async-start(f32[8,8,2048]{2,1,0:T(8,128)} %bitcast.11), calls=%async_computation.5 | async-start | bytes 1048576 | tf_op jit(solution)/shard_map/gather_sums/all_to_all | solution.py:124
  113.6 13.1 %all-to-all-done.5 = f32[8,8,2048]{2,1,0:T(8,128)S(1)} async-done(((f32[8,8,2048]{2,1,0:T(8,128)}), f32[8,8,2048]{2,1,0:T(8,128)S(1)}, u32[]{:S(2)}, u32[]{:S(2)}) %all-to-all-start.5) | async-done | bytes 524320 | tf_op jit(solution)/shard_map/gather_sums/all_to_all | solution.py:124
  126.7 1.6 pad_maximum_fusion
  128.2 5.0 %all-to-all-start.6 = ((f32[4,64,2048]{2,1,0:T(8,128)}), f32[4,64,2048]{2,1,0:T(8,128)S(1)}, u32[]{:S(2)}, u32[]{:S(2)}) async-start(f32[4,64,2048]{2,1,0:T(8,128)} %bitcast.21), calls=%async_computation.6 | async-start | bytes 4194304 | tf_op jit(solution)/shard_map/gather_sums/all_to_all | solution.py:124
  133.3 1.2 copy-done.1
  134.5 34.1 %factor.1 = (f32[256,256]{1,0:T(8,128)}, f32[256,256]{1,0:T(8,128)S(1)}, bf16[1024,256]{1,0:T(8,128)(2,1)S(1)}) custom-call(s32[1]{0:T(128)} %bitcast.core_ref, f32[256,128]{1,0:T(8,128)S(1)} %bitcast.19, f32[256,128]{1,0:T(8,128)S(1)} %collective-permute-done.1.other_ref, f32[256,1024]{1,0:T(8,128)S(1)} %copy-done.1), custom_call_target="tpu_custom_call" | custom-call | flops 20000000000 | bytes 3000000 | tf_op jit(solution)/shard_map/factor/pallas_call | solution.py:164
  168.6 10.2 %update.1 = (f32[256,2048]{1,0:T(8,128)}, bf16[1024,2048]{1,0:T(8,128)(2,1)}) custom-call(f32[256,2048]{1,0:T(8,128)S(1)} %bitcast.16, f32[256,256]{1,0:T(8,128)S(1)} %get-tuple-element.13.inv_ref, bf16[1024,256]{1,0:T(8,128)(2,1)S(1)} %get-tuple-element.14.low_ref, bf16[1024,2048]{1,0:T(8,128)(2,1)} %trailing_ref.3), custom_call_target="tpu_custom_call" | custom-call | flops 3000000000 | bytes 12000000 | tf_op jit(solution)/shard_map/update/pallas_call | solution.py:179
  (11 shorter events, 2.1 us)
Async XLA Ops:
  15.6 1.9 %collective-permute-start = (f32[128,1024]{1,0:T(8,128)S(1)}, f32[128,1024]{1,0:T(8,128)S(1)}, u32[]{:S(2)}, u32[]{:S(2)}) collective-permute-start(f32[128,1024]{1,0:T(8,128)S(1)} %bitcast.17), channel_id=1, source_target_pairs={{0,1},{1,0},{2,3},{3,2},{4,5},{5,4},{6,7},{7,6},{8,9},{9,8},{10,11... | collective-permute-start | bytes 1572872 | tf_op jit(solution)/shard_map/gather_panel/ppermute | solution.py:143
  25.7 1.0 copy-start
  88.7 11.3 %all-to-all-start.3 = ((f32[8,8,128]{2,1,0:T(8,128)}), f32[8,8,128]{2,1,0:T(8,128)S(1)}, u32[]{:S(2)}, u32[]{:S(2)}) async-start(f32[8,8,128]{2,1,0:T(8,128)} %bitcast.7), calls=%async_computation.3 | async-start | bytes 65536 | tf_op jit(solution)/shard_map/gather_gram/all_to_all | solution.py:124
  100.7 9.3 %all-to-all-start.4 = ((f32[4,64,128]{2,1,0:T(8,128)}), f32[4,64,128]{2,1,0:T(8,128)S(1)}, u32[]{:S(2)}, u32[]{:S(2)}) async-start(f32[4,64,128]{2,1,0:T(8,128)} %bitcast.9), calls=%async_computation.4 | async-start | bytes 262144 | tf_op jit(solution)/shard_map/gather_gram/all_to_all | solution.py:124
  110.0 16.7 %all-to-all-start.5 = ((f32[8,8,2048]{2,1,0:T(8,128)}), f32[8,8,2048]{2,1,0:T(8,128)S(1)}, u32[]{:S(2)}, u32[]{:S(2)}) async-start(f32[8,8,2048]{2,1,0:T(8,128)} %bitcast.11), calls=%async_computation.5 | async-start | bytes 1048576 | tf_op jit(solution)/shard_map/gather_sums/all_to_all | solution.py:124
  113.5 19.8 %collective-permute-start.1 = (f32[256,128]{1,0:T(8,128)S(1)}, f32[256,128]{1,0:T(8,128)S(1)}, u32[]{:S(2)}, u32[]{:S(2)}) collective-permute-start(f32[256,128]{1,0:T(8,128)S(1)} %bitcast.18), channel_id=1, source_target_pairs={{0,1},{1,0},{2,3},{3,2},{4,5},{5,4},{6,7},{7,6},{8,9},{9,8},{10,11... | collective-permute-start | bytes 393224 | tf_op jit(solution)/shard_map/gather_gram/ppermute | solution.py:160
  128.2 40.4 %all-to-all-start.6 = ((f32[4,64,2048]{2,1,0:T(8,128)}), f32[4,64,2048]{2,1,0:T(8,128)S(1)}, u32[]{:S(2)}, u32[]{:S(2)}) async-start(f32[4,64,2048]{2,1,0:T(8,128)} %bitcast.21), calls=%async_computation.6 | async-start | bytes 4194304 | tf_op jit(solution)/shard_map/gather_sums/all_to_all | solution.py:124
  133.3 1.2 copy-start.1

commit v2 on v0

v2 whole, which is shorter than its diff:
```python
import jax
import jax.numpy as jnp
from jax import lax
from jax.experimental import pallas as pl
from jax.experimental.pallas import tpu as pltpu
from jax.sharding import PartitionSpec as P

F32 = jnp.float32
BF16 = jnp.bfloat16
HIGHEST = lax.Precision.HIGHEST
NX, NZ = 4, 8
B, ROWS, COLS, HALF, TILE = 256, 1024, 2048, 128, 256
A_COLS, B_COLS = 1280, 768

Z_GROUPS = [[x * NZ + z for z in range(NZ)] for x in range(NX)]
Y_GROUPS = [[2 * y + core for y in range(4)] for core in range(2)]
SIBLING = [(c, c ^ 1) for c in range(8)]
X_ROUTES = [[(x * NZ + z, (x + k) % NX * NZ + z) for x in range(NX) for z in range(NZ)] for k in range(NX)]


def dot(a, b, contract=((1,), (0,)), precision=None):
    return lax.dot_general(a, b, (contract, ((), ())), precision=precision, preferred_element_type=F32)


def split(value, count):
    terms = []
    for _ in range(count):
        terms.append(value.astype(BF16))
        value = value - terms[-1].astype(F32)
    return terms


def dot_split(left, high, low):
    rows = left.shape[0] // 2
    both = dot(left, high)
    return both[rows:] + dot(left[:rows], low) + both[:rows]


def tile_of(index):
    return slice(index * TILE, index * TILE + TILE)


def fetches(source_ref, target_ref, first, count, arrived):
    copies = [
        pltpu.make_async_copy(source_ref.at[:, tile_of(first + tile)], target_ref.at[:, tile_of(tile)], arrived.at[tile])
        for tile in range(count)
    ]
    for copy in copies:
        copy.start()
    return copies


def product_a_kernel(ids_ref, mine_ref, other_ref, trailing_ref, parts_ref, *refs):
    pieces, (held, third, whole, gram, arrived) = refs[:NX], refs[NX:]
    copies = fetches(trailing_ref, held, 0, A_COLS // TILE, arrived)
    first = ids_ref[0] == 0
    for y in range(4):
        mine, other = mine_ref[y], other_ref[y]
        for offset, value in ((0, jnp.where(first, mine, other)), (32, jnp.where(first, other, mine))):
            start = 64 * y + offset
            high, middle, low = split(value, 3)
            parts_ref[start:start + 32] = high
            parts_ref[B + start:B + start + 32] = middle
            third[start:start + 32] = low
    half = pl.multiple_of(ids_ref[0] * HALF, HALF)
    last = ((1,), (1,))
    one = dot(parts_ref[...], parts_ref[pl.ds(half, HALF)], last)
    two = dot(parts_ref[...], parts_ref[pl.ds(pl.multiple_of(B + half, HALF), HALF)], last)
    small = dot(third[...], parts_ref[pl.ds(half, HALF)], last) + dot(parts_ref[:B], third[pl.ds(half, HALF)], last)
    gram[...] = small + two[B:] + one[B:] + two[:B] + one[:B]

    def hand_out(source, columns):
        for k in range(NX):
            start = pl.multiple_of(64 * lax.rem(ids_ref[1] + k, NX), 64)
            pieces[k][:, columns] = source[pl.ds(start, 64)]

    hand_out(gram, slice(A_COLS, A_COLS + HALF))
    for tile, copy in enumerate(copies):
        copy.wait()
        both = dot(parts_ref[...], held[:, tile_of(tile)])
        slot = whole.at[tile % 2]
        slot[...] = both[B:] + both[:B]
        hand_out(slot, tile_of(tile))


def product_b_kernel(parts_ref, trailing_ref, out_ref, held, arrived):
    copies = fetches(trailing_ref, held, A_COLS // TILE, B_COLS // TILE, arrived)
    for tile, copy in enumerate(copies):
        copy.wait()
        both = dot(parts_ref[...], held[:, tile_of(tile)])
        out_ref[:, tile_of(tile)] = both[B:] + both[:B]


def eliminate(work, unit, upper, inverse):
    n, tiles = HALF, HALF // 8
    shape = (tiles, 8, n)
    row = 8 * lax.broadcasted_iota(jnp.int32, shape, 0) + lax.broadcasted_iota(jnp.int32, shape, 1)
    lane = lax.broadcasted_iota(jnp.int32, shape, 2)
    eight = lax.broadcasted_iota(jnp.int32, (8, n), 0)
    unit[...] = (lane == row).astype(F32)

    def splat(tile, i, k):
        return jnp.broadcast_to(tile[i:i + 1, k:k + 1], (8, n))

    def reciprocal_root(value):
        guess = lax.rsqrt(value)
        return guess * (1.5 - 0.5 * value * guess * guess)

    @pl.loop(0, tiles)
    def _(block):
        s, m = work[...], unit[...]
        pivot_s, pivot_m = work[block], unit[block]
        done_s, done_m = pivot_s, pivot_m
        for half in (0, 4):
            p = {(i, k): splat(pivot_s, half + i, half + k) for i in range(4) for k in range(i + 1)}
            low, root, inv = {}, [], {}
            for k in range(4):
                for i in range(k, 4):
                    value = p[i, k]
                    for q in range(k):
                        value = value - low[i, q] * low[k, q]
                    if i == k:
                        root.append(reciprocal_root(value))
                    else:
                        low[i, k] = value * root[k]
            for i in range(4):
                inv[i, i] = root[i]
                for k in range(i):
                    value = low[i, k] * inv[k, k]
                    for q in range(k + 1, i):
                        value = value + low[i, q] * inv[q, k]
                    inv[i, k] = -value * root[i]

            def combine(items):
                out = []
                for i in range(4):
                    value = inv[i, 0] * items[0]
                    for k in range(1, i + 1):
                        value = value + inv[i, k] * items[k]
                    out.append(value)
                return out

            rows_s = combine([jnp.broadcast_to(pivot_s[half + k:half + k + 1], (8, n)) for k in range(4)])
            rows_m = combine([jnp.broadcast_to(pivot_m[half + k:half + k + 1], (8, n)) for k in range(4)])
            for k in range(4):
                done_s = jnp.where(eight == half + k, rows_s[k], done_s)
                done_m = jnp.where(eight == half + k, rows_m[k], done_m)
            if half == 0:
                factors = combine([jnp.broadcast_to(pivot_s[:, k:k + 1], (8, n)) for k in range(4)])
                for k in range(4):
                    pivot_s = pivot_s - factors[k] * rows_s[k]
                    pivot_m = pivot_m - factors[k] * rows_m[k]
            below = row > 8 * block + half + 3
            factors = combine([jnp.broadcast_to(s[:, :, half + k:half + k + 1], shape) for k in range(4)])
            for k in range(4):
                factor = jnp.where(below, factors[k], 0.0)
                s = s - factor * rows_s[k]
                m = m - factor * rows_m[k]
        upper[block] = pltpu.roll(done_s, 8 * block, 1)
        inverse[block] = done_m
        work[...] = pltpu.roll(s, n - 8, 2)
        unit[...] = m

    upper[...] = jnp.where(lane >= row, upper[...], 0.0)
    inverse[...] = jnp.where(lane <= row, inverse[...], 0.0)


def factor_kernel(ids_ref, mine_ref, other_ref, parts_ref, r_ref, inv_out_ref, low_out_ref,
                  work, unit, upper, inverse, inv_ref, low_ref, sent):
    tiled, flat = (HALF // 8, 8, HALF), (HALF, HALF)
    first = ids_ref[0] == 0
    for k in range(NX):
        rows = pl.ds(pl.multiple_of(64 * lax.rem(ids_ref[1] + NX - k, NX), 64), 64)
        mine, other = mine_ref[k], other_ref[k]
        r_ref[rows, :HALF] = jnp.where(first, mine, other)
        r_ref[rows, HALF:] = jnp.where(first, other, mine)
    right = r_ref[:, HALF:]
    work[...] = r_ref[:HALF, :HALF].reshape(tiled)
    eliminate(work, unit, upper, inverse)
    r_ref[:HALF, :HALF] = upper[...].reshape(flat)
    inverse_1 = inverse[...].reshape(flat)
    r_ref[HALF:, :HALF] = jnp.zeros(flat, F32)
    cross = dot(inverse_1, right[:HALF], precision=HIGHEST)
    r_ref[:HALF, HALF:] = cross
    work[...] = (right[HALF:] - dot(cross, cross, ((0,), (0,)), HIGHEST)).reshape(tiled)
    lower = dot(cross, inverse_1, ((0,), (0,)), HIGHEST)
    eliminate(work, unit, upper, inverse)
    r_ref[HALF:, HALF:] = upper[...].reshape(flat)
    inverse_2 = inverse[...].reshape(flat)
    below = -dot(inverse_2, lower, precision=HIGHEST)
    zero = jnp.zeros(flat, BF16)
    for start, one, two, three in zip((0, B), split(inverse_1, 2), split(below, 2), split(inverse_2, 2)):
        inv_ref[start:start + HALF, :HALF] = one
        inv_ref[start:start + HALF, HALF:] = zero
        inv_ref[start + HALF:start + B, :HALF] = two
        inv_ref[start + HALF:start + B, HALF:] = three
    basis = dot_split(inv_ref[...], parts_ref[:B], parts_ref[B:])
    low_ref[...] = basis.T.astype(BF16)
    results = [
        pltpu.make_async_copy(inv_ref, inv_out_ref, sent.at[0]),
        pltpu.make_async_copy(low_ref, low_out_ref, sent.at[1]),
    ]
    for result in results:
        result.start()
    for result in results:
        result.wait()


def update_kernel(ids_ref, a0_ref, a1_ref, a2_ref, a3_ref, b_ref, inv_in_ref, low_in_ref, trailing_ref,
                  top_ref, updated_ref, inv_ref, low_ref, sums, held, top, updated, ready, arrived, sent):
    inputs = [
        pltpu.make_async_copy(inv_in_ref, inv_ref, ready.at[0]),
        pltpu.make_async_copy(low_in_ref, low_ref, ready.at[1]),
    ]
    for copy in inputs:
        copy.start()
    copies = fetches(trailing_ref, held, 0, COLS // TILE, arrived)
    for k, a_ref in enumerate((a0_ref, a1_ref, a2_ref, a3_ref)):
        x = lax.rem(ids_ref[1] + NX - k, NX)
        sums[pl.ds(pl.multiple_of(64 * x, 64), 64), :A_COLS] = a_ref[...]
        for z in range(NZ):
            sums[pl.ds(pl.multiple_of(32 * z + 8 * x, 8), 8), A_COLS:] = b_ref[z, k]
    for copy in inputs:
        copy.wait()
    results = []

    def send(source, target, semaphore):
        results.append(pltpu.make_async_copy(source, target, semaphore))
        results[-1].start()

    for tile in range(COLS // TILE):
        columns = tile_of(tile)
        rows = dot_split(inv_ref[...], *split(sums[:, columns], 2))
        top[:, columns] = rows
        send(top.at[:, columns], top_ref.at[:, columns], sent.at[0, tile])
        change = dot(low_ref[...], rows.astype(BF16))
        copies[tile].wait()
        updated[:, columns] = (held[:, columns].astype(F32) - change).astype(BF16)
        send(updated.at[:, columns], updated_ref.at[:, columns], sent.at[1, tile])
    for result in results:
        result.wait()


HBM = pl.BlockSpec(memory_space=pltpu.HBM)
VMEM = pl.BlockSpec(memory_space=pltpu.VMEM)
SMEM = pl.BlockSpec(memory_space=pltpu.SMEM)


def cost(flops, size):
    return pl.CostEstimate(flops=int(flops), bytes_accessed=int(size), transcendentals=0)


def limit(mib):
    return pltpu.CompilerParams(vmem_limit_bytes=mib * 2**20)


def array(*shape, dtype=F32):
    return jax.ShapeDtypeStruct(shape, dtype)


def product_a(ids, mine, other, trailing):
    tiles = A_COLS // TILE
    return pl.pallas_call(
        product_a_kernel,
        out_shape=(array(2 * B, ROWS, dtype=BF16),) + (array(B // NX, A_COLS + HALF),) * NX,
        in_specs=[SMEM, VMEM, VMEM, HBM],
        out_specs=(VMEM,) * (1 + NX),
        scratch_shapes=[
            pltpu.VMEM((ROWS, A_COLS), BF16),
            pltpu.VMEM((B, ROWS), BF16),
            pltpu.VMEM((2, B, TILE), F32),
            pltpu.VMEM((B, HALF), F32),
            pltpu.SemaphoreType.DMA((tiles,)),
        ],
        compiler_params=limit(50),
        cost_estimate=cost(2.4e9, 6e6),
    )(ids, mine.reshape(4, 32, ROWS), other.reshape(4, 32, ROWS), trailing)


def product_b(parts, trailing):
    tiles = B_COLS // TILE
    return pl.pallas_call(
        product_b_kernel,
        out_shape=array(B, B_COLS),
        in_specs=[VMEM, HBM],
        out_specs=VMEM,
        scratch_shapes=[pltpu.VMEM((ROWS, B_COLS), BF16), pltpu.SemaphoreType.DMA((tiles,))],
        compiler_params=limit(50),
        cost_estimate=cost(1.3e9, 4e6),
    )(parts, trailing)


def factor(ids, mine, other, parts):
    return pl.pallas_call(
        factor_kernel,
        out_shape=(
            array(B, B),
            array(2 * B, B, dtype=BF16),
            array(ROWS, B, dtype=BF16),
        ),
        in_specs=[SMEM, VMEM, VMEM, VMEM],
        out_specs=(VMEM, HBM, HBM),
        scratch_shapes=[pltpu.VMEM((HALF // 8, 8, HALF), F32)] * 4
        + [pltpu.VMEM((2 * B, B), BF16), pltpu.VMEM((ROWS, B), BF16), pltpu.SemaphoreType.DMA((2,))],
        compiler_params=limit(20),
        cost_estimate=cost(2e10, 3e6),
    )(ids, mine, other, parts)


def update(ids, a, b, inverse, low, trailing):
    tiles = COLS // TILE
    return pl.pallas_call(
        update_kernel,
        out_shape=(array(B, COLS), array(ROWS, COLS, dtype=BF16)),
        in_specs=[SMEM] + [VMEM] * 5 + [HBM] * 3,
        out_specs=(HBM, HBM),
        scratch_shapes=[
            pltpu.VMEM((2 * B, B), BF16),
            pltpu.VMEM((ROWS, B), BF16),
            pltpu.VMEM((B, COLS), F32),
            pltpu.VMEM((ROWS, COLS), BF16),
            pltpu.VMEM((B, COLS), F32),
            pltpu.VMEM((ROWS, COLS), BF16),
            pltpu.SemaphoreType.DMA((2,)),
            pltpu.SemaphoreType.DMA((tiles,)),
            pltpu.SemaphoreType.DMA((2, tiles)),
        ],
        compiler_params=limit(50),
        cost_estimate=cost(3e9, 12e6),
    )(ids, *a, b, inverse, low, trailing)


def swap(block, axis, groups):
    return lax.all_to_all(block, axis, 0, 0, axis_index_groups=groups)


def gather(block, axis, groups):
    return swap(jnp.broadcast_to(block[None], (len(groups[0]),) + block.shape), axis, groups)


def scatter_z(block):
    return swap(block.reshape((NZ, -1) + block.shape[1:]), "row", Z_GROUPS)


def shift_x(pieces):
    return [pieces[0]] + [lax.ppermute(pieces[k], "row", X_ROUTES[k]) for k in range(1, NX)]


def local(panel, trailing):
    x = lax.axis_index("row") // NZ
    ids = jnp.stack([lax.axis_index("col") % 2, x]).astype(jnp.int32)
    with jax.named_scope("gather_panel"):
        mine = gather(panel.T, "col", Y_GROUPS)
        other = lax.ppermute(mine, "col", SIBLING)
    with jax.named_scope("product"):
        parts, *a = product_a(ids, mine, other, trailing)
        b = product_b(parts, trailing)
    together = lax.optimization_barrier
    with jax.named_scope("sum_first"):
        a, b = together((shift_x(a), scatter_z(b)))
        a, b = together((sum(a), jnp.sum(b, axis=0)))
    with jax.named_scope("sum_second"):
        b = shift_x([lax.dynamic_slice_in_dim(b, (x + k) % NX * 8, 8, 0) for k in range(NX)])
        a, b = together((scatter_z(a), b))
        a, b = together((jnp.sum(a, axis=0), sum(b)))
    with jax.named_scope("gather_first"):
        a, b = together((gather(a, "row", Z_GROUPS), shift_x([b] * NX)))
        a, b = a.reshape(64, A_COLS + HALF), jnp.concatenate(b, axis=0)
    with jax.named_scope("gather_gram"):
        gram_mine = jnp.stack(shift_x([a[:, A_COLS:]] * NX))
        gram_other = lax.ppermute(gram_mine, "col", SIBLING)
    with jax.named_scope("gather_second"):
        a = shift_x([a[:, :A_COLS]] * NX)
        b = gather(b, "row", Z_GROUPS).reshape(NZ, NX, 8, B_COLS)
    with jax.named_scope("factor"):
        r_factor, inverse, low = factor(ids, gram_mine, gram_other, parts)
    with jax.named_scope("update"):
        top, updated = update(ids, a, b, inverse, low, trailing)
    return r_factor, top, updated


def solution(mesh):
    return jax.shard_map(
        local,
        mesh=mesh,
        in_specs=(P("row", "col"), P("row", "col")),
        out_specs=(P(), P(None, "col"), P("row", "col")),
        check_vma=False,
    )
```

time: 334 us -> 152 us (0.46)
  waiting for transfers between devices: 221 us -> 44.4 us
  other arithmetic: 53.9 us -> 3.13 us
  Pallas kernels: 0 us -> 37.5 us
  starting transfers between devices: 14.6 us -> 43.8 us
  matrix products: 18.1 us -> 0 us
  between operations: 15.5 us -> 1 us
  blocking collectives: 0 us -> 13.4 us
    psum x1 -> x0, waiting for transfers between devices: 152 us -> none  [local(): lax.psum(jnp.dot(basis.T, trailing, precision=highest, preferred_element_...]
    another operation x9 -> x2, other arithmetic: 53.7 us -> 0.08 us  [the longest x1 0.07 us: local(): ids = jnp.stack([lax.axis_index('col') % 2, x]).astype(jnp.int32)]
    pallas_call x0 -> x4, Pallas kernels: none -> 37.5 us  [the longest x1 18.6 us: factor(): pl.pallas_call(factor_kernel, out_shape=(array(B, B), array(2 * B, B, dty...]
    all_gather x1 -> x0, waiting for transfers between devices: 32.1 us -> none  [local(): whole = lax.all_gather(panel, 'col', axis=1, tiled=True)]
    all_to_all x0 -> x4, waiting for transfers between devices: none -> 19.9 us  [swap(): return lax.all_to_all(block, axis, 0, 0, axis_index_groups=groups)]
    all_to_all x0 -> x4, starting transfers between devices: none -> 18.6 us  [swap(): return lax.all_to_all(block, axis, 0, 0, axis_index_groups=groups)]
    dot_general x3 -> x0, matrix products: 15.8 us -> none  [the longest x1 6.94 us: local(): jnp.dot(basis.T, trailing, precision=highest, preferred_element_type=jnp....]
    all_to_all x0 -> x1, blocking collectives: none -> 13.4 us  [swap(): return lax.all_to_all(block, axis, 0, 0, axis_index_groups=groups)]
  transfers between devices with their start and end apart: 7 -> 21, of which waited for: 7 -> 12; matrix products, arithmetic and copies ran while one was open for 0% -> 1% of each run, Pallas kernels for 0% -> 12%
where the time goes in v2:
time: 152 us; the launch traced here: 149 us
  waiting for transfers between devices  44.4 us (29%)
  starting transfers between devices  43.8 us (29%)
  Pallas kernels  37.5 us (25%)
  blocking collectives  13.4 us (9%)
  local copies, waits for them, and re-layouts  6.19 us (4%)
  other arithmetic  3.13 us (2%)
    ppermute x15, waiting for transfers between devices, shift_x(): lax.ppermute(pieces[k], 'row', X_ROUTES[k])  23 us
    ppermute x15, starting transfers between devices, shift_x(): lax.ppermute(pieces[k], 'row', X_ROUTES[k])  21.3 us
    all_to_all x4, waiting for transfers between devices, swap(): return lax.all_to_all(block, axis, 0, 0, axis_index_groups=groups)  19.9 us
    all_to_all x4, starting transfers between devices, swap(): return lax.all_to_all(block, axis, 0, 0, axis_index_groups=groups)  18.6 us
    pallas_call x1, Pallas kernels, factor(): pl.pallas_call(factor_kernel, out_shape=(array(B, B), array(2 * B, B, dty...  18.6 us
    all_to_all x1, blocking collectives, swap(): return lax.all_to_all(block, axis, 0, 0, axis_index_groups=groups)  13.4 us
    pallas_call x1, Pallas kernels, update(): pl.pallas_call(update_kernel, out_shape=(array(B, COLS), array(ROWS, COLS...  8.93 us
    pallas_call x1, Pallas kernels, product_a(): pl.pallas_call(product_a_kernel, out_shape=(array(2 * B, ROWS, dtype=BF16...  6.23 us
  transfers between devices with their start and end apart: 21, of which 12 were waited for; matrix products, arithmetic and copies ran while one was open for 1% of the time, Pallas kernels for 12%

profile of v2, /device:TPU:1, one launch (start us, length us, event | category | flops | bytes accessed | tf_op | source)
XLA Modules:
  0.0 149.4 jit_solution(3737256265437630371)
XLA Ops:
  1.6 13.4 %all_to_all.25.mine_ref = f32[4,32,1024]{2,1,0:T(8,128)S(1)} all-to-all(f32[4,32,1024]{2,1,0:T(8,128)S(1)} %broadcast_in_dim.6), channel_id=1, replica_groups={{0,2,4,6},{1,3,5,7},{8,10,12,14},{9,11,13,15},{16,18,20,22},{17,19,21,2..., dimensions={0} | all-to-all | bytes 1048576 | tf_op jit(solution)/shard_map/gather_panel/all_to_all | solution.py:334
  15.0 1.9 %collective-permute-start = (f32[4,32,1024]{2,1,0:T(8,128)S(1)}, f32[4,32,1024]{2,1,0:T(8,128)S(1)}, u32[]{:S(2)}, u32[]{:S(2)}) collective-permute-start(f32[4,32,1024]{2,1,0:T(8,128)S(1)} %all_to_all.25.mine_ref), channel_id=1, source_target_pairs={{0,1},{1,0},{2,3},{3,2},{4,5},{5,4},{6,7},{7,6},{8,9},{9,8},{10,11... | collective-permute-start | bytes 1572872 | tf_op jit(solution)/shard_map/gather_panel/ppermute | solution.py:354
  16.9 1.5 collective-permute-done.other_ref
  18.4 6.2 %product.2 = (bf16[512,1024]{1,0:T(8,128)(2,1)S(1)}, f32[64,1408]{1,0:T(8,128)S(1)}, f32[64,1408]{1,0:T(8,128)S(1)}, f32[64,1408]{1,0:T(8,128)S(1)}, f32[64,1408]{1,0:T(8,128)S(1)}) custom-call(s32[2]{0:T(128)S(1)} %pad_add_fusion.ids_ref, f32[4,32,1024]{2,1,0:T(8,128)S(1)} %all_to_all.25.mine_ref, f32[4,32,1024]{2,1,0:T(8,128)S(1)} %collective-permute-done.other_ref, ...), custom_call_target="tpu_custom_call" | custom-call | flops 2400000000 | bytes 6000000 | tf_op jit(solution)/shard_map/product/pallas_call | solution.py:263
  24.6 3.8 %product.3 = f32[256,768]{1,0:T(8,128)} custom-call(bf16[512,1024]{1,0:T(8,128)(2,1)S(1)} %get-tuple-element.36.parts_ref, bf16[1024,2048]{1,0:T(8,128)(2,1)} %trailing_ref.5), custom_call_target="tpu_custom_call" | custom-call | flops 1300000000 | bytes 4000000 | tf_op jit(solution)/shard_map/product/pallas_call | solution.py:282
  28.4 8.2 %all-to-all-start.1 = ((f32[8,32,768]{2,1,0:T(8,128)}), f32[8,32,768]{2,1,0:T(8,128)}, u32[]{:S(2)}, u32[]{:S(2)}) async-start(f32[8,32,768]{2,1,0:T(8,128)} %bitcast.3), calls=%async_computation.1 | async-start | bytes 1572864 | tf_op jit(solution)/shard_map/sum_first/all_to_all | solution.py:334
  36.6 1.2 collective-permute-start.1
  37.8 2.5 %collective-permute-start.2 = (f32[64,1408]{1,0:T(8,128)S(1)}, f32[64,1408]{1,0:T(8,128)S(1)}, u32[]{:S(2)}, u32[]{:S(2)}) collective-permute-start(f32[64,1408]{1,0:T(8,128)S(1)} %get-tuple-element.34), channel_id=1, source_target_pairs={{0,128},{8,136},{16,144},{24,152},{32,160},{40,168},{48,176},{56,1... | collective-permute-start | bytes 1081352 | tf_op jit(solution)/shard_map/sum_first/ppermute | solution.py:346
  40.3 1.1 collective-permute-start.3
  41.4 5.8 %collective-permute-done.1 = f32[64,1408]{1,0:T(8,128)S(1)} collective-permute-done((f32[64,1408]{1,0:T(8,128)S(1)}, f32[64,1408]{1,0:T(8,128)S(1)}, u32[]{:S(2)}, u32[]{:S(2)}) %collective-permute-start.1) | collective-permute-done | bytes 360480 | tf_op jit(solution)/shard_map/sum_first/ppermute | solution.py:346
  47.2 8.6 %collective-permute-done.2 = f32[64,1408]{1,0:T(8,128)S(1)} collective-permute-done((f32[64,1408]{1,0:T(8,128)S(1)}, f32[64,1408]{1,0:T(8,128)S(1)}, u32[]{:S(2)}, u32[]{:S(2)}) %collective-permute-start.2) | collective-permute-done | bytes 360480 | tf_op jit(solution)/shard_map/sum_first/ppermute | solution.py:346
  55.8 4.4 %all-to-all-done.1 = f32[8,32,768]{2,1,0:T(8,128)} async-done(((f32[8,32,768]{2,1,0:T(8,128)}), f32[8,32,768]{2,1,0:T(8,128)}, u32[]{:S(2)}, u32[]{:S(2)}) %all-to-all-start.1) | async-done | bytes 786464 | tf_op jit(solution)/shard_map/sum_first/all_to_all | solution.py:334
  60.3 1.2 reduce_sum.18
  61.4 1.8 %add_add_fusion = f32[64,1408]{1,0:T(8,128)} fusion(f32[64,1408]{1,0:T(8,128)} %collective-permute-done.3, f32[64,1408]{1,0:T(8,128)S(1)} %collective-permute-done.2, f32[64,1408]{1,0:T(8,128)S(1)} %get-tuple-element.37, f32[64,1408]{1,0:T(8,128)S(1)} %collective-permute-done.1), kind=kLoop, calls=%fused_computation | loop fusion | flops 270336 | bytes 1802240 | tf_op jit(solution)/shard_map/sum_first/add | solution.py:361
  63.3 3.4 %all-to-all-start.2 = ((f32[8,8,1408]{2,1,0:T(8,128)}), f32[8,8,1408]{2,1,0:T(8,128)S(1)}, u32[]{:S(2)}, u32[]{:S(2)}) async-start(f32[8,8,1408]{2,1,0:T(8,128)} %bitcast.4), calls=%async_computation.2 | async-start | bytes 720896 | tf_op jit(solution)/shard_map/sum_second/all_to_all | solution.py:334
  66.8 2.6 %collective-permute-start.6 = (f32[8,768]{1,0:T(8,128)S(1)}, f32[8,768]{1,0:T(8,128)S(1)}, u32[]{:S(2)}, u32[]{:S(2)}) collective-permute-start(f32[8,768]{1,0:T(8,128)S(1)} %get-tuple-element.63), channel_id=1, source_target_pairs={{0,192},{8,200},{16,208},{24,216},{32,224},{40,232},{48,240},{56,2... | collective-permute-start | bytes 73736 | tf_op jit(solution)/shard_map/sum_second/ppermute | solution.py:346
  70.5 3.4 %collective-permute-done.5 = f32[8,768]{1,0:T(8,128)S(1)} collective-permute-done((f32[8,768]{1,0:T(8,128)S(1)}, f32[8,768]{1,0:T(8,128)S(1)}, u32[]{:S(2)}, u32[]{:S(2)}) %collective-permute-start.5) | collective-permute-done | bytes 24608 | tf_op jit(solution)/shard_map/sum_second/ppermute | solution.py:346
  74.1 6.9 %all-to-all-done.2 = f32[8,8,1408]{2,1,0:T(8,128)S(1)} async-done(((f32[8,8,1408]{2,1,0:T(8,128)}), f32[8,8,1408]{2,1,0:T(8,128)S(1)}, u32[]{:S(2)}, u32[]{:S(2)}) %all-to-all-start.2) | async-done | bytes 360480 | tf_op jit(solution)/shard_map/sum_second/all_to_all | solution.py:334
  81.9 3.4 %all-to-all-start.3 = ((f32[8,8,1408]{2,1,0:T(8,128)}), f32[8,8,1408]{2,1,0:T(8,128)S(1)}, u32[]{:S(2)}, u32[]{:S(2)}) async-start(f32[8,8,1408]{2,1,0:T(8,128)} %broadcast_in_dim.7), calls=%async_computation.3 | async-start | bytes 720896 | tf_op jit(solution)/shard_map/gather_first/all_to_all | solution.py:334
  85.3 2.6 %collective-permute-start.9 = (f32[8,768]{1,0:T(8,128)S(1)}, f32[8,768]{1,0:T(8,128)S(1)}, u32[]{:S(2)}, u32[]{:S(2)}) collective-permute-start(f32[8,768]{1,0:T(8,128)S(1)} %add_add_fusion.1), channel_id=1, source_target_pairs={{0,192},{8,200},{16,208},{24,216},{32,224},{40,232},{48,240},{56,2... | collective-permute-start | bytes 73736 | tf_op jit(solution)/shard_map/gather_first/ppermute | solution.py:346
  89.0 3.4 %collective-permute-done.8 = f32[8,768]{1,0:T(8,128)S(1)} collective-permute-done((f32[8,768]{1,0:T(8,128)S(1)}, f32[8,768]{1,0:T(8,128)S(1)}, u32[]{:S(2)}, u32[]{:S(2)}) %collective-permute-start.8) | collective-permute-done | bytes 24608 | tf_op jit(solution)/shard_map/gather_first/ppermute | solution.py:346
  92.6 7.1 %all-to-all-done.3 = f32[8,8,1408]{2,1,0:T(8,128)S(1)} async-done(((f32[8,8,1408]{2,1,0:T(8,128)}), f32[8,8,1408]{2,1,0:T(8,128)S(1)}, u32[]{:S(2)}, u32[]{:S(2)}) %all-to-all-start.3) | async-done | bytes 360480 | tf_op jit(solution)/shard_map/gather_first/all_to_all | solution.py:334
  99.7 2.8 %collective-permute-start.11 = (f32[64,128]{1,0:T(8,128)S(1)}, f32[64,128]{1,0:T(8,128)S(1)}, u32[]{:S(2)}, u32[]{:S(2)}) collective-permute-start(f32[64,128]{1,0:T(8,128)S(1)} %get-tuple-element.62), channel_id=1, source_target_pairs={{0,128},{8,136},{16,144},{24,152},{32,160},{40,168},{48,176},{56,1... | collective-permute-start | bytes 98312 | tf_op jit(solution)/shard_map/gather_gram/ppermute | solution.py:346
  102.8 2.4 %collective-permute-start.12 = (f32[64,128]{1,0:T(8,128)S(1)}, f32[64,128]{1,0:T(8,128)S(1)}, u32[]{:S(2)}, u32[]{:S(2)}) collective-permute-start(f32[64,128]{1,0:T(8,128)S(1)} %get-tuple-element.62), channel_id=1, source_target_pairs={{0,192},{8,200},{16,208},{24,216},{32,224},{40,232},{48,240},{56,2... | collective-permute-start | bytes 98312 | tf_op jit(solution)/shard_map/gather_gram/ppermute | solution.py:346
  105.1 1.3 collective-permute-done.10
  106.4 2.0 %collective-permute-start.13 = (f32[4,64,128]{2,1,0:T(8,128)S(1)}, f32[4,64,128]{2,1,0:T(8,128)S(1)}, u32[]{:S(2)}, u32[]{:S(2)}) collective-permute-start(f32[4,64,128]{2,1,0:T(8,128)S(1)} %pad_maximum_fusion.mine_ref), channel_id=1, source_target_pairs={{0,1},{1,0},{2,3},{3,2},{4,5},{5,4},{6,7},{7,6},{8,9},{9,8},{10,11... | collective-permute-start | bytes 393224 | tf_op jit(solution)/shard_map/gather_gram/ppermute | solution.py:371
  108.5 3.0 %collective-permute-start.16 = (f32[64,1280]{1,0:T(8,128)S(1)}, f32[64,1280]{1,0:T(8,128)S(1)}, u32[]{:S(2)}, u32[]{:S(2)}) collective-permute-start(f32[64,1280]{1,0:T(8,128)S(1)} %slice.9.a0_ref), channel_id=1, source_target_pairs={{0,192},{8,200},{16,208},{24,216},{32,224},{40,232},{48,240},{56,2... | collective-permute-start | bytes 983048 | tf_op jit(solution)/shard_map/gather_second/ppermute | solution.py:346
  113.1 3.5 %all-to-all-start.4 = ((f32[8,32,768]{2,1,0:T(8,128)}), f32[8,32,768]{2,1,0:T(8,128)S(1)}, u32[]{:S(2)}, u32[]{:S(2)}) async-start(f32[8,32,768]{2,1,0:T(8,128)} %broadcast_in_dim.8), calls=%async_computation.4 | async-start | bytes 1572864 | tf_op jit(solution)/shard_map/gather_second/all_to_all | solution.py:334
  116.7 18.6 %factor.1 = (f32[256,256]{1,0:T(8,128)}, bf16[512,256]{1,0:T(8,128)(2,1)S(1)}, bf16[1024,256]{1,0:T(8,128)(2,1)S(1)}) custom-call(s32[2]{0:T(128)S(1)} %pad_add_fusion.ids_ref, f32[4,64,128]{2,1,0:T(8,128)S(1)} %pad_maximum_fusion.mine_ref, f32[4,64,128]{2,1,0:T(8,128)S(1)} %collective-permute-done.13.other_ref, ...), custom_call_target="tpu_custom_call" | custom-call | flops 20000000000 | bytes 3000000 | tf_op jit(solution)/shard_map/factor/pallas_call | solution.py:294
  136.8 1.5 %all-to-all-done.4 = f32[8,32,768]{2,1,0:T(8,128)S(1)} async-done(((f32[8,32,768]{2,1,0:T(8,128)}), f32[8,32,768]{2,1,0:T(8,128)S(1)}, u32[]{:S(2)}, u32[]{:S(2)}) %all-to-all-start.4) | async-done | bytes 786464 | tf_op jit(solution)/shard_map/gather_second/all_to_all | solution.py:334
  138.3 1.0 copy-done.1
  140.3 8.9 %update.1 = (f32[256,2048]{1,0:T(8,128)}, bf16[1024,2048]{1,0:T(8,128)(2,1)}) custom-call(s32[2]{0:T(128)S(1)} %pad_add_fusion.ids_ref, f32[64,1280]{1,0:T(8,128)S(1)} %slice.9.a0_ref, f32[64,1280]{1,0:T(8,128)S(1)} %collective-permute-done.14.a1_ref, f32[64,1280]{1,0:T(8,128)S(1)} %collective-permute-done.15.a2_ref, ...), custom_call_target="tpu_custom_call" | custom-call | flops 3000000000 | bytes 12000000 | tf_op jit(solution)/shard_map/update/pallas_call | solution.py:312
  (36 shorter events, 9.1 us)
Async XLA Ops:
  15.0 3.4 %collective-permute-start = (f32[4,32,1024]{2,1,0:T(8,128)S(1)}, f32[4,32,1024]{2,1,0:T(8,128)S(1)}, u32[]{:S(2)}, u32[]{:S(2)}) collective-permute-start(f32[4,32,1024]{2,1,0:T(8,128)S(1)} %all_to_all.25.mine_ref), channel_id=1, source_target_pairs={{0,1},{1,0},{2,3},{3,2},{4,5},{5,4},{6,7},{7,6},{8,9},{9,8},{10,11... | collective-permute-start | bytes 1572872 | tf_op jit(solution)/shard_map/gather_panel/ppermute | solution.py:354
  28.4 31.9 %all-to-all-start.1 = ((f32[8,32,768]{2,1,0:T(8,128)}), f32[8,32,768]{2,1,0:T(8,128)}, u32[]{:S(2)}, u32[]{:S(2)}) async-start(f32[8,32,768]{2,1,0:T(8,128)} %bitcast.3), calls=%async_computation.1 | async-start | bytes 1572864 | tf_op jit(solution)/shard_map/sum_first/all_to_all | solution.py:334
  36.6 10.6 %collective-permute-start.1 = (f32[64,1408]{1,0:T(8,128)S(1)}, f32[64,1408]{1,0:T(8,128)S(1)}, u32[]{:S(2)}, u32[]{:S(2)}) collective-permute-start(f32[64,1408]{1,0:T(8,128)S(1)} %get-tuple-element.33), channel_id=1, source_target_pairs={{0,64},{8,72},{16,80},{24,88},{32,96},{40,104},{48,112},{56,120},{... | collective-permute-start | bytes 1081352 | tf_op jit(solution)/shard_map/sum_first/ppermute | solution.py:346
  37.8 18.0 %collective-permute-start.2 = (f32[64,1408]{1,0:T(8,128)S(1)}, f32[64,1408]{1,0:T(8,128)S(1)}, u32[]{:S(2)}, u32[]{:S(2)}) collective-permute-start(f32[64,1408]{1,0:T(8,128)S(1)} %get-tuple-element.34), channel_id=1, source_target_pairs={{0,128},{8,136},{16,144},{24,152},{32,160},{40,168},{48,176},{56,1... | collective-permute-start | bytes 1081352 | tf_op jit(solution)/shard_map/sum_first/ppermute | solution.py:346
  40.3 15.6 %collective-permute-start.3 = (f32[64,1408]{1,0:T(8,128)S(1)}, f32[64,1408]{1,0:T(8,128)}, u32[]{:S(2)}, u32[]{:S(2)}) collective-permute-start(f32[64,1408]{1,0:T(8,128)S(1)} %get-tuple-element.35), channel_id=1, source_target_pairs={{0,192},{8,200},{16,208},{24,216},{32,224},{40,232},{48,240},{56,2... | collective-permute-start | bytes 1081352 | tf_op jit(solution)/shard_map/sum_first/ppermute | solution.py:346
  63.3 17.8 %all-to-all-start.2 = ((f32[8,8,1408]{2,1,0:T(8,128)}), f32[8,8,1408]{2,1,0:T(8,128)S(1)}, u32[]{:S(2)}, u32[]{:S(2)}) async-start(f32[8,8,1408]{2,1,0:T(8,128)} %bitcast.4), calls=%async_computation.2 | async-start | bytes 720896 | tf_op jit(solution)/shard_map/sum_second/all_to_all | solution.py:334
  66.8 3.7 %collective-permute-start.6 = (f32[8,768]{1,0:T(8,128)S(1)}, f32[8,768]{1,0:T(8,128)S(1)}, u32[]{:S(2)}, u32[]{:S(2)}) collective-permute-start(f32[8,768]{1,0:T(8,128)S(1)} %get-tuple-element.63), channel_id=1, source_target_pairs={{0,192},{8,200},{16,208},{24,216},{32,224},{40,232},{48,240},{56,2... | collective-permute-start | bytes 73736 | tf_op jit(solution)/shard_map/sum_second/ppermute | solution.py:346
  69.4 4.5 %collective-permute-start.5 = (f32[8,768]{1,0:T(8,128)S(1)}, f32[8,768]{1,0:T(8,128)S(1)}, u32[]{:S(2)}, u32[]{:S(2)}) collective-permute-start(f32[8,768]{1,0:T(8,128)S(1)} %get-tuple-element.64), channel_id=1, source_target_pairs={{0,128},{8,136},{16,144},{24,152},{32,160},{40,168},{48,176},{56,1... | collective-permute-start | bytes 73736 | tf_op jit(solution)/shard_map/sum_second/ppermute | solution.py:346
  69.9 4.2 %collective-permute-start.4 = (f32[8,768]{1,0:T(8,128)S(1)}, f32[8,768]{1,0:T(8,128)S(1)}, u32[]{:S(2)}, u32[]{:S(2)}) collective-permute-start(f32[8,768]{1,0:T(8,128)S(1)} %get-tuple-element.65), channel_id=1, source_target_pairs={{0,64},{8,72},{16,80},{24,88},{32,96},{40,104},{48,112},{56,120},{... | collective-permute-start | bytes 73736 | tf_op jit(solution)/shard_map/sum_second/ppermute | solution.py:346
  81.9 17.8 %all-to-all-start.3 = ((f32[8,8,1408]{2,1,0:T(8,128)}), f32[8,8,1408]{2,1,0:T(8,128)S(1)}, u32[]{:S(2)}, u32[]{:S(2)}) async-start(f32[8,8,1408]{2,1,0:T(8,128)} %broadcast_in_dim.7), calls=%async_computation.3 | async-start | bytes 720896 | tf_op jit(solution)/shard_map/gather_first/all_to_all | solution.py:334
  85.3 3.7 %collective-permute-start.9 = (f32[8,768]{1,0:T(8,128)S(1)}, f32[8,768]{1,0:T(8,128)S(1)}, u32[]{:S(2)}, u32[]{:S(2)}) collective-permute-start(f32[8,768]{1,0:T(8,128)S(1)} %add_add_fusion.1), channel_id=1, source_target_pairs={{0,192},{8,200},{16,208},{24,216},{32,224},{40,232},{48,240},{56,2... | collective-permute-start | bytes 73736 | tf_op jit(solution)/shard_map/gather_first/ppermute | solution.py:346
  87.9 4.5 %collective-permute-start.8 = (f32[8,768]{1,0:T(8,128)S(1)}, f32[8,768]{1,0:T(8,128)S(1)}, u32[]{:S(2)}, u32[]{:S(2)}) collective-permute-start(f32[8,768]{1,0:T(8,128)S(1)} %add_add_fusion.1), channel_id=1, source_target_pairs={{0,128},{8,136},{16,144},{24,152},{32,160},{40,168},{48,176},{56,1... | collective-permute-start | bytes 73736 | tf_op jit(solution)/shard_map/gather_first/ppermute | solution.py:346
  88.4 4.2 %collective-permute-start.7 = (f32[8,768]{1,0:T(8,128)S(1)}, f32[8,768]{1,0:T(8,128)S(1)}, u32[]{:S(2)}, u32[]{:S(2)}) collective-permute-start(f32[8,768]{1,0:T(8,128)S(1)} %add_add_fusion.1), channel_id=1, source_target_pairs={{0,64},{8,72},{16,80},{24,88},{32,96},{40,104},{48,112},{56,120},{... | collective-permute-start | bytes 73736 | tf_op jit(solution)/shard_map/gather_first/ppermute | solution.py:346
  99.7 5.4 %collective-permute-start.11 = (f32[64,128]{1,0:T(8,128)S(1)}, f32[64,128]{1,0:T(8,128)S(1)}, u32[]{:S(2)}, u32[]{:S(2)}) collective-permute-start(f32[64,128]{1,0:T(8,128)S(1)} %get-tuple-element.62), channel_id=1, source_target_pairs={{0,128},{8,136},{16,144},{24,152},{32,160},{40,168},{48,176},{56,1... | collective-permute-start | bytes 98312 | tf_op jit(solution)/shard_map/gather_gram/ppermute | solution.py:346
  102.4 4.0 %collective-permute-start.10 = (f32[64,128]{1,0:T(8,128)S(1)}, f32[64,128]{1,0:T(8,128)S(1)}, u32[]{:S(2)}, u32[]{:S(2)}) collective-permute-start(f32[64,128]{1,0:T(8,128)S(1)} %get-tuple-element.62), channel_id=1, source_target_pairs={{0,64},{8,72},{16,80},{24,88},{32,96},{40,104},{48,112},{56,120},{... | collective-permute-start | bytes 98312 | tf_op jit(solution)/shard_map/gather_gram/ppermute | solution.py:346
  102.8 3.7 %collective-permute-start.12 = (f32[64,128]{1,0:T(8,128)S(1)}, f32[64,128]{1,0:T(8,128)S(1)}, u32[]{:S(2)}, u32[]{:S(2)}) collective-permute-start(f32[64,128]{1,0:T(8,128)S(1)} %get-tuple-element.62), channel_id=1, source_target_pairs={{0,192},{8,200},{16,208},{24,216},{32,224},{40,232},{48,240},{56,2... | collective-permute-start | bytes 98312 | tf_op jit(solution)/shard_map/gather_gram/ppermute | solution.py:346
  106.4 10.2 %collective-permute-start.13 = (f32[4,64,128]{2,1,0:T(8,128)S(1)}, f32[4,64,128]{2,1,0:T(8,128)S(1)}, u32[]{:S(2)}, u32[]{:S(2)}) collective-permute-start(f32[4,64,128]{2,1,0:T(8,128)S(1)} %pad_maximum_fusion.mine_ref), channel_id=1, source_target_pairs={{0,1},{1,0},{2,3},{3,2},{4,5},{5,4},{6,7},{7,6},{8,9},{9,8},{10,11... | collective-permute-start | bytes 393224 | tf_op jit(solution)/shard_map/gather_gram/ppermute | solution.py:371
  108.5 28.3 %collective-permute-start.16 = (f32[64,1280]{1,0:T(8,128)S(1)}, f32[64,1280]{1,0:T(8,128)S(1)}, u32[]{:S(2)}, u32[]{:S(2)}) collective-permute-start(f32[64,1280]{1,0:T(8,128)S(1)} %slice.9.a0_ref), channel_id=1, source_target_pairs={{0,192},{8,200},{16,208},{24,216},{32,224},{40,232},{48,240},{56,2... | collective-permute-start | bytes 983048 | tf_op jit(solution)/shard_map/gather_second/ppermute | solution.py:346
  111.5 25.3 %collective-permute-start.15 = (f32[64,1280]{1,0:T(8,128)S(1)}, f32[64,1280]{1,0:T(8,128)S(1)}, u32[]{:S(2)}, u32[]{:S(2)}) collective-permute-start(f32[64,1280]{1,0:T(8,128)S(1)} %slice.9.a0_ref), channel_id=1, source_target_pairs={{0,128},{8,136},{16,144},{24,152},{32,160},{40,168},{48,176},{56,1... | collective-permute-start | bytes 983048 | tf_op jit(solution)/shard_map/gather_second/ppermute | solution.py:346
  111.5 25.3 %collective-permute-start.14 = (f32[64,1280]{1,0:T(8,128)S(1)}, f32[64,1280]{1,0:T(8,128)S(1)}, u32[]{:S(2)}, u32[]{:S(2)}) collective-permute-start(f32[64,1280]{1,0:T(8,128)S(1)} %slice.9.a0_ref), channel_id=1, source_target_pairs={{0,64},{8,72},{16,80},{24,88},{32,96},{40,104},{48,112},{56,120},{... | collective-permute-start | bytes 983048 | tf_op jit(solution)/shard_map/gather_second/ppermute | solution.py:346
  113.1 25.2 %all-to-all-start.4 = ((f32[8,32,768]{2,1,0:T(8,128)}), f32[8,32,768]{2,1,0:T(8,128)S(1)}, u32[]{:S(2)}, u32[]{:S(2)}) async-start(f32[8,32,768]{2,1,0:T(8,128)} %broadcast_in_dim.8), calls=%async_computation.4 | async-start | bytes 1572864 | tf_op jit(solution)/shard_map/gather_second/all_to_all | solution.py:334
  135.3 0.8 copy-start
  136.1 0.7 copy-start.2
  138.3 1.0 copy-start.1
  139.3 0.9 copy-start.3

commit v3 on v2

--- a/solution.py
+++ b/solution.py
@@ -1,3 +1,5 @@
+import functools
+
 import jax
 import jax.numpy as jnp
 from jax import lax
@@ -11,6 +13,7 @@
 NX, NZ = 4, 8
 B, ROWS, COLS, HALF, TILE = 256, 1024, 2048, 128, 256
 A_COLS, B_COLS = 1280, 768
+WIDE = 4
 
 Z_GROUPS = [[x * NZ + z for z in range(NZ)] for x in range(NX)]
 Y_GROUPS = [[2 * y + core for y in range(4)] for core in range(2)]
@@ -85,10 +88,10 @@
 
 def product_b_kernel(parts_ref, trailing_ref, out_ref, held, arrived):
     copies = fetches(trailing_ref, held, A_COLS // TILE, B_COLS // TILE, arrived)
-    for tile, copy in enumerate(copies):
+    for copy in copies:
         copy.wait()
-        both = dot(parts_ref[...], held[:, tile_of(tile)])
-        out_ref[:, tile_of(tile)] = both[B:] + both[:B]
+    both = dot(parts_ref[...], held[...])
+    out_ref[...] = both[B:] + both[:B]
 
 
 def eliminate(work, unit, upper, inverse):
@@ -99,67 +102,55 @@
     eight = lax.broadcasted_iota(jnp.int32, (8, n), 0)
     unit[...] = (lane == row).astype(F32)
 
-    def splat(tile, i, k):
-        return jnp.broadcast_to(tile[i:i + 1, k:k + 1], (8, n))
-
     def reciprocal_root(value):
         guess = lax.rsqrt(value)
         return guess * (1.5 - 0.5 * value * guess * guess)
 
-    @pl.loop(0, tiles)
-    def _(block):
-        s, m = work[...], unit[...]
+    def total(terms):
+        while len(terms) > 1:
+            terms = [sum(terms[at:at + 2]) for at in range(0, len(terms), 2)]
+        return terms[0]
+
+    def step(block, rest):
         pivot_s, pivot_m = work[block], unit[block]
-        done_s, done_m = pivot_s, pivot_m
-        for half in (0, 4):
-            p = {(i, k): splat(pivot_s, half + i, half + k) for i in range(4) for k in range(i + 1)}
-            low, root, inv = {}, [], {}
-            for k in range(4):
-                for i in range(k, 4):
-                    value = p[i, k]
-                    for q in range(k):
-                        value = value - low[i, q] * low[k, q]
-                    if i == k:
-                        root.append(reciprocal_root(value))
-                    else:
-                        low[i, k] = value * root[k]
-            for i in range(4):
-                inv[i, i] = root[i]
-                for k in range(i):
-                    value = low[i, k] * inv[k, k]
-                    for q in range(k + 1, i):
-                        value = value + low[i, q] * inv[q, k]
-                    inv[i, k] = -value * root[i]
-
-            def combine(items):
-                out = []
-                for i in range(4):
-                    value = inv[i, 0] * items[0]
-                    for k in range(1, i + 1):
-                        value = value + inv[i, k] * items[k]
-                    out.append(value)
-                return out
-
-            rows_s = combine([jnp.broadcast_to(pivot_s[half + k:half + k + 1], (8, n)) for k in range(4)])
-            rows_m = combine([jnp.broadcast_to(pivot_m[half + k:half + k + 1], (8, n)) for k in range(4)])
-            for k in range(4):
-                done_s = jnp.where(eight == half + k, rows_s[k], done_s)
-                done_m = jnp.where(eight == half + k, rows_m[k], done_m)
-            if half == 0:
-                factors = combine([jnp.broadcast_to(pivot_s[:, k:k + 1], (8, n)) for k in range(4)])
-                for k in range(4):
-                    pivot_s = pivot_s - factors[k] * rows_s[k]
-                    pivot_m = pivot_m - factors[k] * rows_m[k]
-            below = row > 8 * block + half + 3
-            factors = combine([jnp.broadcast_to(s[:, :, half + k:half + k + 1], shape) for k in range(4)])
-            for k in range(4):
-                factor = jnp.where(below, factors[k], 0.0)
-                s = s - factor * rows_s[k]
-                m = m - factor * rows_m[k]
+        rows_s = [jnp.broadcast_to(pivot_s[k:k + 1], (8, n)) for k in range(8)]
+        rows_m = [jnp.broadcast_to(pivot_m[k:k + 1], (8, n)) for k in range(8)]
+        value = {(i, k): jnp.broadcast_to(pivot_s[i:i + 1, k:k + 1], (8, n)) for i in range(8) for k in range(i + 1)}
+        low, inv = {}, {}
+        for k in range(8):
+            root = reciprocal_root(value[k, k])
+            for i in range(k + 1, 8):
+                low[i, k] = value[i, k] * root
+            for i in range(k + 1, 8):
+                for q in range(k + 1, i + 1):
+                    value[i, q] = value[i, q] - low[i, k] * low[q, k]
+            inv[k, k] = root
+            for q in range(k):
+                inv[k, q] = -root * total([low[k, t] * inv[t, q] for t in range(q, k)])
+
+        def scaled(items):
+            return [total([inv[i, k] * items[k] for k in range(i + 1)]) for i in range(8)]
+
+        def solved(items):
+            return [total([inv[i, k] * items[i] for i in range(k, 8)]) for k in range(8)]
+
+        rows_s, rows_m = scaled(rows_s), scaled(rows_m)
+        done_s, done_m = rows_s[0], rows_m[0]
+        for k in range(1, 8):
+            done_s = jnp.where(eight == k, rows_s[k], done_s)
+            done_m = jnp.where(eight == k, rows_m[k], done_m)
         upper[block] = pltpu.roll(done_s, 8 * block, 1)
         inverse[block] = done_m
-        work[...] = pltpu.roll(s, n - 8, 2)
-        unit[...] = m
+        s, m = work[rest], unit[rest]
+        columns = [jnp.broadcast_to(s[:, :, k:k + 1], s.shape) for k in range(8)]
+        for column, change_s, change_m in zip(columns, solved(rows_s), solved(rows_m)):
+            s = s - column * change_s
+            m = m - column * change_m
+        work[rest] = pltpu.roll(s, n - 8, 2)
+        unit[rest] = m
+
+    for part in range(0, tiles, 4):
+        pl.loop(part, part + 4)(functools.partial(step, rest=slice(part, tiles)))
 
     upper[...] = jnp.where(lane >= row, upper[...], 0.0)
     inverse[...] = jnp.where(lane <= row, inverse[...], 0.0)
@@ -228,13 +219,14 @@
         results.append(pltpu.make_async_copy(source, target, semaphore))
         results[-1].start()
 
-    for tile in range(COLS // TILE):
-        columns = tile_of(tile)
+    for tile in range(0, COLS // TILE, WIDE):
+        columns = slice(tile * TILE, (tile + WIDE) * TILE)
         rows = dot_split(inv_ref[...], *split(sums[:, columns], 2))
         top[:, columns] = rows
         send(top.at[:, columns], top_ref.at[:, columns], sent.at[0, tile])
         change = dot(low_ref[...], rows.astype(BF16))
-        copies[tile].wait()
+        for copy in copies[tile:tile + WIDE]:
+            copy.wait()
         updated[:, columns] = (held[:, columns].astype(F32) - change).astype(BF16)
         send(updated.at[:, columns], updated_ref.at[:, columns], sent.at[1, tile])
     for result in results:
@@ -359,19 +351,23 @@
     with jax.named_scope("sum_first"):
         a, b = together((shift_x(a), scatter_z(b)))
         a, b = together((sum(a), jnp.sum(b, axis=0)))
+        a, gram = a[:, :A_COLS], a[:, A_COLS:]
     with jax.named_scope("sum_second"):
         b = shift_x([lax.dynamic_slice_in_dim(b, (x + k) % NX * 8, 8, 0) for k in range(NX)])
-        a, b = together((scatter_z(a), b))
+        a = scatter_z(a)
+        for apart in (1, 2, 4):
+            gram = gram + lax.ppermute(gram, "row", [(r, r ^ apart) for r in range(NX * NZ)])
+        a, b, gram = together((a, b, gram))
         a, b = together((jnp.sum(a, axis=0), sum(b)))
     with jax.named_scope("gather_first"):
-        a, b = together((gather(a, "row", Z_GROUPS), shift_x([b] * NX)))
-        a, b = a.reshape(64, A_COLS + HALF), jnp.concatenate(b, axis=0)
-    with jax.named_scope("gather_gram"):
-        gram_mine = jnp.stack(shift_x([a[:, A_COLS:]] * NX))
+        gram_mine = jnp.stack(shift_x([gram] * NX))
         gram_other = lax.ppermute(gram_mine, "col", SIBLING)
+        a, b, gram_mine, gram_other = together(
+            (gather(a, "row", Z_GROUPS), shift_x([b] * NX), gram_mine, gram_other)
+        )
     with jax.named_scope("gather_second"):
-        a = shift_x([a[:, :A_COLS]] * NX)
-        b = gather(b, "row", Z_GROUPS).reshape(NZ, NX, 8, B_COLS)
+        a = shift_x([a.reshape(64, A_COLS)] * NX)
+        b = gather(jnp.concatenate(b, axis=0), "row", Z_GROUPS).reshape(NZ, NX, 8, B_COLS)
     with jax.named_scope("factor"):
         r_factor, inverse, low = factor(ids, gram_mine, gram_other, parts)
     with jax.named_scope("update"):

time: 152 us -> 155 us (1.020)
  starting transfers between devices: 43.8 us -> 53.7 us
  Pallas kernels: 37.5 us -> 30.1 us
    all_to_all x4, waiting for transfers between devices: 19.9 us -> 9.23 us  [swap(): return lax.all_to_all(block, axis, 0, 0, axis_index_groups=groups)]
    ppermute x0 -> x3, waiting for transfers between devices: none -> 8.62 us  [local(): lax.ppermute(gram, 'row', [(r, r ^ apart) for r in range(NX * NZ)])]
    ppermute x0 -> x3, starting transfers between devices: none -> 6.96 us  [local(): lax.ppermute(gram, 'row', [(r, r ^ apart) for r in range(NX * NZ)])]
    ppermute x15, starting transfers between devices: 21.3 us -> 16.7 us  [shift_x(): lax.ppermute(pieces[k], 'row', X_ROUTES[k])]
    pallas_call x1, Pallas kernels: 18.6 us -> 14.1 us  [factor(): pl.pallas_call(factor_kernel, out_shape=(array(B, B), array(2 * B, B, dty...]
    ppermute x1, starting transfers between devices: 2 us -> 6.06 us  [local(): gram_other = lax.ppermute(gram_mine, 'col', SIBLING)]
    all_to_all x4, starting transfers between devices: 18.6 us -> 22.2 us  [swap(): return lax.all_to_all(block, axis, 0, 0, axis_index_groups=groups)]
    pallas_call x1, Pallas kernels: 8.93 us -> 6.53 us  [update(): pl.pallas_call(update_kernel, out_shape=(array(B, COLS), array(ROWS, COLS...]
  transfers between devices with their start and end apart: 21 -> 24, of which waited for: 12 -> 15; matrix products, arithmetic and copies ran while one was open for 1% -> 1% of each run, Pallas kernels for 12% -> 9%
where the time goes in v3:
time: 155 us; the launch traced here: 153 us
  starting transfers between devices  53.7 us (35%)
  waiting for transfers between devices  44.3 us (29%)
  Pallas kernels  30.1 us (19%)
  blocking collectives  13.4 us (9%)
  local copies, waits for them, and re-layouts  7.61 us (5%)
  other arithmetic  2.62 us (2%)
    ppermute x15, waiting for transfers between devices, shift_x(): lax.ppermute(pieces[k], 'row', X_ROUTES[k])  25 us
    all_to_all x4, starting transfers between devices, swap(): return lax.all_to_all(block, axis, 0, 0, axis_index_groups=groups)  22.2 us
    ppermute x15, starting transfers between devices, shift_x(): lax.ppermute(pieces[k], 'row', X_ROUTES[k])  16.7 us
    pallas_call x1, Pallas kernels, factor(): pl.pallas_call(factor_kernel, out_shape=(array(B, B), array(2 * B, B, dty...  14.1 us
    all_to_all x1, blocking collectives, swap(): return lax.all_to_all(block, axis, 0, 0, axis_index_groups=groups)  13.4 us
    all_to_all x4, waiting for transfers between devices, swap(): return lax.all_to_all(block, axis, 0, 0, axis_index_groups=groups)  9.23 us
    ppermute x3, waiting for transfers between devices, local(): lax.ppermute(gram, 'row', [(r, r ^ apart) for r in range(NX * NZ)])  8.62 us
    ppermute x3, starting transfers between devices, local(): lax.ppermute(gram, 'row', [(r, r ^ apart) for r in range(NX * NZ)])  6.96 us
  transfers between devices with their start and end apart: 24, of which 15 were waited for; matrix products, arithmetic and copies ran while one was open for 1% of the time, Pallas kernels for 9%

profile of v3, /device:TPU:1, one launch (start us, length us, event | category | flops | bytes accessed | tf_op | source)
XLA Modules:
  0.0 152.6 jit_solution(18332334067186133683)
XLA Ops:
  1.6 13.4 %all_to_all.25.mine_ref = f32[4,32,1024]{2,1,0:T(8,128)S(1)} all-to-all(f32[4,32,1024]{2,1,0:T(8,128)S(1)} %broadcast_in_dim.6), channel_id=1, replica_groups={{0,2,4,6},{1,3,5,7},{8,10,12,14},{9,11,13,15},{16,18,20,22},{17,19,21,2..., dimensions={0} | all-to-all | bytes 1048576 | tf_op jit(solution)/shard_map/gather_panel/all_to_all | solution.py:326
  15.0 1.9 %collective-permute-start = (f32[4,32,1024]{2,1,0:T(8,128)S(1)}, f32[4,32,1024]{2,1,0:T(8,128)S(1)}, u32[]{:S(2)}, u32[]{:S(2)}) collective-permute-start(f32[4,32,1024]{2,1,0:T(8,128)S(1)} %all_to_all.25.mine_ref), channel_id=1, source_target_pairs={{0,1},{1,0},{2,3},{3,2},{4,5},{5,4},{6,7},{7,6},{8,9},{9,8},{10,11... | collective-permute-start | bytes 1572872 | tf_op jit(solution)/shard_map/gather_panel/ppermute | solution.py:346
  16.9 1.5 collective-permute-done.other_ref
  18.4 6.2 %product.2 = (bf16[512,1024]{1,0:T(8,128)(2,1)S(1)}, f32[64,1408]{1,0:T(8,128)S(1)}, f32[64,1408]{1,0:T(8,128)S(1)}, f32[64,1408]{1,0:T(8,128)S(1)}, f32[64,1408]{1,0:T(8,128)S(1)}) custom-call(s32[2]{0:T(128)S(1)} %pad_add_fusion.ids_ref, f32[4,32,1024]{2,1,0:T(8,128)S(1)} %all_to_all.25.mine_ref, f32[4,32,1024]{2,1,0:T(8,128)S(1)} %collective-permute-done.other_ref, ...), custom_call_target="tpu_custom_call" | custom-call | flops 2400000000 | bytes 6000000 | tf_op jit(solution)/shard_map/product/pallas_call | solution.py:255
  24.6 3.3 %product.3 = f32[256,768]{1,0:T(8,128)} custom-call(bf16[512,1024]{1,0:T(8,128)(2,1)S(1)} %get-tuple-element.39.parts_ref, bf16[1024,2048]{1,0:T(8,128)(2,1)} %trailing_ref.5), custom_call_target="tpu_custom_call" | custom-call | flops 1300000000 | bytes 4000000 | tf_op jit(solution)/shard_map/product/pallas_call | solution.py:274
  27.9 8.2 %all-to-all-start.1 = ((f32[8,32,768]{2,1,0:T(8,128)}), f32[8,32,768]{2,1,0:T(8,128)}, u32[]{:S(2)}, u32[]{:S(2)}) async-start(f32[8,32,768]{2,1,0:T(8,128)} %bitcast.3), calls=%async_computation.1 | async-start | bytes 1572864 | tf_op jit(solution)/shard_map/sum_first/all_to_all | solution.py:326
  36.1 1.2 collective-permute-start.1
  37.3 2.5 %collective-permute-start.2 = (f32[64,1408]{1,0:T(8,128)S(1)}, f32[64,1408]{1,0:T(8,128)S(1)}, u32[]{:S(2)}, u32[]{:S(2)}) collective-permute-start(f32[64,1408]{1,0:T(8,128)S(1)} %get-tuple-element.37), channel_id=1, source_target_pairs={{0,128},{8,136},{16,144},{24,152},{32,160},{40,168},{48,176},{56,1... | collective-permute-start | bytes 1081352 | tf_op jit(solution)/shard_map/sum_first/ppermute | solution.py:338
  39.7 1.1 collective-permute-start.3
  40.9 5.8 %collective-permute-done.1 = f32[64,1408]{1,0:T(8,128)S(1)} collective-permute-done((f32[64,1408]{1,0:T(8,128)S(1)}, f32[64,1408]{1,0:T(8,128)S(1)}, u32[]{:S(2)}, u32[]{:S(2)}) %collective-permute-start.1) | collective-permute-done | bytes 360480 | tf_op jit(solution)/shard_map/sum_first/ppermute | solution.py:338
  46.7 8.6 %collective-permute-done.2 = f32[64,1408]{1,0:T(8,128)S(1)} collective-permute-done((f32[64,1408]{1,0:T(8,128)S(1)}, f32[64,1408]{1,0:T(8,128)S(1)}, u32[]{:S(2)}, u32[]{:S(2)}) %collective-permute-start.2) | collective-permute-done | bytes 360480 | tf_op jit(solution)/shard_map/sum_first/ppermute | solution.py:338
  56.0 3.7 %all-to-all-done.1 = f32[8,32,768]{2,1,0:T(8,128)} async-done(((f32[8,32,768]{2,1,0:T(8,128)}), f32[8,32,768]{2,1,0:T(8,128)}, u32[]{:S(2)}, u32[]{:S(2)}) %all-to-all-start.1) | async-done | bytes 786464 | tf_op jit(solution)/shard_map/sum_first/all_to_all | solution.py:326
  59.7 1.2 reduce_sum.18
  60.9 1.3 add_add_fusion
  63.0 3.4 %all-to-all-start.2 = ((f32[8,8,1280]{2,1,0:T(8,128)}), f32[8,8,1280]{2,1,0:T(8,128)S(1)}, u32[]{:S(2)}, u32[]{:S(2)}) async-start(f32[8,8,1280]{2,1,0:T(8,128)} %slice_bitcast_fusion), calls=%async_computation.2 | async-start | bytes 655360 | tf_op jit(solution)/shard_map/sum_second/all_to_all | solution.py:326
  66.4 1.4 collective-permute-start.7
  67.8 6.7 %collective-permute-done.7 = f32[64,128]{1,0:T(8,128)S(1)} collective-permute-done((f32[64,128]{1,0:T(8,128)S(1)}, f32[64,128]{1,0:T(8,128)S(1)}, u32[]{:S(2)}, u32[]{:S(2)}) %collective-permute-start.7) | collective-permute-done | bytes 32800 | tf_op jit(solution)/shard_map/sum_second/ppermute | solution.py:359
  74.5 1.8 %collective-permute-start.8 = (f32[64,128]{1,0:T(8,128)S(1)}, f32[64,128]{1,0:T(8,128)S(1)}, u32[]{:S(2)}, u32[]{:S(2)}) collective-permute-start(f32[64,128]{1,0:T(8,128)S(1)} %slice_add_fusion), channel_id=1, source_target_pairs={{0,16},{8,24},{16,0},{24,8},{32,48},{40,56},{48,32},{56,40},{64,80... | collective-permute-start | bytes 98312 | tf_op jit(solution)/shard_map/sum_second/ppermute | solution.py:359
  76.3 1.9 %collective-permute-done.8 = f32[64,128]{1,0:T(8,128)S(1)} collective-permute-done((f32[64,128]{1,0:T(8,128)S(1)}, f32[64,128]{1,0:T(8,128)S(1)}, u32[]{:S(2)}, u32[]{:S(2)}) %collective-permute-start.8) | collective-permute-done | bytes 32800 | tf_op jit(solution)/shard_map/sum_second/ppermute | solution.py:359
  78.2 3.9 %collective-permute-start.9 = (f32[64,128]{1,0:T(8,128)S(1)}, f32[64,128]{1,0:T(8,128)S(1)}, u32[]{:S(2)}, u32[]{:S(2)}) collective-permute-start(f32[64,128]{1,0:T(8,128)S(1)} %add.81), channel_id=1, source_target_pairs={{0,32},{8,40},{16,48},{24,56},{32,0},{40,8},{48,16},{56,24},{64,96... | collective-permute-start | bytes 98312 | tf_op jit(solution)/shard_map/sum_second/ppermute | solution.py:359
  82.0 4.5 %collective-permute-start.6 = (f32[8,768]{1,0:T(8,128)S(1)}, f32[8,768]{1,0:T(8,128)S(1)}, u32[]{:S(2)}, u32[]{:S(2)}) collective-permute-start(f32[8,768]{1,0:T(8,128)S(1)} %get-tuple-element.67), channel_id=1, source_target_pairs={{0,192},{8,200},{16,208},{24,216},{32,224},{40,232},{48,240},{56,2... | collective-permute-start | bytes 73736 | tf_op jit(solution)/shard_map/sum_second/ppermute | solution.py:338
  87.7 3.0 %collective-permute-done.5 = f32[8,768]{1,0:T(8,128)S(1)} collective-permute-done((f32[8,768]{1,0:T(8,128)S(1)}, f32[8,768]{1,0:T(8,128)S(1)}, u32[]{:S(2)}, u32[]{:S(2)}) %collective-permute-start.5) | collective-permute-done | bytes 24608 | tf_op jit(solution)/shard_map/sum_second/ppermute | solution.py:338
  91.8 3.8 %all-to-all-start.3 = ((f32[8,8,1280]{2,1,0:T(8,128)}), f32[8,8,1280]{2,1,0:T(8,128)S(1)}, u32[]{:S(2)}, u32[]{:S(2)}) async-start(f32[8,8,1280]{2,1,0:T(8,128)} %broadcast_in_dim.7), calls=%async_computation.3 | async-start | bytes 655360 | tf_op jit(solution)/shard_map/gather_first/all_to_all | solution.py:326
  98.3 2.2 %collective-permute-done.14 = f32[64,128]{1,0:T(8,128)S(1)} collective-permute-done((f32[64,128]{1,0:T(8,128)S(1)}, f32[64,128]{1,0:T(8,128)S(1)}, u32[]{:S(2)}, u32[]{:S(2)}) %collective-permute-start.14) | collective-permute-done | bytes 32800 | tf_op jit(solution)/shard_map/gather_first/ppermute | solution.py:338
  100.9 6.1 %collective-permute-start.16 = (f32[4,64,128]{2,1,0:T(8,128)S(1)}, f32[4,64,128]{2,1,0:T(8,128)S(1)}, u32[]{:S(2)}, u32[]{:S(2)}) collective-permute-start(f32[4,64,128]{2,1,0:T(8,128)S(1)} %pad_maximum_fusion.mine_ref), channel_id=1, source_target_pairs={{0,1},{1,0},{2,3},{3,2},{4,5},{5,4},{6,7},{7,6},{8,9},{9,8},{10,11... | collective-permute-start | bytes 393224 | tf_op jit(solution)/shard_map/gather_first/ppermute | solution.py:364
  107.0 1.4 collective-permute-start.12
  110.0 2.6 %collective-permute-done.11 = f32[8,768]{1,0:T(8,128)S(1)} collective-permute-done((f32[8,768]{1,0:T(8,128)S(1)}, f32[8,768]{1,0:T(8,128)S(1)}, u32[]{:S(2)}, u32[]{:S(2)}) %collective-permute-start.11) | collective-permute-done | bytes 24608 | tf_op jit(solution)/shard_map/gather_first/ppermute | solution.py:338
  116.1 6.8 %all-to-all-start.4 = ((f32[8,32,768]{2,1,0:T(8,128)}), f32[8,32,768]{2,1,0:T(8,128)S(1)}, u32[]{:S(2)}, u32[]{:S(2)}) async-start(f32[8,32,768]{2,1,0:T(8,128)} %broadcast_in_dim.8), calls=%async_computation.4 | async-start | bytes 1572864 | tf_op jit(solution)/shard_map/gather_second/all_to_all | solution.py:326
  122.9 14.1 %factor.1 = (f32[256,256]{1,0:T(8,128)}, bf16[512,256]{1,0:T(8,128)(2,1)S(1)}, bf16[1024,256]{1,0:T(8,128)(2,1)S(1)}) custom-call(s32[2]{0:T(128)S(1)} %pad_add_fusion.ids_ref, f32[4,64,128]{2,1,0:T(8,128)S(1)} %pad_maximum_fusion.mine_ref, f32[4,64,128]{2,1,0:T(8,128)S(1)} %collective-permute-done.16.other_ref, ...), custom_call_target="tpu_custom_call" | custom-call | flops 20000000000 | bytes 3000000 | tf_op jit(solution)/shard_map/factor/pallas_call | solution.py:286
  138.4 5.5 %all-to-all-done.4 = f32[8,32,768]{2,1,0:T(8,128)S(1)} async-done(((f32[8,32,768]{2,1,0:T(8,128)}), f32[8,32,768]{2,1,0:T(8,128)S(1)}, u32[]{:S(2)}, u32[]{:S(2)}) %all-to-all-start.4) | async-done | bytes 786464 | tf_op jit(solution)/shard_map/gather_second/all_to_all | solution.py:326
  144.0 1.0 copy-done.1
  146.0 6.5 %update.1 = (f32[256,2048]{1,0:T(8,128)}, bf16[1024,2048]{1,0:T(8,128)(2,1)}) custom-call(s32[2]{0:T(128)S(1)} %pad_add_fusion.ids_ref, f32[64,1280]{1,0:T(8,128)S(1)} %bitcast.16, f32[64,1280]{1,0:T(8,128)S(1)} %collective-permute-done.17.a1_ref, f32[64,1280]{1,0:T(8,128)S(1)} %collective-permute-done.18.a2_ref, ...), custom_call_target="tpu_custom_call" | custom-call | flops 3000000000 | bytes 12000000 | tf_op jit(solution)/shard_map/update/pallas_call | solution.py:304
  (49 shorter events, 15.4 us)
Async XLA Ops:
  15.0 3.4 %collective-permute-start = (f32[4,32,1024]{2,1,0:T(8,128)S(1)}, f32[4,32,1024]{2,1,0:T(8,128)S(1)}, u32[]{:S(2)}, u32[]{:S(2)}) collective-permute-start(f32[4,32,1024]{2,1,0:T(8,128)S(1)} %all_to_all.25.mine_ref), channel_id=1, source_target_pairs={{0,1},{1,0},{2,3},{3,2},{4,5},{5,4},{6,7},{7,6},{8,9},{9,8},{10,11... | collective-permute-start | bytes 1572872 | tf_op jit(solution)/shard_map/gather_panel/ppermute | solution.py:346
  27.9 31.9 %all-to-all-start.1 = ((f32[8,32,768]{2,1,0:T(8,128)}), f32[8,32,768]{2,1,0:T(8,128)}, u32[]{:S(2)}, u32[]{:S(2)}) async-start(f32[8,32,768]{2,1,0:T(8,128)} %bitcast.3), calls=%async_computation.1 | async-start | bytes 1572864 | tf_op jit(solution)/shard_map/sum_first/all_to_all | solution.py:326
  36.1 10.6 %collective-permute-start.1 = (f32[64,1408]{1,0:T(8,128)S(1)}, f32[64,1408]{1,0:T(8,128)S(1)}, u32[]{:S(2)}, u32[]{:S(2)}) collective-permute-start(f32[64,1408]{1,0:T(8,128)S(1)} %get-tuple-element.36), channel_id=1, source_target_pairs={{0,64},{8,72},{16,80},{24,88},{32,96},{40,104},{48,112},{56,120},{... | collective-permute-start | bytes 1081352 | tf_op jit(solution)/shard_map/sum_first/ppermute | solution.py:338
  37.3 18.0 %collective-permute-start.2 = (f32[64,1408]{1,0:T(8,128)S(1)}, f32[64,1408]{1,0:T(8,128)S(1)}, u32[]{:S(2)}, u32[]{:S(2)}) collective-permute-start(f32[64,1408]{1,0:T(8,128)S(1)} %get-tuple-element.37), channel_id=1, source_target_pairs={{0,128},{8,136},{16,144},{24,152},{32,160},{40,168},{48,176},{56,1... | collective-permute-start | bytes 1081352 | tf_op jit(solution)/shard_map/sum_first/ppermute | solution.py:338
  39.7 16.3 %collective-permute-start.3 = (f32[64,1408]{1,0:T(8,128)S(1)}, f32[64,1408]{1,0:T(8,128)}, u32[]{:S(2)}, u32[]{:S(2)}) collective-permute-start(f32[64,1408]{1,0:T(8,128)S(1)} %get-tuple-element.38), channel_id=1, source_target_pairs={{0,192},{8,200},{16,208},{24,216},{32,224},{40,232},{48,240},{56,2... | collective-permute-start | bytes 1081352 | tf_op jit(solution)/shard_map/sum_first/ppermute | solution.py:338
  46.7 8.6 %copy-start.4 = (f32[64,1408]{1,0:T(8,128)}, f32[64,1408]{1,0:T(8,128)S(1)}, u32[]{:S(2)}) copy-start(f32[64,1408]{1,0:T(8,128)S(1)} %collective-permute-done.1) | copy-start | bytes 1081348
  55.3 0.7 copy-start.5
  63.0 28.1 %all-to-all-start.2 = ((f32[8,8,1280]{2,1,0:T(8,128)}), f32[8,8,1280]{2,1,0:T(8,128)S(1)}, u32[]{:S(2)}, u32[]{:S(2)}) async-start(f32[8,8,1280]{2,1,0:T(8,128)} %slice_bitcast_fusion), calls=%async_computation.2 | async-start | bytes 655360 | tf_op jit(solution)/shard_map/sum_second/all_to_all | solution.py:326
  66.4 8.1 %collective-permute-start.7 = (f32[64,128]{1,0:T(8,128)S(1)}, f32[64,128]{1,0:T(8,128)S(1)}, u32[]{:S(2)}, u32[]{:S(2)}) collective-permute-start(f32[64,128]{1,0:T(8,128)S(1)} %slice.7), channel_id=1, source_target_pairs={{0,8},{8,0},{16,24},{24,16},{32,40},{40,32},{48,56},{56,48},{64,72... | collective-permute-start | bytes 98312 | tf_op jit(solution)/shard_map/sum_second/ppermute | solution.py:359
  74.5 3.7 %collective-permute-start.8 = (f32[64,128]{1,0:T(8,128)S(1)}, f32[64,128]{1,0:T(8,128)S(1)}, u32[]{:S(2)}, u32[]{:S(2)}) collective-permute-start(f32[64,128]{1,0:T(8,128)S(1)} %slice_add_fusion), channel_id=1, source_target_pairs={{0,16},{8,24},{16,0},{24,8},{32,48},{40,56},{48,32},{56,40},{64,80... | collective-permute-start | bytes 98312 | tf_op jit(solution)/shard_map/sum_second/ppermute | solution.py:359
  78.2 9.5 %collective-permute-start.9 = (f32[64,128]{1,0:T(8,128)S(1)}, f32[64,128]{1,0:T(8,128)S(1)}, u32[]{:S(2)}, u32[]{:S(2)}) collective-permute-start(f32[64,128]{1,0:T(8,128)S(1)} %add.81), channel_id=1, source_target_pairs={{0,32},{8,40},{16,48},{24,56},{32,0},{40,8},{48,16},{56,24},{64,96... | collective-permute-start | bytes 98312 | tf_op jit(solution)/shard_map/sum_second/ppermute | solution.py:359
  82.0 5.7 %collective-permute-start.6 = (f32[8,768]{1,0:T(8,128)S(1)}, f32[8,768]{1,0:T(8,128)S(1)}, u32[]{:S(2)}, u32[]{:S(2)}) collective-permute-start(f32[8,768]{1,0:T(8,128)S(1)} %get-tuple-element.67), channel_id=1, source_target_pairs={{0,192},{8,200},{16,208},{24,216},{32,224},{40,232},{48,240},{56,2... | collective-permute-start | bytes 73736 | tf_op jit(solution)/shard_map/sum_second/ppermute | solution.py:338
  86.6 4.2 %collective-permute-start.5 = (f32[8,768]{1,0:T(8,128)S(1)}, f32[8,768]{1,0:T(8,128)S(1)}, u32[]{:S(2)}, u32[]{:S(2)}) collective-permute-start(f32[8,768]{1,0:T(8,128)S(1)} %get-tuple-element.68), channel_id=1, source_target_pairs={{0,128},{8,136},{16,144},{24,152},{32,160},{40,168},{48,176},{56,1... | collective-permute-start | bytes 73736 | tf_op jit(solution)/shard_map/sum_second/ppermute | solution.py:338
  87.1 4.0 %collective-permute-start.4 = (f32[8,768]{1,0:T(8,128)S(1)}, f32[8,768]{1,0:T(8,128)S(1)}, u32[]{:S(2)}, u32[]{:S(2)}) collective-permute-start(f32[8,768]{1,0:T(8,128)S(1)} %get-tuple-element.69), channel_id=1, source_target_pairs={{0,64},{8,72},{16,80},{24,88},{32,96},{40,104},{48,112},{56,120},{... | collective-permute-start | bytes 73736 | tf_op jit(solution)/shard_map/sum_second/ppermute | solution.py:338
  91.8 21.1 %all-to-all-start.3 = ((f32[8,8,1280]{2,1,0:T(8,128)}), f32[8,8,1280]{2,1,0:T(8,128)S(1)}, u32[]{:S(2)}, u32[]{:S(2)}) async-start(f32[8,8,1280]{2,1,0:T(8,128)} %broadcast_in_dim.7), calls=%async_computation.3 | async-start | bytes 655360 | tf_op jit(solution)/shard_map/gather_first/all_to_all | solution.py:326
  95.6 2.8 %collective-permute-start.15 = (f32[64,128]{1,0:T(8,128)S(1)}, f32[64,128]{1,0:T(8,128)S(1)}, u32[]{:S(2)}, u32[]{:S(2)}) collective-permute-start(f32[64,128]{1,0:T(8,128)S(1)} %add.82), channel_id=1, source_target_pairs={{0,192},{8,200},{16,208},{24,216},{32,224},{40,232},{48,240},{56,2... | collective-permute-start | bytes 98312 | tf_op jit(solution)/shard_map/gather_first/ppermute | solution.py:338
  96.3 4.3 %collective-permute-start.14 = (f32[64,128]{1,0:T(8,128)S(1)}, f32[64,128]{1,0:T(8,128)S(1)}, u32[]{:S(2)}, u32[]{:S(2)}) collective-permute-start(f32[64,128]{1,0:T(8,128)S(1)} %add.82), channel_id=1, source_target_pairs={{0,128},{8,136},{16,144},{24,152},{32,160},{40,168},{48,176},{56,1... | collective-permute-start | bytes 98312 | tf_op jit(solution)/shard_map/gather_first/ppermute | solution.py:338
  96.9 4.0 %collective-permute-start.13 = (f32[64,128]{1,0:T(8,128)S(1)}, f32[64,128]{1,0:T(8,128)S(1)}, u32[]{:S(2)}, u32[]{:S(2)}) collective-permute-start(f32[64,128]{1,0:T(8,128)S(1)} %add.82), channel_id=1, source_target_pairs={{0,64},{8,72},{16,80},{24,88},{32,96},{40,104},{48,112},{56,120},{... | collective-permute-start | bytes 98312 | tf_op jit(solution)/shard_map/gather_first/ppermute | solution.py:338
  100.9 12.0 %collective-permute-start.16 = (f32[4,64,128]{2,1,0:T(8,128)S(1)}, f32[4,64,128]{2,1,0:T(8,128)S(1)}, u32[]{:S(2)}, u32[]{:S(2)}) collective-permute-start(f32[4,64,128]{2,1,0:T(8,128)S(1)} %pad_maximum_fusion.mine_ref), channel_id=1, source_target_pairs={{0,1},{1,0},{2,3},{3,2},{4,5},{5,4},{6,7},{7,6},{8,9},{9,8},{10,11... | collective-permute-start | bytes 393224 | tf_op jit(solution)/shard_map/gather_first/ppermute | solution.py:364
  107.0 3.0 %collective-permute-start.12 = (f32[8,768]{1,0:T(8,128)S(1)}, f32[8,768]{1,0:T(8,128)S(1)}, u32[]{:S(2)}, u32[]{:S(2)}) collective-permute-start(f32[8,768]{1,0:T(8,128)S(1)} %add_add_fusion.1), channel_id=1, source_target_pairs={{0,192},{8,200},{16,208},{24,216},{32,224},{40,232},{48,240},{56,2... | collective-permute-start | bytes 73736 | tf_op jit(solution)/shard_map/gather_first/ppermute | solution.py:338
  108.4 4.2 %collective-permute-start.11 = (f32[8,768]{1,0:T(8,128)S(1)}, f32[8,768]{1,0:T(8,128)S(1)}, u32[]{:S(2)}, u32[]{:S(2)}) collective-permute-start(f32[8,768]{1,0:T(8,128)S(1)} %add_add_fusion.1), channel_id=1, source_target_pairs={{0,128},{8,136},{16,144},{24,152},{32,160},{40,168},{48,176},{56,1... | collective-permute-start | bytes 73736 | tf_op jit(solution)/shard_map/gather_first/ppermute | solution.py:338
  109.0 3.9 %collective-permute-start.10 = (f32[8,768]{1,0:T(8,128)S(1)}, f32[8,768]{1,0:T(8,128)S(1)}, u32[]{:S(2)}, u32[]{:S(2)}) collective-permute-start(f32[8,768]{1,0:T(8,128)S(1)} %add_add_fusion.1), channel_id=1, source_target_pairs={{0,64},{8,72},{16,80},{24,88},{32,96},{40,104},{48,112},{56,120},{... | collective-permute-start | bytes 73736 | tf_op jit(solution)/shard_map/gather_first/ppermute | solution.py:338
  112.9 25.5 %collective-permute-start.19 = (f32[64,1280]{1,0:T(8,128)S(1)}, f32[64,1280]{1,0:T(8,128)S(1)}, u32[]{:S(2)}, u32[]{:S(2)}) collective-permute-start(f32[64,1280]{1,0:T(8,128)S(1)} %bitcast.13), channel_id=1, source_target_pairs={{0,192},{8,200},{16,208},{24,216},{32,224},{40,232},{48,240},{56,2... | collective-permute-start | bytes 983048 | tf_op jit(solution)/shard_map/gather_second/ppermute | solution.py:338
  113.7 24.8 %collective-permute-start.18 = (f32[64,1280]{1,0:T(8,128)S(1)}, f32[64,1280]{1,0:T(8,128)S(1)}, u32[]{:S(2)}, u32[]{:S(2)}) collective-permute-start(f32[64,1280]{1,0:T(8,128)S(1)} %bitcast.14), channel_id=1, source_target_pairs={{0,128},{8,136},{16,144},{24,152},{32,160},{40,168},{48,176},{56,1... | collective-permute-start | bytes 983048 | tf_op jit(solution)/shard_map/gather_second/ppermute | solution.py:338
  114.5 23.9 %collective-permute-start.17 = (f32[64,1280]{1,0:T(8,128)S(1)}, f32[64,1280]{1,0:T(8,128)S(1)}, u32[]{:S(2)}, u32[]{:S(2)}) collective-permute-start(f32[64,1280]{1,0:T(8,128)S(1)} %bitcast.15), channel_id=1, source_target_pairs={{0,64},{8,72},{16,80},{24,88},{32,96},{40,104},{48,112},{56,120},{... | collective-permute-start | bytes 983048 | tf_op jit(solution)/shard_map/gather_second/ppermute | solution.py:338
  116.1 27.8 %all-to-all-start.4 = ((f32[8,32,768]{2,1,0:T(8,128)}), f32[8,32,768]{2,1,0:T(8,128)S(1)}, u32[]{:S(2)}, u32[]{:S(2)}) async-start(f32[8,32,768]{2,1,0:T(8,128)} %broadcast_in_dim.8), calls=%async_computation.4 | async-start | bytes 1572864 | tf_op jit(solution)/shard_map/gather_second/all_to_all | solution.py:326
  136.9 0.8 copy-start
  137.7 0.7 copy-start.2
  144.0 1.0 copy-start.1
  145.0 0.9 copy-start.3

commit v4 on v3

v4 whole, which is shorter than its diff:
```python
import functools

import jax
import jax.numpy as jnp
from jax import lax
from jax.experimental import pallas as pl
from jax.experimental.pallas import tpu as pltpu
from jax.sharding import PartitionSpec as P

F32 = jnp.float32
BF16 = jnp.bfloat16
HIGHEST = lax.Precision.HIGHEST
NX, NZ = 4, 8
B, ROWS, COLS, HALF, TILE = 256, 1024, 2048, 128, 256
WIDE = 4

Z_GROUPS = [[x * NZ + z for z in range(NZ)] for x in range(NX)]
SIBLING = [(c, c ^ 1) for c in range(8)]
Y_ROUTES = [[(c, (c + 2 * k) % 8) for c in range(8)] for k in range(4)]
X_ROUTES = [[(x * NZ + z, (x + k) % NX * NZ + z) for x in range(NX) for z in range(NZ)] for k in range(NX)]


def dot(a, b, contract=((1,), (0,)), precision=None):
    return lax.dot_general(a, b, (contract, ((), ())), precision=precision, preferred_element_type=F32)


def split(value, count):
    terms = []
    for _ in range(count):
        terms.append(value.astype(BF16))
        value = value - terms[-1].astype(F32)
    return terms


def dot_split(left, high, low):
    rows = left.shape[0] // 2
    both = dot(left, high)
    return both[rows:] + dot(left[:rows], low) + both[:rows]


def tile_of(index):
    return slice(index * TILE, index * TILE + TILE)


def fetches(source_ref, target_ref, arrived):
    copies = [
        pltpu.make_async_copy(source_ref.at[:, tile_of(tile)], target_ref.at[:, tile_of(tile)], arrived.at[tile])
        for tile in range(COLS // TILE)
    ]
    for copy in copies:
        copy.start()
    return copies


def product_kernel(ids_ref, mine_ref, other_ref, trailing_ref, parts_ref, *refs):
    pieces, (held, third, whole, gram, arrived) = refs[:NX], refs[NX:]
    copies = fetches(trailing_ref, held, arrived)
    core, x, y = ids_ref[0], ids_ref[1], ids_ref[2]
    for k in range(4):
        for ref, offset in ((mine_ref, 32 * core), (other_ref, 32 - 32 * core)):
            start = 64 * lax.rem(y + 4 - k, 4) + offset
            high, middle, low = split(ref[k], 3)
            parts_ref[pl.ds(pl.multiple_of(start, 32), 32)] = high
            parts_ref[pl.ds(pl.multiple_of(B + start, 32), 32)] = middle
            third[pl.ds(pl.multiple_of(start, 32), 32)] = low
    half = pl.multiple_of(core * HALF, HALF)
    last = ((1,), (1,))
    one = dot(parts_ref[...], parts_ref[pl.ds(half, HALF)], last)
    two = dot(parts_ref[...], parts_ref[pl.ds(pl.multiple_of(B + half, HALF), HALF)], last)
    small = dot(third[...], parts_ref[pl.ds(half, HALF)], last) + dot(parts_ref[:B], third[pl.ds(half, HALF)], last)
    gram[...] = small + two[B:] + one[B:] + two[:B] + one[:B]

    def hand_out(source, columns):
        for k in range(NX):
            start = pl.multiple_of(64 * lax.rem(x + k, NX), 64)
            pieces[k][:, columns] = source[pl.ds(start, 64)]

    hand_out(gram, slice(COLS, COLS + HALF))
    for tile in range(0, COLS // TILE, 2):
        for copy in copies[tile:tile + 2]:
            copy.wait()
        columns = slice(tile * TILE, (tile + 2) * TILE)
        both = dot(parts_ref[...], held[:, columns])
        slot = whole.at[tile // 2 % 2]
        slot[...] = both[B:] + both[:B]
        hand_out(slot, columns)


def eliminate(work, unit, upper, inverse):
    n, tiles = HALF, HALF // 8
    shape = (tiles, 8, n)
    row = 8 * lax.broadcasted_iota(jnp.int32, shape, 0) + lax.broadcasted_iota(jnp.int32, shape, 1)
    lane = lax.broadcasted_iota(jnp.int32, shape, 2)
    eight = lax.broadcasted_iota(jnp.int32, (8, n), 0)
    unit[...] = (lane == row).astype(F32)

    def reciprocal_root(value):
        guess = lax.rsqrt(value)
        return guess * (1.5 - 0.5 * value * guess * guess)

    def total(terms):
        while len(terms) > 1:
            terms = [sum(terms[at:at + 2]) for at in range(0, len(terms), 2)]
        return terms[0]

    def step(block, rest):
        pivot_s, pivot_m = work[block], unit[block]
        rows_s = [jnp.broadcast_to(pivot_s[k:k + 1], (8, n)) for k in range(8)]
        rows_m = [jnp.broadcast_to(pivot_m[k:k + 1], (8, n)) for k in range(8)]
        value = {(i, k): jnp.broadcast_to(pivot_s[i:i + 1, k:k + 1], (8, n)) for i in range(8) for k in range(i + 1)}
        low, inv = {}, {}
        for k in range(8):
            root = reciprocal_root(value[k, k])
            for i in range(k + 1, 8):
                low[i, k] = value[i, k] * root
            for i in range(k + 1, 8):
                for q in range(k + 1, i + 1):
                    value[i, q] = value[i, q] - low[i, k] * low[q, k]
            inv[k, k] = root
            for q in range(k):
                inv[k, q] = -root * total([low[k, t] * inv[t, q] for t in range(q, k)])

        def scaled(items):
            return [total([inv[i, k] * items[k] for k in range(i + 1)]) for i in range(8)]

        def solved(items):
            return [total([inv[i, k] * items[i] for i in range(k, 8)]) for k in range(8)]

        rows_s, rows_m = scaled(rows_s), scaled(rows_m)
        done_s, done_m = rows_s[0], rows_m[0]
        for k in range(1, 8):
            done_s = jnp.where(eight == k, rows_s[k], done_s)
            done_m = jnp.where(eight == k, rows_m[k], done_m)
        upper[block] = pltpu.roll(done_s, 8 * block, 1)
        inverse[block] = done_m
        s, m = work[rest], unit[rest]
        columns = [jnp.broadcast_to(s[:, :, k:k + 1], s.shape) for k in range(8)]
        for column, change_s, change_m in zip(columns, solved(rows_s), solved(rows_m)):
            s = s - column * change_s
            m = m - column * change_m
        work[rest] = pltpu.roll(s, n - 8, 2)
        unit[rest] = m

    for part in range(0, tiles, 4):
        pl.loop(part, part + 4)(functools.partial(step, rest=slice(part, tiles)))

    upper[...] = jnp.where(lane >= row, upper[...], 0.0)
    inverse[...] = jnp.where(lane <= row, inverse[...], 0.0)


def factor_kernel(ids_ref, mine_ref, other_ref, parts_ref, r_ref, inv_ref, low_ref, work, unit, upper, inverse):
    tiled, flat = (HALF // 8, 8, HALF), (HALF, HALF)
    first = ids_ref[0] == 0
    for k in range(NX):
        rows = pl.ds(pl.multiple_of(64 * lax.rem(ids_ref[1] + NX - k, NX), 64), 64)
        mine, other = mine_ref[k], other_ref[k]
        r_ref[rows, :HALF] = jnp.where(first, mine, other)
        r_ref[rows, HALF:] = jnp.where(first, other, mine)
    right = r_ref[:, HALF:]
    work[...] = r_ref[:HALF, :HALF].reshape(tiled)
    eliminate(work, unit, upper, inverse)
    r_ref[:HALF, :HALF] = upper[...].reshape(flat)
    inverse_1 = inverse[...].reshape(flat)
    r_ref[HALF:, :HALF] = jnp.zeros(flat, F32)
    cross = dot(inverse_1, right[:HALF], precision=HIGHEST)
    r_ref[:HALF, HALF:] = cross
    work[...] = (right[HALF:] - dot(cross, cross, ((0,), (0,)), HIGHEST)).reshape(tiled)
    lower = dot(cross, inverse_1, ((0,), (0,)), HIGHEST)
    eliminate(work, unit, upper, inverse)
    r_ref[HALF:, HALF:] = upper[...].reshape(flat)
    inverse_2 = inverse[...].reshape(flat)
    below = -dot(inverse_2, lower, precision=HIGHEST)
    zero = jnp.zeros(flat, BF16)
    for start, one, two, three in zip((0, B), split(inverse_1, 2), split(below, 2), split(inverse_2, 2)):
        inv_ref[start:start + HALF, :HALF] = one
        inv_ref[start:start + HALF, HALF:] = zero
        inv_ref[start + HALF:start + B, :HALF] = two
        inv_ref[start + HALF:start + B, HALF:] = three
    basis = dot_split(inv_ref[...], parts_ref[:B], parts_ref[B:])
    low_ref[...] = basis.T.astype(BF16)


def update_kernel(ids_ref, a0_ref, a1_ref, a2_ref, a3_ref, inv_ref, low_ref, trailing_ref, top_ref, updated_ref,
                  sums, held, top, updated, arrived, sent):
    copies = fetches(trailing_ref, held, arrived)
    for k, a_ref in enumerate((a0_ref, a1_ref, a2_ref, a3_ref)):
        sums[pl.ds(pl.multiple_of(64 * lax.rem(ids_ref[1] + NX - k, NX), 64), 64)] = a_ref[...]
    results = []

    def send(source, target, semaphore):
        results.append(pltpu.make_async_copy(source, target, semaphore))
        results[-1].start()

    for tile in range(0, COLS // TILE, WIDE):
        columns = slice(tile * TILE, (tile + WIDE) * TILE)
        rows = dot_split(inv_ref[...], *split(sums[:, columns], 2))
        top[:, columns] = rows
        send(top.at[:, columns], top_ref.at[:, columns], sent.at[0, tile])
        change = dot(low_ref[...], rows.astype(BF16))
        for copy in copies[tile:tile + WIDE]:
            copy.wait()
        updated[:, columns] = (held[:, columns].astype(F32) - change).astype(BF16)
        send(updated.at[:, columns], updated_ref.at[:, columns], sent.at[1, tile])
    for result in results:
        result.wait()


HBM = pl.BlockSpec(memory_space=pltpu.HBM)
VMEM = pl.BlockSpec(memory_space=pltpu.VMEM)
SMEM = pl.BlockSpec(memory_space=pltpu.SMEM)


def cost(flops, size):
    return pl.CostEstimate(flops=int(flops), bytes_accessed=int(size), transcendentals=0)


def limit(mib):
    return pltpu.CompilerParams(vmem_limit_bytes=mib * 2**20)


def array(*shape, dtype=F32):
    return jax.ShapeDtypeStruct(shape, dtype)


def product(ids, mine, other, trailing):
    return pl.pallas_call(
        product_kernel,
        out_shape=(array(2 * B, ROWS, dtype=BF16),) + (array(B // NX, COLS + HALF),) * NX,
        in_specs=[SMEM, VMEM, VMEM, HBM],
        out_specs=(VMEM,) * (1 + NX),
        scratch_shapes=[
            pltpu.VMEM((ROWS, COLS), BF16),
            pltpu.VMEM((B, ROWS), BF16),
            pltpu.VMEM((2, B, 2 * TILE), F32),
            pltpu.VMEM((B, HALF), F32),
            pltpu.SemaphoreType.DMA((COLS // TILE,)),
        ],
        compiler_params=limit(50),
        cost_estimate=cost(3.6e9, 8e6),
    )(ids, mine, other, trailing)


def factor(ids, mine, other, parts):
    return pl.pallas_call(
        factor_kernel,
        out_shape=(array(B, B), array(2 * B, B, dtype=BF16), array(ROWS, B, dtype=BF16)),
        in_specs=[SMEM, VMEM, VMEM, VMEM],
        out_specs=(VMEM,) * 3,
        scratch_shapes=[pltpu.VMEM((HALF // 8, 8, HALF), F32)] * 4,
        compiler_params=limit(20),
        cost_estimate=cost(1.5e10, 3e6),
    )(ids, mine, other, parts)


def update(ids, a, inverse, low, trailing):
    tiles = COLS // TILE
    return pl.pallas_call(
        update_kernel,
        out_shape=(array(B, COLS), array(ROWS, COLS, dtype=BF16)),
        in_specs=[SMEM] + [VMEM] * 6 + [HBM],
        out_specs=(HBM, HBM),
        scratch_shapes=[
            pltpu.VMEM((B, COLS), F32),
            pltpu.VMEM((ROWS, COLS), BF16),
            pltpu.VMEM((B, COLS), F32),
            pltpu.VMEM((ROWS, COLS), BF16),
            pltpu.SemaphoreType.DMA((tiles,)),
            pltpu.SemaphoreType.DMA((2, tiles)),
        ],
        compiler_params=limit(50),
        cost_estimate=cost(3e9, 12e6),
    )(ids, *a, inverse, low, trailing)


def swap_z(block):
    return lax.all_to_all(block, "row", 0, 0, axis_index_groups=Z_GROUPS)


def shift(pieces, axis, routes):
    return [pieces[0]] + [lax.ppermute(pieces[k], axis, routes[k]) for k in range(1, 4)]


def local(panel, trailing):
    row, col = lax.axis_index("row"), lax.axis_index("col")
    ids = jnp.stack([col % 2, row // NZ, col // 2]).astype(jnp.int32)
    with jax.named_scope("gather_panel"):
        mine = jnp.stack(shift([panel.T] * 4, "col", Y_ROUTES))
        other = lax.ppermute(mine, "col", SIBLING)
    with jax.named_scope("product"):
        parts, *pieces = product(ids, mine, other, trailing)
    with jax.named_scope("sum_x"):
        sums = sum(shift(pieces, "row", X_ROUTES))
    with jax.named_scope("sum_z"):
        sums = jnp.sum(swap_z(sums.reshape(NZ, 8, COLS + HALF)), axis=0)
    with jax.named_scope("gather_z"):
        sums = swap_z(jnp.broadcast_to(sums[None], (NZ, 8, COLS + HALF))).reshape(64, COLS + HALF)
    with jax.named_scope("gather_gram"):
        gram_mine = jnp.stack(shift([sums[:, COLS:]] * NX, "row", X_ROUTES))
        gram_other = lax.ppermute(gram_mine, "col", SIBLING)
    with jax.named_scope("gather_x"):
        blocks = shift([sums[:, :COLS]] * NX, "row", X_ROUTES)
    with jax.named_scope("factor"):
        r_factor, inverse, low = factor(ids, gram_mine, gram_other, parts)
    with jax.named_scope("update"):
        top, updated = update(ids, blocks, inverse, low, trailing)
    return r_factor, top, updated


def solution(mesh):
    return jax.shard_map(
        local,
        mesh=mesh,
        in_specs=(P("row", "col"), P("row", "col")),
        out_specs=(P(), P(None, "col"), P("row", "col")),
        check_vma=False,
    )
```

time: 155 us -> 139 us (0.90); the launches traced: 153 us -> 139 us
  blocking collectives: 13.4 us -> 42 us
  starting transfers between devices: 53.7 us -> 25.5 us
  local copies, waits for them, and re-layouts: 7.61 us -> 0.08 us
  Pallas kernels: 30.1 us -> 26.9 us
  waiting for transfers between devices: 44.3 us -> 42.5 us
    all_to_all x1 -> x2, blocking collectives: 13.4 us -> 42 us  [swap_z(): return lax.all_to_all(block, 'row', 0, 0, axis_index_groups=Z_GROUPS)]
    all_to_all x4 -> x0, starting transfers between devices: 22.2 us -> none  [swap(): return lax.all_to_all(block, axis, 0, 0, axis_index_groups=groups)]
    all_to_all x4 -> x0, waiting for transfers between devices: 9.23 us -> none  [swap(): return lax.all_to_all(block, axis, 0, 0, axis_index_groups=groups)]
    ppermute x18 -> x12, waiting for transfers between devices: 33.6 us -> 41.1 us  [shift(): lax.ppermute(pieces[k], axis, routes[k])]
    ppermute x18 -> x12, starting transfers between devices: 23.7 us -> 18.3 us  [shift(): lax.ppermute(pieces[k], axis, routes[k])]
    unnamed x12 -> x2, local copies, waits for them, and re-layouts: 4.21 us -> 0.01 us
    pallas_call x2 -> x1, Pallas kernels: 9.49 us -> 6.08 us  [product(): pl.pallas_call(product_kernel, out_shape=(array(2 * B, ROWS, dtype=BF16),...]
    broadcast_in_dim x3 -> x1, local copies, waits for them, and re-layouts: 2.64 us -> 0.04 us  [local(): jnp.broadcast_to(sums[None], (NZ, 8, COLS + HALF))]
  transfers between devices with their start and end apart: 24 -> 14, of which waited for: 15 -> 9; matrix products, arithmetic and copies ran while one was open for 1% -> 0% of each run, Pallas kernels for 9% -> 10%
where the time goes in v4:
time: 139 us
  waiting for transfers between devices  42.5 us (31%)
  blocking collectives  42 us (30%)
  Pallas kernels  26.9 us (19%)
  starting transfers between devices  25.5 us (18%)
    all_to_all x2, blocking collectives, swap_z(): return lax.all_to_all(block, 'row', 0, 0, axis_index_groups=Z_GROUPS)  42 us
    ppermute x12, waiting for transfers between devices, shift(): lax.ppermute(pieces[k], axis, routes[k])  41.1 us
    ppermute x12, starting transfers between devices, shift(): lax.ppermute(pieces[k], axis, routes[k])  18.3 us
    pallas_call x1, Pallas kernels, factor(): pl.pallas_call(factor_kernel, out_shape=(array(B, B), array(2 * B, B, dty...  13.9 us
    pallas_call x1, Pallas kernels, update(): pl.pallas_call(update_kernel, out_shape=(array(B, COLS), array(ROWS, COLS...  6.91 us
    pallas_call x1, Pallas kernels, product(): pl.pallas_call(product_kernel, out_shape=(array(2 * B, ROWS, dtype=BF16),...  6.08 us
    ppermute x1, starting transfers between devices, local(): gram_other = lax.ppermute(gram_mine, 'col', SIBLING)  5.99 us
  transfers between devices with their start and end apart: 14, of which 9 were waited for; matrix products, arithmetic and copies ran while one was open for 0% of the time, Pallas kernels for 10%

profile of v4, /device:TPU:1, one launch (start us, length us, event | category | flops | bytes accessed | tf_op | source)
XLA Modules:
  0.0 139.1 jit_solution(11985153379634879835)
XLA Ops:
  0.6 3.8 %collective-permute-start.1 = (f32[32,1024]{1,0:T(8,128)}, f32[32,1024]{1,0:T(8,128)S(1)}, u32[]{:S(2)}, u32[]{:S(2)}) collective-permute-start(f32[32,1024]{1,0:T(8,128)} %bitcast.19), channel_id=1, source_target_pairs={{0,4},{1,5},{2,6},{3,7},{4,0},{5,1},{6,2},{7,3},{8,12},{9,13},{10,... | collective-permute-start | bytes 393224 | tf_op jit(solution)/shard_map/gather_panel/ppermute | solution.py:280
  4.5 0.4 collective-permute-start
  4.9 2.3 %collective-permute-start.2 = (f32[32,1024]{1,0:T(8,128)}, f32[32,1024]{1,0:T(8,128)S(1)}, u32[]{:S(2)}, u32[]{:S(2)}) collective-permute-start(f32[32,1024]{1,0:T(8,128)} %bitcast.21), channel_id=1, source_target_pairs={{0,6},{1,7},{2,0},{3,1},{4,2},{5,3},{6,4},{7,5},{8,14},{9,15},{10,... | collective-permute-start | bytes 393224 | tf_op jit(solution)/shard_map/gather_panel/ppermute | solution.py:280
  7.1 4.9 %collective-permute-done = f32[32,1024]{1,0:T(8,128)S(1)} collective-permute-done((f32[32,1024]{1,0:T(8,128)}, f32[32,1024]{1,0:T(8,128)S(1)}, u32[]{:S(2)}, u32[]{:S(2)}) %collective-permute-start) | collective-permute-done | bytes 131104 | tf_op jit(solution)/shard_map/gather_panel/ppermute | solution.py:280
  12.0 0.9 pad_maximum_fusion.mine_ref
  13.0 1.2 collective-permute-start.3
  14.2 0.1 pad_add_fusion.ids_ref
  14.3 1.5 %collective-permute-done.3.other_ref = f32[4,32,1024]{2,1,0:T(8,128)S(1)} collective-permute-done((f32[4,32,1024]{2,1,0:T(8,128)S(1)}, f32[4,32,1024]{2,1,0:T(8,128)S(1)}, u32[]{:S(2)}, u32[]{:S(2)}) %collective-permute-start.3) | collective-permute-done | bytes 524320 | tf_op jit(solution)/shard_map/gather_panel/ppermute | solution.py:288
  15.8 6.1 %product.1 = (bf16[512,1024]{1,0:T(8,128)(2,1)}, f32[64,2176]{1,0:T(8,128)S(1)}, f32[64,2176]{1,0:T(8,128)S(1)}, f32[64,2176]{1,0:T(8,128)S(1)}, f32[64,2176]{1,0:T(8,128)S(1)}) custom-call(s32[3]{0:T(128)S(1)} %pad_add_fusion.ids_ref, f32[4,32,1024]{2,1,0:T(8,128)S(1)} %pad_maximum_fusion.mine_ref, f32[4,32,1024]{2,1,0:T(8,128)S(1)} %collective-permute-done.3.other_ref, ...), custom_call_target="tpu_custom_call" | custom-call | flops 3600000000 | bytes 8000000 | tf_op jit(solution)/shard_map/product/pallas_call | solution.py:226
  21.9 0.0 copy-start
  21.9 0.4 collective-permute-start.4
  22.3 2.5 %collective-permute-start.5 = (f32[64,2176]{1,0:T(8,128)S(1)}, f32[64,2176]{1,0:T(8,128)S(1)}, u32[]{:S(2)}, u32[]{:S(2)}) collective-permute-start(f32[64,2176]{1,0:T(8,128)S(1)} %get-tuple-element.15), channel_id=1, source_target_pairs={{0,128},{8,136},{16,144},{24,152},{32,160},{40,168},{48,176},{56,1... | collective-permute-start | bytes 1671176 | tf_op jit(solution)/shard_map/sum_x/ppermute | solution.py:280
  24.8 1.2 collective-permute-start.6
  25.9 11.1 %collective-permute-done.4 = f32[64,2176]{1,0:T(8,128)S(1)} collective-permute-done((f32[64,2176]{1,0:T(8,128)S(1)}, f32[64,2176]{1,0:T(8,128)S(1)}, u32[]{:S(2)}, u32[]{:S(2)}) %collective-permute-start.4) | collective-permute-done | bytes 557088 | tf_op jit(solution)/shard_map/sum_x/ppermute | solution.py:280
  37.0 12.1 %collective-permute-done.5 = f32[64,2176]{1,0:T(8,128)S(1)} collective-permute-done((f32[64,2176]{1,0:T(8,128)S(1)}, f32[64,2176]{1,0:T(8,128)S(1)}, u32[]{:S(2)}, u32[]{:S(2)}) %collective-permute-start.5) | collective-permute-done | bytes 557088 | tf_op jit(solution)/shard_map/sum_x/ppermute | solution.py:280
  49.1 0.2 collective-permute-done.6
  49.2 0.1 add_bitcast_fusion
  49.3 23.9 %all_to_all.10 = f32[8,8,2176]{2,1,0:T(8,128)S(1)} all-to-all(f32[8,8,2176]{2,1,0:T(8,128)S(1)} %add_bitcast_fusion), channel_id=1, replica_groups={{0,8,16,24,32,40,48,56},{64,72,80,88,96,104,112,120},{128,136,144,152,1..., dimensions={0} | all-to-all | bytes 1114112 | tf_op jit(solution)/shard_map/sum_z/all_to_all | solution.py:276
  73.3 18.1 %all_to_all.11 = f32[8,8,2176]{2,1,0:T(8,128)S(1)} all-to-all(f32[8,8,2176]{2,1,0:T(8,128)S(1)} %broadcast_in_dim.2), channel_id=1, replica_groups={{0,8,16,24,32,40,48,56},{64,72,80,88,96,104,112,120},{128,136,144,152,1..., dimensions={0} | all-to-all | bytes 1114112 | tf_op jit(solution)/shard_map/gather_z/all_to_all | solution.py:276
  91.4 2.1 %collective-permute-start.8 = (f32[64,128]{1,0:T(8,128)S(1)}, f32[64,128]{1,0:T(8,128)S(1)}, u32[]{:S(2)}, u32[]{:S(2)}) collective-permute-start(f32[64,128]{1,0:T(8,128)S(1)} %get-tuple-element.24), channel_id=1, source_target_pairs={{0,128},{8,136},{16,144},{24,152},{32,160},{40,168},{48,176},{56,1... | collective-permute-start | bytes 98312 | tf_op jit(solution)/shard_map/gather_gram/ppermute | solution.py:280
  93.5 1.5 %collective-permute-start.7 = (f32[64,128]{1,0:T(8,128)S(1)}, f32[64,128]{1,0:T(8,128)S(1)}, u32[]{:S(2)}, u32[]{:S(2)}) collective-permute-start(f32[64,128]{1,0:T(8,128)S(1)} %get-tuple-element.24), channel_id=1, source_target_pairs={{0,64},{8,72},{16,80},{24,88},{32,96},{40,104},{48,112},{56,120},{... | collective-permute-start | bytes 98312 | tf_op jit(solution)/shard_map/gather_gram/ppermute | solution.py:280
  95.0 1.2 collective-permute-start.9
  96.2 1.3 collective-permute-done.7
  97.5 0.3 collective-permute-done.9
  97.8 6.0 %collective-permute-start.10 = (f32[4,64,128]{2,1,0:T(8,128)S(1)}, f32[4,64,128]{2,1,0:T(8,128)S(1)}, u32[]{:S(2)}, u32[]{:S(2)}) collective-permute-start(f32[4,64,128]{2,1,0:T(8,128)S(1)} %pad_maximum_fusion.1.mine_ref), channel_id=1, source_target_pairs={{0,1},{1,0},{2,3},{3,2},{4,5},{5,4},{6,7},{7,6},{8,9},{9,8},{10,11... | collective-permute-start | bytes 393224 | tf_op jit(solution)/shard_map/gather_gram/ppermute | solution.py:299
  103.8 2.1 %collective-permute-start.13 = (f32[64,2048]{1,0:T(8,128)S(1)}, f32[64,2048]{1,0:T(8,128)S(1)}, u32[]{:S(2)}, u32[]{:S(2)}) collective-permute-start(f32[64,2048]{1,0:T(8,128)S(1)} %slice.9.a0_ref), channel_id=1, source_target_pairs={{0,192},{8,200},{16,208},{24,216},{32,224},{40,232},{48,240},{56,2... | collective-permute-start | bytes 1572872 | tf_op jit(solution)/shard_map/gather_x/ppermute | solution.py:280
  106.0 0.0 collective-permute-start.12
  106.0 0.9 collective-permute-start.11
  106.8 13.9 %factor.1 = (f32[256,256]{1,0:T(8,128)}, bf16[512,256]{1,0:T(8,128)(2,1)S(1)}, bf16[1024,256]{1,0:T(8,128)(2,1)S(1)}) custom-call(s32[3]{0:T(128)S(1)} %pad_add_fusion.ids_ref, f32[4,64,128]{2,1,0:T(8,128)S(1)} %pad_maximum_fusion.1.mine_ref, f32[4,64,128]{2,1,0:T(8,128)S(1)} %collective-permute-done.10.other_ref, bf16[512,1024]{1,0:T(8,128)(2,1)S(1)} %copy-done), custom_call_target="tpu_custom_call" | custom-call | flops 15000000512 | bytes 3000000 | tf_op jit(solution)/shard_map/factor/pallas_call | solution.py:244
  120.7 7.7 %collective-permute-done.13.a3_ref = f32[64,2048]{1,0:T(8,128)S(1)} collective-permute-done((f32[64,2048]{1,0:T(8,128)S(1)}, f32[64,2048]{1,0:T(8,128)S(1)}, u32[]{:S(2)}, u32[]{:S(2)}) %collective-permute-start.13) | collective-permute-done | bytes 524320 | tf_op jit(solution)/shard_map/gather_x/ppermute | solution.py:280
  128.4 3.6 %collective-permute-done.11.a1_ref = f32[64,2048]{1,0:T(8,128)S(1)} collective-permute-done((f32[64,2048]{1,0:T(8,128)S(1)}, f32[64,2048]{1,0:T(8,128)S(1)}, u32[]{:S(2)}, u32[]{:S(2)}) %collective-permute-start.11) | collective-permute-done | bytes 524320 | tf_op jit(solution)/shard_map/gather_x/ppermute | solution.py:280
  132.0 6.9 %update.1 = (f32[256,2048]{1,0:T(8,128)}, bf16[1024,2048]{1,0:T(8,128)(2,1)}) custom-call(s32[3]{0:T(128)S(1)} %pad_add_fusion.ids_ref, f32[64,2048]{1,0:T(8,128)S(1)} %slice.9.a0_ref, f32[64,2048]{1,0:T(8,128)S(1)} %collective-permute-done.11.a1_ref, f32[64,2048]{1,0:T(8,128)S(1)} %collective-permute-done.12.a2_ref, ...), custom_call_target="tpu_custom_call" | custom-call | flops 3000000000 | bytes 12000000 | tf_op jit(solution)/shard_map/update/pallas_call | solution.py:257
  (11 shorter events, 0.1 us)
Async XLA Ops:
  0.6 6.5 %collective-permute-start.1 = (f32[32,1024]{1,0:T(8,128)}, f32[32,1024]{1,0:T(8,128)S(1)}, u32[]{:S(2)}, u32[]{:S(2)}) collective-permute-start(f32[32,1024]{1,0:T(8,128)} %bitcast.19), channel_id=1, source_target_pairs={{0,4},{1,5},{2,6},{3,7},{4,0},{5,1},{6,2},{7,3},{8,12},{9,13},{10,... | collective-permute-start | bytes 393224 | tf_op jit(solution)/shard_map/gather_panel/ppermute | solution.py:280
  4.5 7.6 %collective-permute-start = (f32[32,1024]{1,0:T(8,128)}, f32[32,1024]{1,0:T(8,128)S(1)}, u32[]{:S(2)}, u32[]{:S(2)}) collective-permute-start(f32[32,1024]{1,0:T(8,128)} %bitcast.20), channel_id=1, source_target_pairs={{0,2},{1,3},{2,4},{3,5},{4,6},{5,7},{6,0},{7,1},{8,10},{9,11},{10,... | collective-permute-start | bytes 393224 | tf_op jit(solution)/shard_map/gather_panel/ppermute | solution.py:280
  4.9 7.2 %collective-permute-start.2 = (f32[32,1024]{1,0:T(8,128)}, f32[32,1024]{1,0:T(8,128)S(1)}, u32[]{:S(2)}, u32[]{:S(2)}) collective-permute-start(f32[32,1024]{1,0:T(8,128)} %bitcast.21), channel_id=1, source_target_pairs={{0,6},{1,7},{2,0},{3,1},{4,2},{5,3},{6,4},{7,5},{8,14},{9,15},{10,... | collective-permute-start | bytes 393224 | tf_op jit(solution)/shard_map/gather_panel/ppermute | solution.py:280
  13.0 2.8 %collective-permute-start.3 = (f32[4,32,1024]{2,1,0:T(8,128)S(1)}, f32[4,32,1024]{2,1,0:T(8,128)S(1)}, u32[]{:S(2)}, u32[]{:S(2)}) collective-permute-start(f32[4,32,1024]{2,1,0:T(8,128)S(1)} %pad_maximum_fusion.mine_ref), channel_id=1, source_target_pairs={{0,1},{1,0},{2,3},{3,2},{4,5},{5,4},{6,7},{7,6},{8,9},{9,8},{10,11... | collective-permute-start | bytes 1572872 | tf_op jit(solution)/shard_map/gather_panel/ppermute | solution.py:288
  21.9 85.0 %copy-start = (bf16[512,1024]{1,0:T(8,128)(2,1)S(1)}, bf16[512,1024]{1,0:T(8,128)(2,1)}, u32[]{:S(2)}) copy-start(bf16[512,1024]{1,0:T(8,128)(2,1)} %get-tuple-element.17.parts_ref) | copy-start | bytes 3145732
  21.9 15.1 %collective-permute-start.4 = (f32[64,2176]{1,0:T(8,128)S(1)}, f32[64,2176]{1,0:T(8,128)S(1)}, u32[]{:S(2)}, u32[]{:S(2)}) collective-permute-start(f32[64,2176]{1,0:T(8,128)S(1)} %get-tuple-element.14), channel_id=1, source_target_pairs={{0,64},{8,72},{16,80},{24,88},{32,96},{40,104},{48,112},{56,120},{... | collective-permute-start | bytes 1671176 | tf_op jit(solution)/shard_map/sum_x/ppermute | solution.py:280
  22.3 26.8 %collective-permute-start.5 = (f32[64,2176]{1,0:T(8,128)S(1)}, f32[64,2176]{1,0:T(8,128)S(1)}, u32[]{:S(2)}, u32[]{:S(2)}) collective-permute-start(f32[64,2176]{1,0:T(8,128)S(1)} %get-tuple-element.15), channel_id=1, source_target_pairs={{0,128},{8,136},{16,144},{24,152},{32,160},{40,168},{48,176},{56,1... | collective-permute-start | bytes 1671176 | tf_op jit(solution)/shard_map/sum_x/ppermute | solution.py:280
  24.8 24.5 %collective-permute-start.6 = (f32[64,2176]{1,0:T(8,128)S(1)}, f32[64,2176]{1,0:T(8,128)S(1)}, u32[]{:S(2)}, u32[]{:S(2)}) collective-permute-start(f32[64,2176]{1,0:T(8,128)S(1)} %get-tuple-element.16), channel_id=1, source_target_pairs={{0,192},{8,200},{16,208},{24,216},{32,224},{40,232},{48,240},{56,2... | collective-permute-start | bytes 1671176 | tf_op jit(solution)/shard_map/sum_x/ppermute | solution.py:280
  91.4 4.8 %collective-permute-start.8 = (f32[64,128]{1,0:T(8,128)S(1)}, f32[64,128]{1,0:T(8,128)S(1)}, u32[]{:S(2)}, u32[]{:S(2)}) collective-permute-start(f32[64,128]{1,0:T(8,128)S(1)} %get-tuple-element.24), channel_id=1, source_target_pairs={{0,128},{8,136},{16,144},{24,152},{32,160},{40,168},{48,176},{56,1... | collective-permute-start | bytes 98312 | tf_op jit(solution)/shard_map/gather_gram/ppermute | solution.py:280
  93.5 4.0 %collective-permute-start.7 = (f32[64,128]{1,0:T(8,128)S(1)}, f32[64,128]{1,0:T(8,128)S(1)}, u32[]{:S(2)}, u32[]{:S(2)}) collective-permute-start(f32[64,128]{1,0:T(8,128)S(1)} %get-tuple-element.24), channel_id=1, source_target_pairs={{0,64},{8,72},{16,80},{24,88},{32,96},{40,104},{48,112},{56,120},{... | collective-permute-start | bytes 98312 | tf_op jit(solution)/shard_map/gather_gram/ppermute | solution.py:280
  95.0 2.8 %collective-permute-start.9 = (f32[64,128]{1,0:T(8,128)S(1)}, f32[64,128]{1,0:T(8,128)S(1)}, u32[]{:S(2)}, u32[]{:S(2)}) collective-permute-start(f32[64,128]{1,0:T(8,128)S(1)} %get-tuple-element.24), channel_id=1, source_target_pairs={{0,192},{8,200},{16,208},{24,216},{32,224},{40,232},{48,240},{56,2... | collective-permute-start | bytes 98312 | tf_op jit(solution)/shard_map/gather_gram/ppermute | solution.py:280
  97.8 9.0 %collective-permute-start.10 = (f32[4,64,128]{2,1,0:T(8,128)S(1)}, f32[4,64,128]{2,1,0:T(8,128)S(1)}, u32[]{:S(2)}, u32[]{:S(2)}) collective-permute-start(f32[4,64,128]{2,1,0:T(8,128)S(1)} %pad_maximum_fusion.1.mine_ref), channel_id=1, source_target_pairs={{0,1},{1,0},{2,3},{3,2},{4,5},{5,4},{6,7},{7,6},{8,9},{9,8},{10,11... | collective-permute-start | bytes 393224 | tf_op jit(solution)/shard_map/gather_gram/ppermute | solution.py:299
  103.8 24.6 %collective-permute-start.13 = (f32[64,2048]{1,0:T(8,128)S(1)}, f32[64,2048]{1,0:T(8,128)S(1)}, u32[]{:S(2)}, u32[]{:S(2)}) collective-permute-start(f32[64,2048]{1,0:T(8,128)S(1)} %slice.9.a0_ref), channel_id=1, source_target_pairs={{0,192},{8,200},{16,208},{24,216},{32,224},{40,232},{48,240},{56,2... | collective-permute-start | bytes 1572872 | tf_op jit(solution)/shard_map/gather_x/ppermute | solution.py:280
  106.0 22.4 %collective-permute-start.12 = (f32[64,2048]{1,0:T(8,128)S(1)}, f32[64,2048]{1,0:T(8,128)S(1)}, u32[]{:S(2)}, u32[]{:S(2)}) collective-permute-start(f32[64,2048]{1,0:T(8,128)S(1)} %slice.9.a0_ref), channel_id=1, source_target_pairs={{0,128},{8,136},{16,144},{24,152},{32,160},{40,168},{48,176},{56,1... | collective-permute-start | bytes 1572872 | tf_op jit(solution)/shard_map/gather_x/ppermute | solution.py:280
  106.0 26.0 %collective-permute-start.11 = (f32[64,2048]{1,0:T(8,128)S(1)}, f32[64,2048]{1,0:T(8,128)S(1)}, u32[]{:S(2)}, u32[]{:S(2)}) collective-permute-start(f32[64,2048]{1,0:T(8,128)S(1)} %slice.9.a0_ref), channel_id=1, source_target_pairs={{0,64},{8,72},{16,80},{24,88},{32,96},{40,104},{48,112},{56,120},{... | collective-permute-start | bytes 1572872 | tf_op jit(solution)/shard_map/gather_x/ppermute | solution.py:280

commit v5 on v4

--- a/solution.py
+++ b/solution.py
@@ -52,14 +52,15 @@
     return copies
 
 
-def product_kernel(ids_ref, mine_ref, other_ref, trailing_ref, parts_ref, *refs):
-    pieces, (held, third, whole, gram, arrived) = refs[:NX], refs[NX:]
+def product_kernel(ids_ref, *refs):
+    mine, other, trailing_ref, parts_ref, pieces = refs[:4], refs[4:8], refs[8], refs[9], refs[10:10 + NX]
+    held, third, whole, gram, arrived = refs[10 + NX:]
     copies = fetches(trailing_ref, held, arrived)
     core, x, y = ids_ref[0], ids_ref[1], ids_ref[2]
     for k in range(4):
-        for ref, offset in ((mine_ref, 32 * core), (other_ref, 32 - 32 * core)):
+        for ref, offset in ((mine[k], 32 * core), (other[k], 32 - 32 * core)):
             start = 64 * lax.rem(y + 4 - k, 4) + offset
-            high, middle, low = split(ref[k], 3)
+            high, middle, low = split(ref[...], 3)
             parts_ref[pl.ds(pl.multiple_of(start, 32), 32)] = high
             parts_ref[pl.ds(pl.multiple_of(B + start, 32), 32)] = middle
             third[pl.ds(pl.multiple_of(start, 32), 32)] = low
@@ -148,7 +149,10 @@
     inverse[...] = jnp.where(lane <= row, inverse[...], 0.0)
 
 
-def factor_kernel(ids_ref, mine_ref, other_ref, parts_ref, r_ref, inv_ref, low_ref, work, unit, upper, inverse):
+def factor_kernel(ids_ref, mine_ref, other_ref, parts_ref, trailing_ref, r_ref, inv_ref, low_ref, copy_ref,
+                  work, unit, upper, inverse, arrived):
+    fetch = pltpu.make_async_copy(trailing_ref, copy_ref, arrived)
+    fetch.start()
     tiled, flat = (HALF // 8, 8, HALF), (HALF, HALF)
     first = ids_ref[0] == 0
     for k in range(NX):
@@ -178,11 +182,11 @@
         inv_ref[start + HALF:start + B, HALF:] = three
     basis = dot_split(inv_ref[...], parts_ref[:B], parts_ref[B:])
     low_ref[...] = basis.T.astype(BF16)
+    fetch.wait()
 
 
 def update_kernel(ids_ref, a0_ref, a1_ref, a2_ref, a3_ref, inv_ref, low_ref, trailing_ref, top_ref, updated_ref,
-                  sums, held, top, updated, arrived, sent):
-    copies = fetches(trailing_ref, held, arrived)
+                  sums, top, updated, sent):
     for k, a_ref in enumerate((a0_ref, a1_ref, a2_ref, a3_ref)):
         sums[pl.ds(pl.multiple_of(64 * lax.rem(ids_ref[1] + NX - k, NX), 64), 64)] = a_ref[...]
     results = []
@@ -197,9 +201,7 @@
         top[:, columns] = rows
         send(top.at[:, columns], top_ref.at[:, columns], sent.at[0, tile])
         change = dot(low_ref[...], rows.astype(BF16))
-        for copy in copies[tile:tile + WIDE]:
-            copy.wait()
-        updated[:, columns] = (held[:, columns].astype(F32) - change).astype(BF16)
+        updated[:, columns] = (trailing_ref[:, columns].astype(F32) - change).astype(BF16)
         send(updated.at[:, columns], updated_ref.at[:, columns], sent.at[1, tile])
     for result in results:
         result.wait()
@@ -226,7 +228,7 @@
     return pl.pallas_call(
         product_kernel,
         out_shape=(array(2 * B, ROWS, dtype=BF16),) + (array(B // NX, COLS + HALF),) * NX,
-        in_specs=[SMEM, VMEM, VMEM, HBM],
+        in_specs=[SMEM] + [VMEM] * 8 + [HBM],
         out_specs=(VMEM,) * (1 + NX),
         scratch_shapes=[
             pltpu.VMEM((ROWS, COLS), BF16),
@@ -237,19 +239,24 @@
         ],
         compiler_params=limit(50),
         cost_estimate=cost(3.6e9, 8e6),
-    )(ids, mine, other, trailing)
-
-
-def factor(ids, mine, other, parts):
+    )(ids, *mine, *other, trailing)
+
+
+def factor(ids, mine, other, parts, trailing):
     return pl.pallas_call(
         factor_kernel,
-        out_shape=(array(B, B), array(2 * B, B, dtype=BF16), array(ROWS, B, dtype=BF16)),
-        in_specs=[SMEM, VMEM, VMEM, VMEM],
-        out_specs=(VMEM,) * 3,
-        scratch_shapes=[pltpu.VMEM((HALF // 8, 8, HALF), F32)] * 4,
-        compiler_params=limit(20),
-        cost_estimate=cost(1.5e10, 3e6),
-    )(ids, mine, other, parts)
+        out_shape=(
+            array(B, B),
+            array(2 * B, B, dtype=BF16),
+            array(ROWS, B, dtype=BF16),
+            array(ROWS, COLS, dtype=BF16),
+        ),
+        in_specs=[SMEM, VMEM, VMEM, VMEM, HBM],
+        out_specs=(VMEM,) * 4,
+        scratch_shapes=[pltpu.VMEM((HALF // 8, 8, HALF), F32)] * 4 + [pltpu.SemaphoreType.DMA],
+        compiler_params=limit(45),
+        cost_estimate=cost(1e6, 1e3),
+    )(ids, mine, other, parts, trailing)
 
 
 def update(ids, a, inverse, low, trailing):
@@ -257,17 +264,15 @@
     return pl.pallas_call(
         update_kernel,
         out_shape=(array(B, COLS), array(ROWS, COLS, dtype=BF16)),
-        in_specs=[SMEM] + [VMEM] * 6 + [HBM],
+        in_specs=[SMEM] + [VMEM] * 7,
         out_specs=(HBM, HBM),
         scratch_shapes=[
             pltpu.VMEM((B, COLS), F32),
-            pltpu.VMEM((ROWS, COLS), BF16),
             pltpu.VMEM((B, COLS), F32),
             pltpu.VMEM((ROWS, COLS), BF16),
-            pltpu.SemaphoreType.DMA((tiles,)),
             pltpu.SemaphoreType.DMA((2, tiles)),
         ],
-        compiler_params=limit(50),
+        compiler_params=limit(36),
         cost_estimate=cost(3e9, 12e6),
     )(ids, *a, inverse, low, trailing)
 
@@ -284,8 +289,8 @@
     row, col = lax.axis_index("row"), lax.axis_index("col")
     ids = jnp.stack([col % 2, row // NZ, col // 2]).astype(jnp.int32)
     with jax.named_scope("gather_panel"):
-        mine = jnp.stack(shift([panel.T] * 4, "col", Y_ROUTES))
-        other = lax.ppermute(mine, "col", SIBLING)
+        mine = shift([panel.T] * 4, "col", Y_ROUTES)
+        other = [lax.ppermute(piece, "col", SIBLING) for piece in mine]
     with jax.named_scope("product"):
         parts, *pieces = product(ids, mine, other, trailing)
     with jax.named_scope("sum_x"):
@@ -300,7 +305,7 @@
     with jax.named_scope("gather_x"):
         blocks = shift([sums[:, :COLS]] * NX, "row", X_ROUTES)
     with jax.named_scope("factor"):
-        r_factor, inverse, low = factor(ids, gram_mine, gram_other, parts)
+        r_factor, inverse, low, trailing = factor(ids, gram_mine, gram_other, parts, trailing)
     with jax.named_scope("update"):
         top, updated = update(ids, blocks, inverse, low, trailing)
     return r_factor, top, updated

time: 139 us -> 148 us (1.065)
  waiting for transfers between devices: 42.5 us -> 51 us
  starting transfers between devices: 25.5 us -> 28.3 us
  Pallas kernels: 26.9 us -> 24.7 us
    ppermute x12, waiting for transfers between devices: 41.1 us -> 49.1 us  [shift(): lax.ppermute(pieces[k], axis, routes[k])]
    ppermute x1 -> x4, starting transfers between devices: 1.25 us -> 7.23 us  [local(): other = [lax.ppermute(piece, 'col', SIBLING) for piece in mine]]
    ppermute x12, starting transfers between devices: 18.3 us -> 15.9 us  [shift(): lax.ppermute(pieces[k], axis, routes[k])]
    pallas_call x1, Pallas kernels: 6.91 us -> 4.6 us  [update(): pl.pallas_call(update_kernel, out_shape=(array(B, COLS), array(ROWS, COLS...]
  transfers between devices with their start and end apart: 14 -> 17, of which waited for: 9 -> 8; matrix products, arithmetic and copies ran while one was open for 0% -> 0% of each run, Pallas kernels for 10% -> 9%
where the time goes in v5:
time: 148 us
  waiting for transfers between devices  51 us (34%)
  blocking collectives  42.2 us (29%)
  starting transfers between devices  28.3 us (19%)
  Pallas kernels  24.7 us (17%)
    ppermute x12, waiting for transfers between devices, shift(): lax.ppermute(pieces[k], axis, routes[k])  49.1 us
    all_to_all x2, blocking collectives, swap_z(): return lax.all_to_all(block, 'row', 0, 0, axis_index_groups=Z_GROUPS)  42.2 us
    ppermute x12, starting transfers between devices, shift(): lax.ppermute(pieces[k], axis, routes[k])  15.9 us
    pallas_call x1, Pallas kernels, factor(): pl.pallas_call(factor_kernel, out_shape=(array(B, B), array(2 * B, B, dty...  14 us
    ppermute x4, starting transfers between devices, local(): other = [lax.ppermute(piece, 'col', SIBLING) for piece in mine]  7.23 us
    pallas_call x1, Pallas kernels, product(): pl.pallas_call(product_kernel, out_shape=(array(2 * B, ROWS, dtype=BF16),...  6.08 us
    ppermute x1, starting transfers between devices, local(): gram_other = lax.ppermute(gram_mine, 'col', SIBLING)  5.2 us
    pallas_call x1, Pallas kernels, update(): pl.pallas_call(update_kernel, out_shape=(array(B, COLS), array(ROWS, COLS...  4.6 us
  transfers between devices with their start and end apart: 17, of which 8 were waited for; matrix products, arithmetic and copies ran while one was open for 0% of the time, Pallas kernels for 9%

profile of v5, /device:TPU:1, one launch (start us, length us, event | category | flops | bytes accessed | tf_op | source)
XLA Modules:
  0.0 148.2 jit_solution(10395017700981948704)
XLA Ops:
  0.6 3.6 %collective-permute-start.2 = (f32[32,1024]{1,0:T(8,128)}, f32[32,1024]{1,0:T(8,128)S(1)}, u32[]{:S(2)}, u32[]{:S(2)}) collective-permute-start(f32[32,1024]{1,0:T(8,128)} %bitcast.12), channel_id=1, source_target_pairs={{0,6},{1,7},{2,0},{3,1},{4,2},{5,3},{6,4},{7,5},{8,14},{9,15},{10,... | collective-permute-start | bytes 393224 | tf_op jit(solution)/shard_map/gather_panel/ppermute | solution.py:285
  4.3 0.3 collective-permute-start.1
  4.6 0.7 collective-permute-start
  5.3 1.5 %collective-permute-start.3 = (f32[32,1024]{1,0:T(8,128)}, f32[32,1024]{1,0:T(8,128)S(1)}, u32[]{:S(2)}, u32[]{:S(2)}) collective-permute-start(f32[32,1024]{1,0:T(8,128)} %bitcast.15), channel_id=1, source_target_pairs={{0,1},{1,0},{2,3},{3,2},{4,5},{5,4},{6,7},{7,6},{8,9},{9,8},{10,11... | collective-permute-start | bytes 393224 | tf_op jit(solution)/shard_map/gather_panel/ppermute | solution.py:293
  6.8 1.4 collective-permute-done.2.refs_3_
  8.2 2.9 %collective-permute-start.6 = (f32[32,1024]{1,0:T(8,128)S(1)}, f32[32,1024]{1,0:T(8,128)S(1)}, u32[]{:S(2)}, u32[]{:S(2)}) collective-permute-start(f32[32,1024]{1,0:T(8,128)S(1)} %collective-permute-done.2.refs_3_), channel_id=1, source_target_pairs={{0,1},{1,0},{2,3},{3,2},{4,5},{5,4},{6,7},{7,6},{8,9},{9,8},{10,11... | collective-permute-start | bytes 393224 | tf_op jit(solution)/shard_map/gather_panel/ppermute | solution.py:293
  11.1 2.2 %collective-permute-start.5 = (f32[32,1024]{1,0:T(8,128)S(1)}, f32[32,1024]{1,0:T(8,128)S(1)}, u32[]{:S(2)}, u32[]{:S(2)}) collective-permute-start(f32[32,1024]{1,0:T(8,128)S(1)} %collective-permute-done.1.refs_2_), channel_id=1, source_target_pairs={{0,1},{1,0},{2,3},{3,2},{4,5},{5,4},{6,7},{7,6},{8,9},{9,8},{10,11... | collective-permute-start | bytes 393224 | tf_op jit(solution)/shard_map/gather_panel/ppermute | solution.py:293
  13.3 0.8 collective-permute-done.refs_1_
  14.1 0.6 collective-permute-start.4
  14.7 0.1 pad_add_fusion.ids_ref
  14.8 0.9 collective-permute-done.4.refs_5_
  15.7 0.9 copy-done.1
  16.6 6.1 %product.1 = (bf16[512,1024]{1,0:T(8,128)(2,1)}, f32[64,2176]{1,0:T(8,128)S(1)}, f32[64,2176]{1,0:T(8,128)S(1)}, f32[64,2176]{1,0:T(8,128)S(1)}, f32[64,2176]{1,0:T(8,128)S(1)}) custom-call(s32[3]{0:T(128)S(1)} %pad_add_fusion.ids_ref, f32[32,1024]{1,0:T(8,128)S(1)} %bitcast.16, f32[32,1024]{1,0:T(8,128)S(1)} %collective-permute-done.refs_1_, ...), custom_call_target="tpu_custom_call" | custom-call | flops 3600000000 | bytes 8000000 | tf_op jit(solution)/shard_map/product/pallas_call | solution.py:228
  22.7 0.0 copy-start
  22.7 1.3 collective-permute-start.7
  24.0 2.5 %collective-permute-start.8 = (f32[64,2176]{1,0:T(8,128)S(1)}, f32[64,2176]{1,0:T(8,128)S(1)}, u32[]{:S(2)}, u32[]{:S(2)}) collective-permute-start(f32[64,2176]{1,0:T(8,128)S(1)} %get-tuple-element.16), channel_id=1, source_target_pairs={{0,128},{8,136},{16,144},{24,152},{32,160},{40,168},{48,176},{56,1... | collective-permute-start | bytes 1671176 | tf_op jit(solution)/shard_map/sum_x/ppermute | solution.py:285
  26.4 1.2 collective-permute-start.9
  27.6 10.2 %collective-permute-done.7 = f32[64,2176]{1,0:T(8,128)S(1)} collective-permute-done((f32[64,2176]{1,0:T(8,128)S(1)}, f32[64,2176]{1,0:T(8,128)S(1)}, u32[]{:S(2)}, u32[]{:S(2)}) %collective-permute-start.7) | collective-permute-done | bytes 557088 | tf_op jit(solution)/shard_map/sum_x/ppermute | solution.py:285
  37.8 12.9 %collective-permute-done.8 = f32[64,2176]{1,0:T(8,128)S(1)} collective-permute-done((f32[64,2176]{1,0:T(8,128)S(1)}, f32[64,2176]{1,0:T(8,128)S(1)}, u32[]{:S(2)}, u32[]{:S(2)}) %collective-permute-start.8) | collective-permute-done | bytes 557088 | tf_op jit(solution)/shard_map/sum_x/ppermute | solution.py:285
  50.8 0.1 add_bitcast_fusion
  50.9 24.1 %all_to_all.10 = f32[8,8,2176]{2,1,0:T(8,128)S(1)} all-to-all(f32[8,8,2176]{2,1,0:T(8,128)S(1)} %add_bitcast_fusion), channel_id=1, replica_groups={{0,8,16,24,32,40,48,56},{64,72,80,88,96,104,112,120},{128,136,144,152,1..., dimensions={0} | all-to-all | bytes 1114112 | tf_op jit(solution)/shard_map/sum_z/all_to_all | solution.py:281
  75.0 18.1 %all_to_all.11 = f32[8,8,2176]{2,1,0:T(8,128)S(1)} all-to-all(f32[8,8,2176]{2,1,0:T(8,128)S(1)} %broadcast_in_dim.2), channel_id=1, replica_groups={{0,8,16,24,32,40,48,56},{64,72,80,88,96,104,112,120},{128,136,144,152,1..., dimensions={0} | all-to-all | bytes 1114112 | tf_op jit(solution)/shard_map/gather_z/all_to_all | solution.py:281
  93.1 3.1 %collective-permute-start.16 = (f32[64,2048]{1,0:T(8,128)S(1)}, f32[64,2048]{1,0:T(8,128)S(1)}, u32[]{:S(2)}, u32[]{:S(2)}) collective-permute-start(f32[64,2048]{1,0:T(8,128)S(1)} %slice.9.a0_ref), channel_id=1, source_target_pairs={{0,192},{8,200},{16,208},{24,216},{32,224},{40,232},{48,240},{56,2... | collective-permute-start | bytes 1572872 | tf_op jit(solution)/shard_map/gather_x/ppermute | solution.py:285
  96.2 0.7 collective-permute-start.14
  96.9 2.6 %collective-permute-start.11 = (f32[64,128]{1,0:T(8,128)S(1)}, f32[64,128]{1,0:T(8,128)S(1)}, u32[]{:S(2)}, u32[]{:S(2)}) collective-permute-start(f32[64,128]{1,0:T(8,128)S(1)} %get-tuple-element.26), channel_id=1, source_target_pairs={{0,128},{8,136},{16,144},{24,152},{32,160},{40,168},{48,176},{56,1... | collective-permute-start | bytes 98312 | tf_op jit(solution)/shard_map/gather_gram/ppermute | solution.py:285
  99.5 0.0 collective-permute-start.10
  99.5 18.9 %collective-permute-done.11 = f32[64,128]{1,0:T(8,128)S(1)} collective-permute-done((f32[64,128]{1,0:T(8,128)S(1)}, f32[64,128]{1,0:T(8,128)S(1)}, u32[]{:S(2)}, u32[]{:S(2)}) %collective-permute-start.11) | collective-permute-done | bytes 32800 | tf_op jit(solution)/shard_map/gather_gram/ppermute | solution.py:285
  118.4 4.8 %collective-permute-done.10 = f32[64,128]{1,0:T(8,128)S(1)} collective-permute-done((f32[64,128]{1,0:T(8,128)S(1)}, f32[64,128]{1,0:T(8,128)S(1)}, u32[]{:S(2)}, u32[]{:S(2)}) %collective-permute-start.10) | collective-permute-done | bytes 32800 | tf_op jit(solution)/shard_map/gather_gram/ppermute | solution.py:285
  123.2 5.2 %collective-permute-start.13 = (f32[4,64,128]{2,1,0:T(8,128)S(1)}, f32[4,64,128]{2,1,0:T(8,128)S(1)}, u32[]{:S(2)}, u32[]{:S(2)}) collective-permute-start(f32[4,64,128]{2,1,0:T(8,128)S(1)} %pad_maximum_fusion.mine_ref), channel_id=1, source_target_pairs={{0,1},{1,0},{2,3},{3,2},{4,5},{5,4},{6,7},{7,6},{8,9},{9,8},{10,11... | collective-permute-start | bytes 393224 | tf_op jit(solution)/shard_map/gather_gram/ppermute | solution.py:304
  128.4 1.0 collective-permute-done.13.other_ref
  129.4 14.0 %factor.1 = (f32[256,256]{1,0:T(8,128)}, bf16[512,256]{1,0:T(8,128)(2,1)S(1)}, bf16[1024,256]{1,0:T(8,128)(2,1)S(1)}, bf16[1024,2048]{1,0:T(8,128)(2,1)S(1)}) custom-call(s32[3]{0:T(128)S(1)} %pad_add_fusion.ids_ref, f32[4,64,128]{2,1,0:T(8,128)S(1)} %pad_maximum_fusion.mine_ref, f32[4,64,128]{2,1,0:T(8,128)S(1)} %collective-permute-done.13.other_ref, ...), custom_call_target="tpu_custom_call" | custom-call | flops 1000000 | bytes 1000 | tf_op jit(solution)/shard_map/factor/pallas_call | solution.py:246
  143.4 4.6 %update.1 = (f32[256,2048]{1,0:T(8,128)}, bf16[1024,2048]{1,0:T(8,128)(2,1)}) custom-call(s32[3]{0:T(128)S(1)} %pad_add_fusion.ids_ref, f32[64,2048]{1,0:T(8,128)S(1)} %slice.9.a0_ref, f32[64,2048]{1,0:T(8,128)S(1)} %collective-permute-done.14.a1_ref, f32[64,2048]{1,0:T(8,128)S(1)} %collective-permute-done.15.a2_ref, ...), custom_call_target="tpu_custom_call" | custom-call | flops 3000000000 | bytes 12000000 | tf_op jit(solution)/shard_map/update/pallas_call | solution.py:264
  (18 shorter events, 0.2 us)
Async XLA Ops:
  0.6 7.6 %collective-permute-start.2 = (f32[32,1024]{1,0:T(8,128)}, f32[32,1024]{1,0:T(8,128)S(1)}, u32[]{:S(2)}, u32[]{:S(2)}) collective-permute-start(f32[32,1024]{1,0:T(8,128)} %bitcast.12), channel_id=1, source_target_pairs={{0,6},{1,7},{2,0},{3,1},{4,2},{5,3},{6,4},{7,5},{8,14},{9,15},{10,... | collective-permute-start | bytes 393224 | tf_op jit(solution)/shard_map/gather_panel/ppermute | solution.py:285
  4.3 6.9 %collective-permute-start.1 = (f32[32,1024]{1,0:T(8,128)}, f32[32,1024]{1,0:T(8,128)S(1)}, u32[]{:S(2)}, u32[]{:S(2)}) collective-permute-start(f32[32,1024]{1,0:T(8,128)} %bitcast.13), channel_id=1, source_target_pairs={{0,4},{1,5},{2,6},{3,7},{4,0},{5,1},{6,2},{7,3},{8,12},{9,13},{10,... | collective-permute-start | bytes 393224 | tf_op jit(solution)/shard_map/gather_panel/ppermute | solution.py:285
  4.6 9.5 %collective-permute-start = (f32[32,1024]{1,0:T(8,128)}, f32[32,1024]{1,0:T(8,128)S(1)}, u32[]{:S(2)}, u32[]{:S(2)}) collective-permute-start(f32[32,1024]{1,0:T(8,128)} %bitcast.14), channel_id=1, source_target_pairs={{0,2},{1,3},{2,4},{3,5},{4,6},{5,7},{6,0},{7,1},{8,10},{9,11},{10,... | collective-permute-start | bytes 393224 | tf_op jit(solution)/shard_map/gather_panel/ppermute | solution.py:285
  5.3 9.5 %collective-permute-start.3 = (f32[32,1024]{1,0:T(8,128)}, f32[32,1024]{1,0:T(8,128)S(1)}, u32[]{:S(2)}, u32[]{:S(2)}) collective-permute-start(f32[32,1024]{1,0:T(8,128)} %bitcast.15), channel_id=1, source_target_pairs={{0,1},{1,0},{2,3},{3,2},{4,5},{5,4},{6,7},{7,6},{8,9},{9,8},{10,11... | collective-permute-start | bytes 393224 | tf_op jit(solution)/shard_map/gather_panel/ppermute | solution.py:293
  8.2 6.6 %collective-permute-start.6 = (f32[32,1024]{1,0:T(8,128)S(1)}, f32[32,1024]{1,0:T(8,128)S(1)}, u32[]{:S(2)}, u32[]{:S(2)}) collective-permute-start(f32[32,1024]{1,0:T(8,128)S(1)} %collective-permute-done.2.refs_3_), channel_id=1, source_target_pairs={{0,1},{1,0},{2,3},{3,2},{4,5},{5,4},{6,7},{7,6},{8,9},{9,8},{10,11... | collective-permute-start | bytes 393224 | tf_op jit(solution)/shard_map/gather_panel/ppermute | solution.py:293
  11.1 3.6 %collective-permute-start.5 = (f32[32,1024]{1,0:T(8,128)S(1)}, f32[32,1024]{1,0:T(8,128)S(1)}, u32[]{:S(2)}, u32[]{:S(2)}) collective-permute-start(f32[32,1024]{1,0:T(8,128)S(1)} %collective-permute-done.1.refs_2_), channel_id=1, source_target_pairs={{0,1},{1,0},{2,3},{3,2},{4,5},{5,4},{6,7},{7,6},{8,9},{9,8},{10,11... | collective-permute-start | bytes 393224 | tf_op jit(solution)/shard_map/gather_panel/ppermute | solution.py:293
  14.1 1.6 %collective-permute-start.4 = (f32[32,1024]{1,0:T(8,128)S(1)}, f32[32,1024]{1,0:T(8,128)S(1)}, u32[]{:S(2)}, u32[]{:S(2)}) collective-permute-start(f32[32,1024]{1,0:T(8,128)S(1)} %collective-permute-done.refs_1_), channel_id=1, source_target_pairs={{0,1},{1,0},{2,3},{3,2},{4,5},{5,4},{6,7},{7,6},{8,9},{9,8},{10,11... | collective-permute-start | bytes 393224 | tf_op jit(solution)/shard_map/gather_panel/ppermute | solution.py:293
  15.7 0.9 copy-start.1
  22.7 106.7 %copy-start = (bf16[512,1024]{1,0:T(8,128)(2,1)S(1)}, bf16[512,1024]{1,0:T(8,128)(2,1)}, u32[]{:S(2)}) copy-start(bf16[512,1024]{1,0:T(8,128)(2,1)} %get-tuple-element.18.parts_ref) | copy-start | bytes 3145732
  22.7 15.1 %collective-permute-start.7 = (f32[64,2176]{1,0:T(8,128)S(1)}, f32[64,2176]{1,0:T(8,128)S(1)}, u32[]{:S(2)}, u32[]{:S(2)}) collective-permute-start(f32[64,2176]{1,0:T(8,128)S(1)} %get-tuple-element.15), channel_id=1, source_target_pairs={{0,64},{8,72},{16,80},{24,88},{32,96},{40,104},{48,112},{56,120},{... | collective-permute-start | bytes 1671176 | tf_op jit(solution)/shard_map/sum_x/ppermute | solution.py:285
  24.0 26.8 %collective-permute-start.8 = (f32[64,2176]{1,0:T(8,128)S(1)}, f32[64,2176]{1,0:T(8,128)S(1)}, u32[]{:S(2)}, u32[]{:S(2)}) collective-permute-start(f32[64,2176]{1,0:T(8,128)S(1)} %get-tuple-element.16), channel_id=1, source_target_pairs={{0,128},{8,136},{16,144},{24,152},{32,160},{40,168},{48,176},{56,1... | collective-permute-start | bytes 1671176 | tf_op jit(solution)/shard_map/sum_x/ppermute | solution.py:285
  26.4 24.3 %collective-permute-start.9 = (f32[64,2176]{1,0:T(8,128)S(1)}, f32[64,2176]{1,0:T(8,128)S(1)}, u32[]{:S(2)}, u32[]{:S(2)}) collective-permute-start(f32[64,2176]{1,0:T(8,128)S(1)} %get-tuple-element.17), channel_id=1, source_target_pairs={{0,192},{8,200},{16,208},{24,216},{32,224},{40,232},{48,240},{56,2... | collective-permute-start | bytes 1671176 | tf_op jit(solution)/shard_map/sum_x/ppermute | solution.py:285
  93.1 50.3 %collective-permute-start.16 = (f32[64,2048]{1,0:T(8,128)S(1)}, f32[64,2048]{1,0:T(8,128)S(1)}, u32[]{:S(2)}, u32[]{:S(2)}) collective-permute-start(f32[64,2048]{1,0:T(8,128)S(1)} %slice.9.a0_ref), channel_id=1, source_target_pairs={{0,192},{8,200},{16,208},{24,216},{32,224},{40,232},{48,240},{56,2... | collective-permute-start | bytes 1572872 | tf_op jit(solution)/shard_map/gather_x/ppermute | solution.py:285
  96.2 47.2 %collective-permute-start.15 = (f32[64,2048]{1,0:T(8,128)S(1)}, f32[64,2048]{1,0:T(8,128)S(1)}, u32[]{:S(2)}, u32[]{:S(2)}) collective-permute-start(f32[64,2048]{1,0:T(8,128)S(1)} %slice.9.a0_ref), channel_id=1, source_target_pairs={{0,128},{8,136},{16,144},{24,152},{32,160},{40,168},{48,176},{56,1... | collective-permute-start | bytes 1572872 | tf_op jit(solution)/shard_map/gather_x/ppermute | solution.py:285
  96.2 47.2 %collective-permute-start.14 = (f32[64,2048]{1,0:T(8,128)S(1)}, f32[64,2048]{1,0:T(8,128)S(1)}, u32[]{:S(2)}, u32[]{:S(2)}) collective-permute-start(f32[64,2048]{1,0:T(8,128)S(1)} %slice.9.a0_ref), channel_id=1, source_target_pairs={{0,64},{8,72},{16,80},{24,88},{32,96},{40,104},{48,112},{56,120},{... | collective-permute-start | bytes 1572872 | tf_op jit(solution)/shard_map/gather_x/ppermute | solution.py:285
  96.9 21.5 %collective-permute-start.11 = (f32[64,128]{1,0:T(8,128)S(1)}, f32[64,128]{1,0:T(8,128)S(1)}, u32[]{:S(2)}, u32[]{:S(2)}) collective-permute-start(f32[64,128]{1,0:T(8,128)S(1)} %get-tuple-element.26), channel_id=1, source_target_pairs={{0,128},{8,136},{16,144},{24,152},{32,160},{40,168},{48,176},{56,1... | collective-permute-start | bytes 98312 | tf_op jit(solution)/shard_map/gather_gram/ppermute | solution.py:285
  99.5 23.7 %collective-permute-start.10 = (f32[64,128]{1,0:T(8,128)S(1)}, f32[64,128]{1,0:T(8,128)S(1)}, u32[]{:S(2)}, u32[]{:S(2)}) collective-permute-start(f32[64,128]{1,0:T(8,128)S(1)} %get-tuple-element.26), channel_id=1, source_target_pairs={{0,64},{8,72},{16,80},{24,88},{32,96},{40,104},{48,112},{56,120},{... | collective-permute-start | bytes 98312 | tf_op jit(solution)/shard_map/gather_gram/ppermute | solution.py:285
  118.4 4.8 %collective-permute-start.12 = (f32[64,128]{1,0:T(8,128)S(1)}, f32[64,128]{1,0:T(8,128)S(1)}, u32[]{:S(2)}, u32[]{:S(2)}) collective-permute-start(f32[64,128]{1,0:T(8,128)S(1)} %get-tuple-element.26), channel_id=1, source_target_pairs={{0,192},{8,200},{16,208},{24,216},{32,224},{40,232},{48,240},{56,2... | collective-permute-start | bytes 98312 | tf_op jit(solution)/shard_map/gather_gram/ppermute | solution.py:285
  123.2 6.2 %collective-permute-start.13 = (f32[4,64,128]{2,1,0:T(8,128)S(1)}, f32[4,64,128]{2,1,0:T(8,128)S(1)}, u32[]{:S(2)}, u32[]{:S(2)}) collective-permute-start(f32[4,64,128]{2,1,0:T(8,128)S(1)} %pad_maximum_fusion.mine_ref), channel_id=1, source_target_pairs={{0,1},{1,0},{2,3},{3,2},{4,5},{5,4},{6,7},{7,6},{8,9},{9,8},{10,11... | collective-permute-start | bytes 393224 | tf_op jit(solution)/shard_map/gather_gram/ppermute | solution.py:304

commit v6 on v5

--- a/solution.py
+++ b/solution.py
@@ -255,7 +255,7 @@
         out_specs=(VMEM,) * 4,
         scratch_shapes=[pltpu.VMEM((HALF // 8, 8, HALF), F32)] * 4 + [pltpu.SemaphoreType.DMA],
         compiler_params=limit(45),
-        cost_estimate=cost(1e6, 1e3),
+        cost_estimate=cost(3.5e9, 1e3),
     )(ids, mine, other, parts, trailing)
 
 

time: 148 us -> 129 us (0.87)
  waiting for transfers between devices: 51 us -> 27.2 us
  starting transfers between devices: 28.3 us -> 33.1 us
    ppermute x12, waiting for transfers between devices: 49.1 us -> 25.4 us  [shift(): lax.ppermute(pieces[k], axis, routes[k])]
    ppermute x1, starting transfers between devices: 5.2 us -> 9.25 us  [local(): gram_other = lax.ppermute(gram_mine, 'col', SIBLING)]
  transfers between devices with their start and end apart: 17 -> 17, of which waited for: 8 -> 6; matrix products, arithmetic and copies ran while one was open for 0% -> 0% of each run, Pallas kernels for 9% -> 11%
where the time goes in v6:
time: 129 us
  blocking collectives  42.2 us (33%)
  starting transfers between devices  33.1 us (26%)
  waiting for transfers between devices  27.2 us (21%)
  Pallas kernels  24.7 us (19%)
    all_to_all x2, blocking collectives, swap_z(): return lax.all_to_all(block, 'row', 0, 0, axis_index_groups=Z_GROUPS)  42.2 us
    ppermute x12, waiting for transfers between devices, shift(): lax.ppermute(pieces[k], axis, routes[k])  25.4 us
    ppermute x12, starting transfers between devices, shift(): lax.ppermute(pieces[k], axis, routes[k])  16.7 us
    pallas_call x1, Pallas kernels, factor(): pl.pallas_call(factor_kernel, out_shape=(array(B, B), array(2 * B, B, dty...  14 us
    ppermute x1, starting transfers between devices, local(): gram_other = lax.ppermute(gram_mine, 'col', SIBLING)  9.25 us
    ppermute x4, starting transfers between devices, local(): other = [lax.ppermute(piece, 'col', SIBLING) for piece in mine]  7.23 us
    pallas_call x1, Pallas kernels, product(): pl.pallas_call(product_kernel, out_shape=(array(2 * B, ROWS, dtype=BF16),...  6.08 us
    pallas_call x1, Pallas kernels, update(): pl.pallas_call(update_kernel, out_shape=(array(B, COLS), array(ROWS, COLS...  4.6 us
  transfers between devices with their start and end apart: 17, of which 6 were waited for; matrix products, arithmetic and copies ran while one was open for 0% of the time, Pallas kernels for 11%

profile of v6, /device:TPU:1, one launch (start us, length us, event | category | flops | bytes accessed | tf_op | source)
XLA Modules:
  0.0 129.3 jit_solution(18443059663403827600)
XLA Ops:
  0.6 3.6 %collective-permute-start.2 = (f32[32,1024]{1,0:T(8,128)}, f32[32,1024]{1,0:T(8,128)S(1)}, u32[]{:S(2)}, u32[]{:S(2)}) collective-permute-start(f32[32,1024]{1,0:T(8,128)} %bitcast.12), channel_id=1, source_target_pairs={{0,6},{1,7},{2,0},{3,1},{4,2},{5,3},{6,4},{7,5},{8,14},{9,15},{10,... | collective-permute-start | bytes 393224 | tf_op jit(solution)/shard_map/gather_panel/ppermute | solution.py:285
  4.3 0.3 collective-permute-start.1
  4.6 0.7 collective-permute-start
  5.3 1.5 %collective-permute-start.3 = (f32[32,1024]{1,0:T(8,128)}, f32[32,1024]{1,0:T(8,128)S(1)}, u32[]{:S(2)}, u32[]{:S(2)}) collective-permute-start(f32[32,1024]{1,0:T(8,128)} %bitcast.15), channel_id=1, source_target_pairs={{0,1},{1,0},{2,3},{3,2},{4,5},{5,4},{6,7},{7,6},{8,9},{9,8},{10,11... | collective-permute-start | bytes 393224 | tf_op jit(solution)/shard_map/gather_panel/ppermute | solution.py:293
  6.8 1.4 %collective-permute-done.2.refs_3_ = f32[32,1024]{1,0:T(8,128)S(1)} collective-permute-done((f32[32,1024]{1,0:T(8,128)}, f32[32,1024]{1,0:T(8,128)S(1)}, u32[]{:S(2)}, u32[]{:S(2)}) %collective-permute-start.2) | collective-permute-done | bytes 131104 | tf_op jit(solution)/shard_map/gather_panel/ppermute | solution.py:285
  8.2 2.9 %collective-permute-start.6 = (f32[32,1024]{1,0:T(8,128)S(1)}, f32[32,1024]{1,0:T(8,128)S(1)}, u32[]{:S(2)}, u32[]{:S(2)}) collective-permute-start(f32[32,1024]{1,0:T(8,128)S(1)} %collective-permute-done.2.refs_3_), channel_id=1, source_target_pairs={{0,1},{1,0},{2,3},{3,2},{4,5},{5,4},{6,7},{7,6},{8,9},{9,8},{10,11... | collective-permute-start | bytes 393224 | tf_op jit(solution)/shard_map/gather_panel/ppermute | solution.py:293
  11.1 2.2 %collective-permute-start.5 = (f32[32,1024]{1,0:T(8,128)S(1)}, f32[32,1024]{1,0:T(8,128)S(1)}, u32[]{:S(2)}, u32[]{:S(2)}) collective-permute-start(f32[32,1024]{1,0:T(8,128)S(1)} %collective-permute-done.1.refs_2_), channel_id=1, source_target_pairs={{0,1},{1,0},{2,3},{3,2},{4,5},{5,4},{6,7},{7,6},{8,9},{9,8},{10,11... | collective-permute-start | bytes 393224 | tf_op jit(solution)/shard_map/gather_panel/ppermute | solution.py:293
  13.3 0.8 collective-permute-done.refs_1_
  14.1 0.6 collective-permute-start.4
  14.7 0.1 pad_add_fusion.ids_ref
  14.8 0.9 collective-permute-done.4.refs_5_
  15.7 0.9 copy-done
  16.6 6.1 %product.1 = (bf16[512,1024]{1,0:T(8,128)(2,1)}, f32[64,2176]{1,0:T(8,128)S(1)}, f32[64,2176]{1,0:T(8,128)S(1)}, f32[64,2176]{1,0:T(8,128)S(1)}, f32[64,2176]{1,0:T(8,128)S(1)}) custom-call(s32[3]{0:T(128)S(1)} %pad_add_fusion.ids_ref, f32[32,1024]{1,0:T(8,128)S(1)} %bitcast.16, f32[32,1024]{1,0:T(8,128)S(1)} %collective-permute-done.refs_1_, ...), custom_call_target="tpu_custom_call" | custom-call | flops 3600000000 | bytes 8000000 | tf_op jit(solution)/shard_map/product/pallas_call | solution.py:228
  22.7 0.0 copy-start.1
  22.7 1.3 collective-permute-start.7
  24.0 2.5 %collective-permute-start.8 = (f32[64,2176]{1,0:T(8,128)S(1)}, f32[64,2176]{1,0:T(8,128)S(1)}, u32[]{:S(2)}, u32[]{:S(2)}) collective-permute-start(f32[64,2176]{1,0:T(8,128)S(1)} %get-tuple-element.16), channel_id=1, source_target_pairs={{0,128},{8,136},{16,144},{24,152},{32,160},{40,168},{48,176},{56,1... | collective-permute-start | bytes 1671176 | tf_op jit(solution)/shard_map/sum_x/ppermute | solution.py:285
  26.4 1.2 collective-permute-start.9
  27.6 10.2 %collective-permute-done.7 = f32[64,2176]{1,0:T(8,128)S(1)} collective-permute-done((f32[64,2176]{1,0:T(8,128)S(1)}, f32[64,2176]{1,0:T(8,128)S(1)}, u32[]{:S(2)}, u32[]{:S(2)}) %collective-permute-start.7) | collective-permute-done | bytes 557088 | tf_op jit(solution)/shard_map/sum_x/ppermute | solution.py:285
  37.8 12.9 %collective-permute-done.8 = f32[64,2176]{1,0:T(8,128)S(1)} collective-permute-done((f32[64,2176]{1,0:T(8,128)S(1)}, f32[64,2176]{1,0:T(8,128)S(1)}, u32[]{:S(2)}, u32[]{:S(2)}) %collective-permute-start.8) | collective-permute-done | bytes 557088 | tf_op jit(solution)/shard_map/sum_x/ppermute | solution.py:285
  50.8 0.1 add_bitcast_fusion
  50.9 24.1 %all_to_all.10 = f32[8,8,2176]{2,1,0:T(8,128)S(1)} all-to-all(f32[8,8,2176]{2,1,0:T(8,128)S(1)} %add_bitcast_fusion), channel_id=1, replica_groups={{0,8,16,24,32,40,48,56},{64,72,80,88,96,104,112,120},{128,136,144,152,1..., dimensions={0} | all-to-all | bytes 1114112 | tf_op jit(solution)/shard_map/sum_z/all_to_all | solution.py:281
  75.0 18.1 %all_to_all.11 = f32[8,8,2176]{2,1,0:T(8,128)S(1)} all-to-all(f32[8,8,2176]{2,1,0:T(8,128)S(1)} %broadcast_in_dim.2), channel_id=1, replica_groups={{0,8,16,24,32,40,48,56},{64,72,80,88,96,104,112,120},{128,136,144,152,1..., dimensions={0} | all-to-all | bytes 1114112 | tf_op jit(solution)/shard_map/gather_z/all_to_all | solution.py:281
  93.1 2.1 %collective-permute-start.11 = (f32[64,128]{1,0:T(8,128)S(1)}, f32[64,128]{1,0:T(8,128)S(1)}, u32[]{:S(2)}, u32[]{:S(2)}) collective-permute-start(f32[64,128]{1,0:T(8,128)S(1)} %get-tuple-element.26), channel_id=1, source_target_pairs={{0,128},{8,136},{16,144},{24,152},{32,160},{40,168},{48,176},{56,1... | collective-permute-start | bytes 98312 | tf_op jit(solution)/shard_map/gather_gram/ppermute | solution.py:285
  95.2 1.5 %collective-permute-start.10 = (f32[64,128]{1,0:T(8,128)S(1)}, f32[64,128]{1,0:T(8,128)S(1)}, u32[]{:S(2)}, u32[]{:S(2)}) collective-permute-start(f32[64,128]{1,0:T(8,128)S(1)} %get-tuple-element.26), channel_id=1, source_target_pairs={{0,64},{8,72},{16,80},{24,88},{32,96},{40,104},{48,112},{56,120},{... | collective-permute-start | bytes 98312 | tf_op jit(solution)/shard_map/gather_gram/ppermute | solution.py:285
  96.7 1.2 collective-permute-start.12
  97.9 0.4 collective-permute-start.16
  98.3 2.0 %collective-permute-start.15 = (f32[64,2048]{1,0:T(8,128)S(1)}, f32[64,2048]{1,0:T(8,128)S(1)}, u32[]{:S(2)}, u32[]{:S(2)}) collective-permute-start(f32[64,2048]{1,0:T(8,128)S(1)} %slice.9.a0_ref), channel_id=1, source_target_pairs={{0,128},{8,136},{16,144},{24,152},{32,160},{40,168},{48,176},{56,1... | collective-permute-start | bytes 1572872 | tf_op jit(solution)/shard_map/gather_x/ppermute | solution.py:285
  100.2 0.0 collective-permute-done.12
  100.3 9.3 %collective-permute-start.13 = (f32[4,64,128]{2,1,0:T(8,128)S(1)}, f32[4,64,128]{2,1,0:T(8,128)S(1)}, u32[]{:S(2)}, u32[]{:S(2)}) collective-permute-start(f32[4,64,128]{2,1,0:T(8,128)S(1)} %pad_maximum_fusion.mine_ref), channel_id=1, source_target_pairs={{0,1},{1,0},{2,3},{3,2},{4,5},{5,4},{6,7},{7,6},{8,9},{9,8},{10,11... | collective-permute-start | bytes 393224 | tf_op jit(solution)/shard_map/gather_gram/ppermute | solution.py:304
  109.5 1.0 collective-permute-done.13.other_ref
  110.5 14.0 %factor.1 = (f32[256,256]{1,0:T(8,128)}, bf16[512,256]{1,0:T(8,128)(2,1)S(1)}, bf16[1024,256]{1,0:T(8,128)(2,1)S(1)}, bf16[1024,2048]{1,0:T(8,128)(2,1)S(1)}) custom-call(s32[3]{0:T(128)S(1)} %pad_add_fusion.ids_ref, f32[4,64,128]{2,1,0:T(8,128)S(1)} %pad_maximum_fusion.mine_ref, f32[4,64,128]{2,1,0:T(8,128)S(1)} %collective-permute-done.13.other_ref, ...), custom_call_target="tpu_custom_call" | custom-call | flops 3500000000 | bytes 1000 | tf_op jit(solution)/shard_map/factor/pallas_call | solution.py:246
  124.5 4.6 %update.1 = (f32[256,2048]{1,0:T(8,128)}, bf16[1024,2048]{1,0:T(8,128)(2,1)}) custom-call(s32[3]{0:T(128)S(1)} %pad_add_fusion.ids_ref, f32[64,2048]{1,0:T(8,128)S(1)} %slice.9.a0_ref, f32[64,2048]{1,0:T(8,128)S(1)} %collective-permute-done.14.a1_ref, f32[64,2048]{1,0:T(8,128)S(1)} %collective-permute-done.15.a2_ref, ...), custom_call_target="tpu_custom_call" | custom-call | flops 3000000000 | bytes 12000000 | tf_op jit(solution)/shard_map/update/pallas_call | solution.py:264
  (18 shorter events, 0.2 us)
Async XLA Ops:
  0.6 7.6 %collective-permute-start.2 = (f32[32,1024]{1,0:T(8,128)}, f32[32,1024]{1,0:T(8,128)S(1)}, u32[]{:S(2)}, u32[]{:S(2)}) collective-permute-start(f32[32,1024]{1,0:T(8,128)} %bitcast.12), channel_id=1, source_target_pairs={{0,6},{1,7},{2,0},{3,1},{4,2},{5,3},{6,4},{7,5},{8,14},{9,15},{10,... | collective-permute-start | bytes 393224 | tf_op jit(solution)/shard_map/gather_panel/ppermute | solution.py:285
  4.3 6.9 %collective-permute-start.1 = (f32[32,1024]{1,0:T(8,128)}, f32[32,1024]{1,0:T(8,128)S(1)}, u32[]{:S(2)}, u32[]{:S(2)}) collective-permute-start(f32[32,1024]{1,0:T(8,128)} %bitcast.13), channel_id=1, source_target_pairs={{0,4},{1,5},{2,6},{3,7},{4,0},{5,1},{6,2},{7,3},{8,12},{9,13},{10,... | collective-permute-start | bytes 393224 | tf_op jit(solution)/shard_map/gather_panel/ppermute | solution.py:285
  4.6 9.5 %collective-permute-start = (f32[32,1024]{1,0:T(8,128)}, f32[32,1024]{1,0:T(8,128)S(1)}, u32[]{:S(2)}, u32[]{:S(2)}) collective-permute-start(f32[32,1024]{1,0:T(8,128)} %bitcast.14), channel_id=1, source_target_pairs={{0,2},{1,3},{2,4},{3,5},{4,6},{5,7},{6,0},{7,1},{8,10},{9,11},{10,... | collective-permute-start | bytes 393224 | tf_op jit(solution)/shard_map/gather_panel/ppermute | solution.py:285
  5.3 9.5 %collective-permute-start.3 = (f32[32,1024]{1,0:T(8,128)}, f32[32,1024]{1,0:T(8,128)S(1)}, u32[]{:S(2)}, u32[]{:S(2)}) collective-permute-start(f32[32,1024]{1,0:T(8,128)} %bitcast.15), channel_id=1, source_target_pairs={{0,1},{1,0},{2,3},{3,2},{4,5},{5,4},{6,7},{7,6},{8,9},{9,8},{10,11... | collective-permute-start | bytes 393224 | tf_op jit(solution)/shard_map/gather_panel/ppermute | solution.py:293
  8.2 6.6 %collective-permute-start.6 = (f32[32,1024]{1,0:T(8,128)S(1)}, f32[32,1024]{1,0:T(8,128)S(1)}, u32[]{:S(2)}, u32[]{:S(2)}) collective-permute-start(f32[32,1024]{1,0:T(8,128)S(1)} %collective-permute-done.2.refs_3_), channel_id=1, source_target_pairs={{0,1},{1,0},{2,3},{3,2},{4,5},{5,4},{6,7},{7,6},{8,9},{9,8},{10,11... | collective-permute-start | bytes 393224 | tf_op jit(solution)/shard_map/gather_panel/ppermute | solution.py:293
  11.1 3.6 %collective-permute-start.5 = (f32[32,1024]{1,0:T(8,128)S(1)}, f32[32,1024]{1,0:T(8,128)S(1)}, u32[]{:S(2)}, u32[]{:S(2)}) collective-permute-start(f32[32,1024]{1,0:T(8,128)S(1)} %collective-permute-done.1.refs_2_), channel_id=1, source_target_pairs={{0,1},{1,0},{2,3},{3,2},{4,5},{5,4},{6,7},{7,6},{8,9},{9,8},{10,11... | collective-permute-start | bytes 393224 | tf_op jit(solution)/shard_map/gather_panel/ppermute | solution.py:293
  14.1 1.6 %collective-permute-start.4 = (f32[32,1024]{1,0:T(8,128)S(1)}, f32[32,1024]{1,0:T(8,128)S(1)}, u32[]{:S(2)}, u32[]{:S(2)}) collective-permute-start(f32[32,1024]{1,0:T(8,128)S(1)} %collective-permute-done.refs_1_), channel_id=1, source_target_pairs={{0,1},{1,0},{2,3},{3,2},{4,5},{5,4},{6,7},{7,6},{8,9},{9,8},{10,11... | collective-permute-start | bytes 393224 | tf_op jit(solution)/shard_map/gather_panel/ppermute | solution.py:293
  15.7 0.9 copy-start
  22.7 87.8 %copy-start.1 = (bf16[512,1024]{1,0:T(8,128)(2,1)S(1)}, bf16[512,1024]{1,0:T(8,128)(2,1)}, u32[]{:S(2)}) copy-start(bf16[512,1024]{1,0:T(8,128)(2,1)} %get-tuple-element.18.parts_ref) | copy-start | bytes 3145732
  22.7 15.1 %collective-permute-start.7 = (f32[64,2176]{1,0:T(8,128)S(1)}, f32[64,2176]{1,0:T(8,128)S(1)}, u32[]{:S(2)}, u32[]{:S(2)}) collective-permute-start(f32[64,2176]{1,0:T(8,128)S(1)} %get-tuple-element.15), channel_id=1, source_target_pairs={{0,64},{8,72},{16,80},{24,88},{32,96},{40,104},{48,112},{56,120},{... | collective-permute-start | bytes 1671176 | tf_op jit(solution)/shard_map/sum_x/ppermute | solution.py:285
  24.0 26.8 %collective-permute-start.8 = (f32[64,2176]{1,0:T(8,128)S(1)}, f32[64,2176]{1,0:T(8,128)S(1)}, u32[]{:S(2)}, u32[]{:S(2)}) collective-permute-start(f32[64,2176]{1,0:T(8,128)S(1)} %get-tuple-element.16), channel_id=1, source_target_pairs={{0,128},{8,136},{16,144},{24,152},{32,160},{40,168},{48,176},{56,1... | collective-permute-start | bytes 1671176 | tf_op jit(solution)/shard_map/sum_x/ppermute | solution.py:285
  26.4 24.3 %collective-permute-start.9 = (f32[64,2176]{1,0:T(8,128)S(1)}, f32[64,2176]{1,0:T(8,128)S(1)}, u32[]{:S(2)}, u32[]{:S(2)}) collective-permute-start(f32[64,2176]{1,0:T(8,128)S(1)} %get-tuple-element.17), channel_id=1, source_target_pairs={{0,192},{8,200},{16,208},{24,216},{32,224},{40,232},{48,240},{56,2... | collective-permute-start | bytes 1671176 | tf_op jit(solution)/shard_map/sum_x/ppermute | solution.py:285
  93.1 7.1 %collective-permute-start.11 = (f32[64,128]{1,0:T(8,128)S(1)}, f32[64,128]{1,0:T(8,128)S(1)}, u32[]{:S(2)}, u32[]{:S(2)}) collective-permute-start(f32[64,128]{1,0:T(8,128)S(1)} %get-tuple-element.26), channel_id=1, source_target_pairs={{0,128},{8,136},{16,144},{24,152},{32,160},{40,168},{48,176},{56,1... | collective-permute-start | bytes 98312 | tf_op jit(solution)/shard_map/gather_gram/ppermute | solution.py:285
  95.2 5.1 %collective-permute-start.10 = (f32[64,128]{1,0:T(8,128)S(1)}, f32[64,128]{1,0:T(8,128)S(1)}, u32[]{:S(2)}, u32[]{:S(2)}) collective-permute-start(f32[64,128]{1,0:T(8,128)S(1)} %get-tuple-element.26), channel_id=1, source_target_pairs={{0,64},{8,72},{16,80},{24,88},{32,96},{40,104},{48,112},{56,120},{... | collective-permute-start | bytes 98312 | tf_op jit(solution)/shard_map/gather_gram/ppermute | solution.py:285
  96.7 3.6 %collective-permute-start.12 = (f32[64,128]{1,0:T(8,128)S(1)}, f32[64,128]{1,0:T(8,128)S(1)}, u32[]{:S(2)}, u32[]{:S(2)}) collective-permute-start(f32[64,128]{1,0:T(8,128)S(1)} %get-tuple-element.26), channel_id=1, source_target_pairs={{0,192},{8,200},{16,208},{24,216},{32,224},{40,232},{48,240},{56,2... | collective-permute-start | bytes 98312 | tf_op jit(solution)/shard_map/gather_gram/ppermute | solution.py:285
  97.9 26.6 %collective-permute-start.16 = (f32[64,2048]{1,0:T(8,128)S(1)}, f32[64,2048]{1,0:T(8,128)S(1)}, u32[]{:S(2)}, u32[]{:S(2)}) collective-permute-start(f32[64,2048]{1,0:T(8,128)S(1)} %slice.9.a0_ref), channel_id=1, source_target_pairs={{0,192},{8,200},{16,208},{24,216},{32,224},{40,232},{48,240},{56,2... | collective-permute-start | bytes 1572872 | tf_op jit(solution)/shard_map/gather_x/ppermute | solution.py:285
  98.3 26.3 %collective-permute-start.15 = (f32[64,2048]{1,0:T(8,128)S(1)}, f32[64,2048]{1,0:T(8,128)S(1)}, u32[]{:S(2)}, u32[]{:S(2)}) collective-permute-start(f32[64,2048]{1,0:T(8,128)S(1)} %slice.9.a0_ref), channel_id=1, source_target_pairs={{0,128},{8,136},{16,144},{24,152},{32,160},{40,168},{48,176},{56,1... | collective-permute-start | bytes 1572872 | tf_op jit(solution)/shard_map/gather_x/ppermute | solution.py:285
  100.2 24.3 %collective-permute-start.14 = (f32[64,2048]{1,0:T(8,128)S(1)}, f32[64,2048]{1,0:T(8,128)S(1)}, u32[]{:S(2)}, u32[]{:S(2)}) collective-permute-start(f32[64,2048]{1,0:T(8,128)S(1)} %slice.9.a0_ref), channel_id=1, source_target_pairs={{0,64},{8,72},{16,80},{24,88},{32,96},{40,104},{48,112},{56,120},{... | collective-permute-start | bytes 1572872 | tf_op jit(solution)/shard_map/gather_x/ppermute | solution.py:285
  100.3 10.2 %collective-permute-start.13 = (f32[4,64,128]{2,1,0:T(8,128)S(1)}, f32[4,64,128]{2,1,0:T(8,128)S(1)}, u32[]{:S(2)}, u32[]{:S(2)}) collective-permute-start(f32[4,64,128]{2,1,0:T(8,128)S(1)} %pad_maximum_fusion.mine_ref), channel_id=1, source_target_pairs={{0,1},{1,0},{2,3},{3,2},{4,5},{5,4},{6,7},{7,6},{8,9},{9,8},{10,11... | collective-permute-start | bytes 393224 | tf_op jit(solution)/shard_map/gather_gram/ppermute | solution.py:304

commit v7 on v6

--- a/solution.py
+++ b/solution.py
@@ -85,6 +85,27 @@
         slot = whole.at[tile // 2 % 2]
         slot[...] = both[B:] + both[:B]
         hand_out(slot, columns)
+
+
+def blocks_of(ref):
+    return [(slice(r, r + 16), slice(c, c + HALF)) for r in range(0, 64, 16) for c in range(0, ref.shape[1], HALF)]
+
+
+def add_kernel(p0_ref, p1_ref, p2_ref, p3_ref, *outs):
+    for out, place in zip(outs, blocks_of(p0_ref)):
+        out[...] = p0_ref[place] + p1_ref[place] + (p2_ref[place] + p3_ref[place])
+
+
+def join_kernel(*refs):
+    blocks, sums_ref, gram_ref = refs[:-2], refs[-2], refs[-1]
+    count = (COLS + HALF) // HALF
+    for at, block in enumerate(blocks):
+        row, column = divmod(at, count)
+        rows = slice(16 * row, 16 * row + 16)
+        if column < count - 1:
+            sums_ref[rows, column * HALF:column * HALF + HALF] = block[...]
+        else:
+            gram_ref[rows] = block[...]
 
 
 def eliminate(work, unit, upper, inverse):
@@ -277,8 +298,27 @@
     )(ids, *a, inverse, low, trailing)
 
 
-def swap_z(block):
-    return lax.all_to_all(block, "row", 0, 0, axis_index_groups=Z_GROUPS)
+def add(pieces):
+    count = 4 * (COLS + HALF) // HALF
+    return pl.pallas_call(
+        add_kernel,
+        out_shape=(array(16, HALF),) * count,
+        in_specs=[VMEM] * 4,
+        out_specs=(VMEM,) * count,
+        compiler_params=limit(16),
+        cost_estimate=cost(1e6, 3e6),
+    )(*pieces)
+
+
+def join(blocks):
+    return pl.pallas_call(
+        join_kernel,
+        out_shape=(array(64, COLS), array(64, HALF)),
+        in_specs=[VMEM] * len(blocks),
+        out_specs=(VMEM,) * 2,
+        compiler_params=limit(16),
+        cost_estimate=cost(1e6, 1e6),
+    )(*blocks)
 
 
 def shift(pieces, axis, routes):
@@ -294,16 +334,14 @@
     with jax.named_scope("product"):
         parts, *pieces = product(ids, mine, other, trailing)
     with jax.named_scope("sum_x"):
-        sums = sum(shift(pieces, "row", X_ROUTES))
+        blocks = add(shift(pieces, "row", X_ROUTES))
     with jax.named_scope("sum_z"):
-        sums = jnp.sum(swap_z(sums.reshape(NZ, 8, COLS + HALF)), axis=0)
-    with jax.named_scope("gather_z"):
-        sums = swap_z(jnp.broadcast_to(sums[None], (NZ, 8, COLS + HALF))).reshape(64, COLS + HALF)
+        sums, gram = join(lax.psum(tuple(blocks), "row", axis_index_groups=Z_GROUPS))
     with jax.named_scope("gather_gram"):
-        gram_mine = jnp.stack(shift([sums[:, COLS:]] * NX, "row", X_ROUTES))
+        gram_mine = jnp.stack(shift([gram] * NX, "row", X_ROUTES))
         gram_other = lax.ppermute(gram_mine, "col", SIBLING)
     with jax.named_scope("gather_x"):
-        blocks = shift([sums[:, :COLS]] * NX, "row", X_ROUTES)
+        blocks = shift([sums] * NX, "row", X_ROUTES)
     with jax.named_scope("factor"):
         r_factor, inverse, low, trailing = factor(ids, gram_mine, gram_other, parts, trailing)
     with jax.named_scope("update"):

time: 129 us -> 124 us (0.961)
  blocking collectives: 42.2 us -> 34.3 us
    all_to_all x2 -> x0, blocking collectives: 42.2 us -> none  [swap_z(): return lax.all_to_all(block, 'row', 0, 0, axis_index_groups=Z_GROUPS)]
    psum x0 -> x1, blocking collectives: none -> 34.3 us  [local(): lax.psum(tuple(blocks), 'row', axis_index_groups=Z_GROUPS)]
  transfers between devices with their start and end apart: 17 -> 17, of which waited for: 6 -> 7; matrix products, arithmetic and copies ran while one was open for 0% -> 0% of each run, Pallas kernels for 11% -> 11%
where the time goes in v7:
time: 124 us
  blocking collectives  34.3 us (28%)
  starting transfers between devices  33.5 us (27%)
  waiting for transfers between devices  27.8 us (22%)
  Pallas kernels  24.9 us (20%)
  local copies, waits for them, and re-layouts  2.13 us (2%)
    psum x1, blocking collectives, local(): lax.psum(tuple(blocks), 'row', axis_index_groups=Z_GROUPS)  34.3 us
    ppermute x12, waiting for transfers between devices, shift(): lax.ppermute(pieces[k], axis, routes[k])  25.9 us
    ppermute x12, starting transfers between devices, shift(): lax.ppermute(pieces[k], axis, routes[k])  15.8 us
    pallas_call x1, Pallas kernels, factor(): pl.pallas_call(factor_kernel, out_shape=(array(B, B), array(2 * B, B, dty...  14 us
    ppermute x1, starting transfers between devices, local(): gram_other = lax.ppermute(gram_mine, 'col', SIBLING)  10.5 us
    ppermute x4, starting transfers between devices, local(): other = [lax.ppermute(piece, 'col', SIBLING) for piece in mine]  7.23 us
    pallas_call x1, Pallas kernels, product(): pl.pallas_call(product_kernel, out_shape=(array(2 * B, ROWS, dtype=BF16),...  6.08 us
    pallas_call x1, Pallas kernels, update(): pl.pallas_call(update_kernel, out_shape=(array(B, COLS), array(ROWS, COLS...  4.59 us
  transfers between devices with their start and end apart: 17, of which 7 were waited for; matrix products, arithmetic and copies ran while one was open for 0% of the time, Pallas kernels for 11%

profile of v7, /device:TPU:1, one launch (start us, length us, event | category | flops | bytes accessed | tf_op | source)
XLA Modules:
  0.0 123.5 jit_solution(3861968389092242232)
XLA Ops:
  0.6 3.6 %collective-permute-start.2 = (f32[32,1024]{1,0:T(8,128)}, f32[32,1024]{1,0:T(8,128)S(1)}, u32[]{:S(2)}, u32[]{:S(2)}) collective-permute-start(f32[32,1024]{1,0:T(8,128)} %bitcast.9), channel_id=1, source_target_pairs={{0,6},{1,7},{2,0},{3,1},{4,2},{5,3},{6,4},{7,5},{8,14},{9,15},{10,... | collective-permute-start | bytes 393224 | tf_op jit(solution)/shard_map/gather_panel/ppermute | solution.py:325
  4.3 0.3 collective-permute-start.1
  4.6 0.7 collective-permute-start
  5.3 1.5 %collective-permute-start.3 = (f32[32,1024]{1,0:T(8,128)}, f32[32,1024]{1,0:T(8,128)S(1)}, u32[]{:S(2)}, u32[]{:S(2)}) collective-permute-start(f32[32,1024]{1,0:T(8,128)} %bitcast.12), channel_id=1, source_target_pairs={{0,1},{1,0},{2,3},{3,2},{4,5},{5,4},{6,7},{7,6},{8,9},{9,8},{10,11... | collective-permute-start | bytes 393224 | tf_op jit(solution)/shard_map/gather_panel/ppermute | solution.py:333
  6.8 1.4 %collective-permute-done.2.refs_3_ = f32[32,1024]{1,0:T(8,128)S(1)} collective-permute-done((f32[32,1024]{1,0:T(8,128)}, f32[32,1024]{1,0:T(8,128)S(1)}, u32[]{:S(2)}, u32[]{:S(2)}) %collective-permute-start.2) | collective-permute-done | bytes 131104 | tf_op jit(solution)/shard_map/gather_panel/ppermute | solution.py:325
  8.2 2.9 %collective-permute-start.6 = (f32[32,1024]{1,0:T(8,128)S(1)}, f32[32,1024]{1,0:T(8,128)S(1)}, u32[]{:S(2)}, u32[]{:S(2)}) collective-permute-start(f32[32,1024]{1,0:T(8,128)S(1)} %collective-permute-done.2.refs_3_), channel_id=1, source_target_pairs={{0,1},{1,0},{2,3},{3,2},{4,5},{5,4},{6,7},{7,6},{8,9},{9,8},{10,11... | collective-permute-start | bytes 393224 | tf_op jit(solution)/shard_map/gather_panel/ppermute | solution.py:333
  11.1 2.2 %collective-permute-start.5 = (f32[32,1024]{1,0:T(8,128)S(1)}, f32[32,1024]{1,0:T(8,128)S(1)}, u32[]{:S(2)}, u32[]{:S(2)}) collective-permute-start(f32[32,1024]{1,0:T(8,128)S(1)} %collective-permute-done.1.refs_2_), channel_id=1, source_target_pairs={{0,1},{1,0},{2,3},{3,2},{4,5},{5,4},{6,7},{7,6},{8,9},{9,8},{10,11... | collective-permute-start | bytes 393224 | tf_op jit(solution)/shard_map/gather_panel/ppermute | solution.py:333
  13.3 0.8 collective-permute-done.refs_1_
  14.1 0.6 collective-permute-start.4
  14.7 0.1 pad_add_fusion.ids_ref
  14.8 0.9 collective-permute-done.4.refs_5_
  15.7 0.9 copy-done
  16.6 6.1 %product.1 = (bf16[512,1024]{1,0:T(8,128)(2,1)}, f32[64,2176]{1,0:T(8,128)S(1)}, f32[64,2176]{1,0:T(8,128)S(1)}, f32[64,2176]{1,0:T(8,128)S(1)}, f32[64,2176]{1,0:T(8,128)S(1)}) custom-call(s32[3]{0:T(128)S(1)} %pad_add_fusion.ids_ref, f32[32,1024]{1,0:T(8,128)S(1)} %bitcast.13, f32[32,1024]{1,0:T(8,128)S(1)} %collective-permute-done.refs_1_, ...), custom_call_target="tpu_custom_call" | custom-call | flops 3600000000 | bytes 8000000 | tf_op jit(solution)/shard_map/product/pallas_call | solution.py:249
  22.7 1.3 %collective-permute-start.7 = (f32[64,2176]{1,0:T(8,128)S(1)}, f32[64,2176]{1,0:T(8,128)S(1)}, u32[]{:S(2)}, u32[]{:S(2)}) collective-permute-start(f32[64,2176]{1,0:T(8,128)S(1)} %get-tuple-element.85), channel_id=1, source_target_pairs={{0,64},{8,72},{16,80},{24,88},{32,96},{40,104},{48,112},{56,120},{... | collective-permute-start | bytes 1671176 | tf_op jit(solution)/shard_map/sum_x/ppermute | solution.py:325
  24.0 2.5 %collective-permute-start.8 = (f32[64,2176]{1,0:T(8,128)S(1)}, f32[64,2176]{1,0:T(8,128)S(1)}, u32[]{:S(2)}, u32[]{:S(2)}) collective-permute-start(f32[64,2176]{1,0:T(8,128)S(1)} %get-tuple-element.86), channel_id=1, source_target_pairs={{0,128},{8,136},{16,144},{24,152},{32,160},{40,168},{48,176},{56,1... | collective-permute-start | bytes 1671176 | tf_op jit(solution)/shard_map/sum_x/ppermute | solution.py:325
  26.4 1.2 collective-permute-start.9
  27.6 10.2 %collective-permute-done.7.p1_ref = f32[64,2176]{1,0:T(8,128)S(1)} collective-permute-done((f32[64,2176]{1,0:T(8,128)S(1)}, f32[64,2176]{1,0:T(8,128)S(1)}, u32[]{:S(2)}, u32[]{:S(2)}) %collective-permute-start.7) | collective-permute-done | bytes 557088 | tf_op jit(solution)/shard_map/sum_x/ppermute | solution.py:325
  37.8 12.9 %collective-permute-done.8.p2_ref = f32[64,2176]{1,0:T(8,128)S(1)} collective-permute-done((f32[64,2176]{1,0:T(8,128)S(1)}, f32[64,2176]{1,0:T(8,128)S(1)}, u32[]{:S(2)}, u32[]{:S(2)}) %collective-permute-start.8) | collective-permute-done | bytes 557088 | tf_op jit(solution)/shard_map/sum_x/ppermute | solution.py:325
  50.8 0.1 sum_x.1
  50.9 34.3 %all-reduce.2 = (f32[16,128]{1,0:T(8,128)S(1)}, f32[16,128]{1,0:T(8,128)S(1)}, f32[16,128]{1,0:T(8,128)S(1)}, f32[16,128]{1,0:T(8,128)S(1)}, f32[16,128]{1,0:T(8...) all-reduce(f32[16,128]{1,0:T(8,128)S(1)} %get-tuple-element.88, ...), channel_id=1, replica_groups={{0,8,16,24,32,40,48,56},{64,72,80,88,96,104,112,120},{128,136,144,152,1..., use_global_device_ids=true, to_apply=%region_0.1 | all-reduce | flops 139264 | bytes 1114112 | tf_op jit(solution)/shard_map/sum_z/psum | solution.py:339
  85.2 0.1 sum_z.1
  85.3 1.8 %collective-permute-start.12 = (f32[64,128]{1,0:T(8,128)S(1)}, f32[64,128]{1,0:T(8,128)S(1)}, u32[]{:S(2)}, u32[]{:S(2)}) collective-permute-start(f32[64,128]{1,0:T(8,128)S(1)} %get-tuple-element.156), channel_id=1, source_target_pairs={{0,192},{8,200},{16,208},{24,216},{32,224},{40,232},{48,240},{56,2... | collective-permute-start | bytes 98312 | tf_op jit(solution)/shard_map/gather_gram/ppermute | solution.py:325
  87.1 1.0 collective-permute-start.11
  88.1 0.5 collective-permute-start.10
  88.6 2.2 %collective-permute-start.16 = (f32[64,2048]{1,0:T(8,128)S(1)}, f32[64,2048]{1,0:T(8,128)S(1)}, u32[]{:S(2)}, u32[]{:S(2)}) collective-permute-start(f32[64,2048]{1,0:T(8,128)S(1)} %get-tuple-element.159.a0_ref), channel_id=1, source_target_pairs={{0,192},{8,200},{16,208},{24,216},{32,224},{40,232},{48,240},{56,2... | collective-permute-start | bytes 1572872 | tf_op jit(solution)/shard_map/gather_x/ppermute | solution.py:325
  90.8 0.7 collective-permute-start.15
  91.5 0.5 collective-permute-done.10
  92.1 10.5 %collective-permute-start.13 = (f32[4,64,128]{2,1,0:T(8,128)S(1)}, f32[4,64,128]{2,1,0:T(8,128)S(1)}, u32[]{:S(2)}, u32[]{:S(2)}) collective-permute-start(f32[4,64,128]{2,1,0:T(8,128)S(1)} %pad_maximum_fusion.mine_ref), channel_id=1, source_target_pairs={{0,1},{1,0},{2,3},{3,2},{4,5},{5,4},{6,7},{7,6},{8,9},{9,8},{10,11... | collective-permute-start | bytes 393224 | tf_op jit(solution)/shard_map/gather_gram/ppermute | solution.py:342
  102.5 1.0 collective-permute-done.13.other_ref
  103.5 1.2 copy-done.1
  104.7 14.0 %factor.1 = (f32[256,256]{1,0:T(8,128)}, bf16[512,256]{1,0:T(8,128)(2,1)S(1)}, bf16[1024,256]{1,0:T(8,128)(2,1)S(1)}, bf16[1024,2048]{1,0:T(8,128)(2,1)S(1)}) custom-call(s32[3]{0:T(128)S(1)} %pad_add_fusion.ids_ref, f32[4,64,128]{2,1,0:T(8,128)S(1)} %pad_maximum_fusion.mine_ref, f32[4,64,128]{2,1,0:T(8,128)S(1)} %collective-permute-done.13.other_ref, ...), custom_call_target="tpu_custom_call" | custom-call | flops 3500000000 | bytes 1000 | tf_op jit(solution)/shard_map/factor/pallas_call | solution.py:267
  118.8 4.6 %update.1 = (f32[256,2048]{1,0:T(8,128)}, bf16[1024,2048]{1,0:T(8,128)(2,1)}) custom-call(s32[3]{0:T(128)S(1)} %pad_add_fusion.ids_ref, f32[64,2048]{1,0:T(8,128)S(1)} %get-tuple-element.159.a0_ref, f32[64,2048]{1,0:T(8,128)S(1)} %collective-permute-done.14.a1_ref, f32[64,2048]{1,0:T(8,128)S(1)} %collective-permute-done.15.a2_ref, ...), custom_call_target="tpu_custom_call" | custom-call | flops 3000000000 | bytes 12000000 | tf_op jit(solution)/shard_map/update/pallas_call | solution.py:285
  (14 shorter events, 0.0 us)
Async XLA Ops:
  0.6 7.6 %collective-permute-start.2 = (f32[32,1024]{1,0:T(8,128)}, f32[32,1024]{1,0:T(8,128)S(1)}, u32[]{:S(2)}, u32[]{:S(2)}) collective-permute-start(f32[32,1024]{1,0:T(8,128)} %bitcast.9), channel_id=1, source_target_pairs={{0,6},{1,7},{2,0},{3,1},{4,2},{5,3},{6,4},{7,5},{8,14},{9,15},{10,... | collective-permute-start | bytes 393224 | tf_op jit(solution)/shard_map/gather_panel/ppermute | solution.py:325
  4.3 6.9 %collective-permute-start.1 = (f32[32,1024]{1,0:T(8,128)}, f32[32,1024]{1,0:T(8,128)S(1)}, u32[]{:S(2)}, u32[]{:S(2)}) collective-permute-start(f32[32,1024]{1,0:T(8,128)} %bitcast.10), channel_id=1, source_target_pairs={{0,4},{1,5},{2,6},{3,7},{4,0},{5,1},{6,2},{7,3},{8,12},{9,13},{10,... | collective-permute-start | bytes 393224 | tf_op jit(solution)/shard_map/gather_panel/ppermute | solution.py:325
  4.6 9.5 %collective-permute-start = (f32[32,1024]{1,0:T(8,128)}, f32[32,1024]{1,0:T(8,128)S(1)}, u32[]{:S(2)}, u32[]{:S(2)}) collective-permute-start(f32[32,1024]{1,0:T(8,128)} %bitcast.11), channel_id=1, source_target_pairs={{0,2},{1,3},{2,4},{3,5},{4,6},{5,7},{6,0},{7,1},{8,10},{9,11},{10,... | collective-permute-start | bytes 393224 | tf_op jit(solution)/shard_map/gather_panel/ppermute | solution.py:325
  5.3 9.5 %collective-permute-start.3 = (f32[32,1024]{1,0:T(8,128)}, f32[32,1024]{1,0:T(8,128)S(1)}, u32[]{:S(2)}, u32[]{:S(2)}) collective-permute-start(f32[32,1024]{1,0:T(8,128)} %bitcast.12), channel_id=1, source_target_pairs={{0,1},{1,0},{2,3},{3,2},{4,5},{5,4},{6,7},{7,6},{8,9},{9,8},{10,11... | collective-permute-start | bytes 393224 | tf_op jit(solution)/shard_map/gather_panel/ppermute | solution.py:333
  8.2 6.6 %collective-permute-start.6 = (f32[32,1024]{1,0:T(8,128)S(1)}, f32[32,1024]{1,0:T(8,128)S(1)}, u32[]{:S(2)}, u32[]{:S(2)}) collective-permute-start(f32[32,1024]{1,0:T(8,128)S(1)} %collective-permute-done.2.refs_3_), channel_id=1, source_target_pairs={{0,1},{1,0},{2,3},{3,2},{4,5},{5,4},{6,7},{7,6},{8,9},{9,8},{10,11... | collective-permute-start | bytes 393224 | tf_op jit(solution)/shard_map/gather_panel/ppermute | solution.py:333
  11.1 3.6 %collective-permute-start.5 = (f32[32,1024]{1,0:T(8,128)S(1)}, f32[32,1024]{1,0:T(8,128)S(1)}, u32[]{:S(2)}, u32[]{:S(2)}) collective-permute-start(f32[32,1024]{1,0:T(8,128)S(1)} %collective-permute-done.1.refs_2_), channel_id=1, source_target_pairs={{0,1},{1,0},{2,3},{3,2},{4,5},{5,4},{6,7},{7,6},{8,9},{9,8},{10,11... | collective-permute-start | bytes 393224 | tf_op jit(solution)/shard_map/gather_panel/ppermute | solution.py:333
  14.1 1.6 %collective-permute-start.4 = (f32[32,1024]{1,0:T(8,128)S(1)}, f32[32,1024]{1,0:T(8,128)S(1)}, u32[]{:S(2)}, u32[]{:S(2)}) collective-permute-start(f32[32,1024]{1,0:T(8,128)S(1)} %collective-permute-done.refs_1_), channel_id=1, source_target_pairs={{0,1},{1,0},{2,3},{3,2},{4,5},{5,4},{6,7},{7,6},{8,9},{9,8},{10,11... | collective-permute-start | bytes 393224 | tf_op jit(solution)/shard_map/gather_panel/ppermute | solution.py:333
  15.7 0.9 copy-start
  22.7 15.1 %collective-permute-start.7 = (f32[64,2176]{1,0:T(8,128)S(1)}, f32[64,2176]{1,0:T(8,128)S(1)}, u32[]{:S(2)}, u32[]{:S(2)}) collective-permute-start(f32[64,2176]{1,0:T(8,128)S(1)} %get-tuple-element.85), channel_id=1, source_target_pairs={{0,64},{8,72},{16,80},{24,88},{32,96},{40,104},{48,112},{56,120},{... | collective-permute-start | bytes 1671176 | tf_op jit(solution)/shard_map/sum_x/ppermute | solution.py:325
  24.0 26.8 %collective-permute-start.8 = (f32[64,2176]{1,0:T(8,128)S(1)}, f32[64,2176]{1,0:T(8,128)S(1)}, u32[]{:S(2)}, u32[]{:S(2)}) collective-permute-start(f32[64,2176]{1,0:T(8,128)S(1)} %get-tuple-element.86), channel_id=1, source_target_pairs={{0,128},{8,136},{16,144},{24,152},{32,160},{40,168},{48,176},{56,1... | collective-permute-start | bytes 1671176 | tf_op jit(solution)/shard_map/sum_x/ppermute | solution.py:325
  26.4 24.3 %collective-permute-start.9 = (f32[64,2176]{1,0:T(8,128)S(1)}, f32[64,2176]{1,0:T(8,128)S(1)}, u32[]{:S(2)}, u32[]{:S(2)}) collective-permute-start(f32[64,2176]{1,0:T(8,128)S(1)} %get-tuple-element.87), channel_id=1, source_target_pairs={{0,192},{8,200},{16,208},{24,216},{32,224},{40,232},{48,240},{56,2... | collective-permute-start | bytes 1671176 | tf_op jit(solution)/shard_map/sum_x/ppermute | solution.py:325
  85.3 6.2 %collective-permute-start.12 = (f32[64,128]{1,0:T(8,128)S(1)}, f32[64,128]{1,0:T(8,128)S(1)}, u32[]{:S(2)}, u32[]{:S(2)}) collective-permute-start(f32[64,128]{1,0:T(8,128)S(1)} %get-tuple-element.156), channel_id=1, source_target_pairs={{0,192},{8,200},{16,208},{24,216},{32,224},{40,232},{48,240},{56,2... | collective-permute-start | bytes 98312 | tf_op jit(solution)/shard_map/gather_gram/ppermute | solution.py:325
  87.1 4.4 %collective-permute-start.11 = (f32[64,128]{1,0:T(8,128)S(1)}, f32[64,128]{1,0:T(8,128)S(1)}, u32[]{:S(2)}, u32[]{:S(2)}) collective-permute-start(f32[64,128]{1,0:T(8,128)S(1)} %get-tuple-element.156), channel_id=1, source_target_pairs={{0,128},{8,136},{16,144},{24,152},{32,160},{40,168},{48,176},{56,1... | collective-permute-start | bytes 98312 | tf_op jit(solution)/shard_map/gather_gram/ppermute | solution.py:325
  88.1 4.0 %collective-permute-start.10 = (f32[64,128]{1,0:T(8,128)S(1)}, f32[64,128]{1,0:T(8,128)S(1)}, u32[]{:S(2)}, u32[]{:S(2)}) collective-permute-start(f32[64,128]{1,0:T(8,128)S(1)} %get-tuple-element.156), channel_id=1, source_target_pairs={{0,64},{8,72},{16,80},{24,88},{32,96},{40,104},{48,112},{56,120},{... | collective-permute-start | bytes 98312 | tf_op jit(solution)/shard_map/gather_gram/ppermute | solution.py:325
  88.6 30.1 %collective-permute-start.16 = (f32[64,2048]{1,0:T(8,128)S(1)}, f32[64,2048]{1,0:T(8,128)S(1)}, u32[]{:S(2)}, u32[]{:S(2)}) collective-permute-start(f32[64,2048]{1,0:T(8,128)S(1)} %get-tuple-element.159.a0_ref), channel_id=1, source_target_pairs={{0,192},{8,200},{16,208},{24,216},{32,224},{40,232},{48,240},{56,2... | collective-permute-start | bytes 1572872 | tf_op jit(solution)/shard_map/gather_x/ppermute | solution.py:325
  90.8 28.0 %collective-permute-start.15 = (f32[64,2048]{1,0:T(8,128)S(1)}, f32[64,2048]{1,0:T(8,128)S(1)}, u32[]{:S(2)}, u32[]{:S(2)}) collective-permute-start(f32[64,2048]{1,0:T(8,128)S(1)} %get-tuple-element.159.a0_ref), channel_id=1, source_target_pairs={{0,128},{8,136},{16,144},{24,152},{32,160},{40,168},{48,176},{56,1... | collective-permute-start | bytes 1572872 | tf_op jit(solution)/shard_map/gather_x/ppermute | solution.py:325
  91.5 27.3 %collective-permute-start.14 = (f32[64,2048]{1,0:T(8,128)S(1)}, f32[64,2048]{1,0:T(8,128)S(1)}, u32[]{:S(2)}, u32[]{:S(2)}) collective-permute-start(f32[64,2048]{1,0:T(8,128)S(1)} %get-tuple-element.159.a0_ref), channel_id=1, source_target_pairs={{0,64},{8,72},{16,80},{24,88},{32,96},{40,104},{48,112},{56,120},{... | collective-permute-start | bytes 1572872 | tf_op jit(solution)/shard_map/gather_x/ppermute | solution.py:325
  92.1 11.4 %collective-permute-start.13 = (f32[4,64,128]{2,1,0:T(8,128)S(1)}, f32[4,64,128]{2,1,0:T(8,128)S(1)}, u32[]{:S(2)}, u32[]{:S(2)}) collective-permute-start(f32[4,64,128]{2,1,0:T(8,128)S(1)} %pad_maximum_fusion.mine_ref), channel_id=1, source_target_pairs={{0,1},{1,0},{2,3},{3,2},{4,5},{5,4},{6,7},{7,6},{8,9},{9,8},{10,11... | collective-permute-start | bytes 393224 | tf_op jit(solution)/shard_map/gather_gram/ppermute | solution.py:342
  103.5 1.2 copy-start.1

commit v8 on v7

--- a/solution.py
+++ b/solution.py
@@ -85,6 +85,12 @@
         slot = whole.at[tile // 2 % 2]
         slot[...] = both[B:] + both[:B]
         hand_out(slot, columns)
+
+
+def bring_kernel(source_ref, target_ref, arrived):
+    fetch = pltpu.make_async_copy(source_ref, target_ref, arrived)
+    fetch.start()
+    fetch.wait()
 
 
 def blocks_of(ref):
@@ -321,6 +327,18 @@
     )(*blocks)
 
 
+def bring(value):
+    return pl.pallas_call(
+        bring_kernel,
+        out_shape=array(*value.shape, dtype=value.dtype),
+        in_specs=[HBM],
+        out_specs=VMEM,
+        scratch_shapes=[pltpu.SemaphoreType.DMA],
+        compiler_params=limit(45),
+        cost_estimate=cost(1e6, 2e6),
+    )(value)
+
+
 def shift(pieces, axis, routes):
     return [pieces[0]] + [lax.ppermute(pieces[k], axis, routes[k]) for k in range(1, 4)]
 
@@ -331,6 +349,7 @@
     with jax.named_scope("gather_panel"):
         mine = shift([panel.T] * 4, "col", Y_ROUTES)
         other = [lax.ppermute(piece, "col", SIBLING) for piece in mine]
+        mine[0] = bring(mine[0])
     with jax.named_scope("product"):
         parts, *pieces = product(ids, mine, other, trailing)
     with jax.named_scope("sum_x"):

time: 124 us -> 123 us (level)
  transfers between devices with their start and end apart: 17 -> 17, of which waited for: 7 -> 6; matrix products, arithmetic and copies ran while one was open for 0% -> 0% of each run, Pallas kernels for 11% -> 12%
where the time goes in v8:
time: 123 us
  blocking collectives  34.1 us (28%)
  starting transfers between devices  33.2 us (27%)
  waiting for transfers between devices  27.3 us (22%)
  Pallas kernels  25 us (20%)
  local copies, waits for them, and re-layouts  2.13 us (2%)
    psum x1, blocking collectives, local(): lax.psum(tuple(blocks), 'row', axis_index_groups=Z_GROUPS)  34.1 us
    ppermute x12, waiting for transfers between devices, shift(): lax.ppermute(pieces[k], axis, routes[k])  26.3 us
    ppermute x12, starting transfers between devices, shift(): lax.ppermute(pieces[k], axis, routes[k])  15.8 us
    pallas_call x1, Pallas kernels, factor(): pl.pallas_call(factor_kernel, out_shape=(array(B, B), array(2 * B, B, dty...  14 us
    ppermute x1, starting transfers between devices, local(): gram_other = lax.ppermute(gram_mine, 'col', SIBLING)  10.2 us
    ppermute x4, starting transfers between devices, local(): other = [lax.ppermute(piece, 'col', SIBLING) for piece in mine]  7.23 us
    pallas_call x1, Pallas kernels, product(): pl.pallas_call(product_kernel, out_shape=(array(2 * B, ROWS, dtype=BF16),...  6.09 us
    pallas_call x1, Pallas kernels, update(): pl.pallas_call(update_kernel, out_shape=(array(B, COLS), array(ROWS, COLS...  4.6 us
  transfers between devices with their start and end apart: 17, of which 6 were waited for; matrix products, arithmetic and copies ran while one was open for 0% of the time, Pallas kernels for 12%

profile of v8, /device:TPU:1, one launch (start us, length us, event | category | flops | bytes accessed | tf_op | source)
XLA Modules:
  0.0 122.8 jit_solution(10542830965817496570)
XLA Ops:
  0.6 3.6 %collective-permute-start.2 = (f32[32,1024]{1,0:T(8,128)}, f32[32,1024]{1,0:T(8,128)S(1)}, u32[]{:S(2)}, u32[]{:S(2)}) collective-permute-start(f32[32,1024]{1,0:T(8,128)} %bitcast.8), channel_id=1, source_target_pairs={{0,6},{1,7},{2,0},{3,1},{4,2},{5,3},{6,4},{7,5},{8,14},{9,15},{10,... | collective-permute-start | bytes 393224 | tf_op jit(solution)/shard_map/gather_panel/ppermute | solution.py:343
  4.3 0.3 collective-permute-start.1
  4.6 0.7 collective-permute-start
  5.3 1.5 %collective-permute-start.3 = (f32[32,1024]{1,0:T(8,128)}, f32[32,1024]{1,0:T(8,128)S(1)}, u32[]{:S(2)}, u32[]{:S(2)}) collective-permute-start(f32[32,1024]{1,0:T(8,128)} %bitcast.11), channel_id=1, source_target_pairs={{0,1},{1,0},{2,3},{3,2},{4,5},{5,4},{6,7},{7,6},{8,9},{9,8},{10,11... | collective-permute-start | bytes 393224 | tf_op jit(solution)/shard_map/gather_panel/ppermute | solution.py:351
  6.8 1.4 %collective-permute-done.2.refs_3_ = f32[32,1024]{1,0:T(8,128)S(1)} collective-permute-done((f32[32,1024]{1,0:T(8,128)}, f32[32,1024]{1,0:T(8,128)S(1)}, u32[]{:S(2)}, u32[]{:S(2)}) %collective-permute-start.2) | collective-permute-done | bytes 131104 | tf_op jit(solution)/shard_map/gather_panel/ppermute | solution.py:343
  8.2 2.9 %collective-permute-start.6 = (f32[32,1024]{1,0:T(8,128)S(1)}, f32[32,1024]{1,0:T(8,128)S(1)}, u32[]{:S(2)}, u32[]{:S(2)}) collective-permute-start(f32[32,1024]{1,0:T(8,128)S(1)} %collective-permute-done.2.refs_3_), channel_id=1, source_target_pairs={{0,1},{1,0},{2,3},{3,2},{4,5},{5,4},{6,7},{7,6},{8,9},{9,8},{10,11... | collective-permute-start | bytes 393224 | tf_op jit(solution)/shard_map/gather_panel/ppermute | solution.py:351
  11.1 2.2 %collective-permute-start.5 = (f32[32,1024]{1,0:T(8,128)S(1)}, f32[32,1024]{1,0:T(8,128)S(1)}, u32[]{:S(2)}, u32[]{:S(2)}) collective-permute-start(f32[32,1024]{1,0:T(8,128)S(1)} %collective-permute-done.1.refs_2_), channel_id=1, source_target_pairs={{0,1},{1,0},{2,3},{3,2},{4,5},{5,4},{6,7},{7,6},{8,9},{9,8},{10,11... | collective-permute-start | bytes 393224 | tf_op jit(solution)/shard_map/gather_panel/ppermute | solution.py:351
  13.3 0.8 collective-permute-done.refs_1_
  14.1 0.6 collective-permute-start.4
  14.7 0.9 copy-done
  15.6 0.1 gather_panel.1.refs_0_
  15.8 0.1 pad_add_fusion.ids_ref
  15.9 6.1 %product.1 = (bf16[512,1024]{1,0:T(8,128)(2,1)}, f32[64,2176]{1,0:T(8,128)S(1)}, f32[64,2176]{1,0:T(8,128)S(1)}, f32[64,2176]{1,0:T(8,128)S(1)}, f32[64,2176]{1,0:T(8,128)S(1)}) custom-call(s32[3]{0:T(128)S(1)} %pad_add_fusion.ids_ref, f32[32,1024]{1,0:T(8,128)S(1)} %gather_panel.1.refs_0_, f32[32,1024]{1,0:T(8,128)S(1)} %collective-permute-done.refs_1_, ...), custom_call_target="tpu_custom_call" | custom-call | flops 3600000000 | bytes 8000000 | tf_op jit(solution)/shard_map/product/pallas_call | solution.py:255
  22.0 1.3 %collective-permute-start.7 = (f32[64,2176]{1,0:T(8,128)S(1)}, f32[64,2176]{1,0:T(8,128)S(1)}, u32[]{:S(2)}, u32[]{:S(2)}) collective-permute-start(f32[64,2176]{1,0:T(8,128)S(1)} %get-tuple-element.85), channel_id=1, source_target_pairs={{0,64},{8,72},{16,80},{24,88},{32,96},{40,104},{48,112},{56,120},{... | collective-permute-start | bytes 1671176 | tf_op jit(solution)/shard_map/sum_x/ppermute | solution.py:343
  23.3 2.5 %collective-permute-start.8 = (f32[64,2176]{1,0:T(8,128)S(1)}, f32[64,2176]{1,0:T(8,128)S(1)}, u32[]{:S(2)}, u32[]{:S(2)}) collective-permute-start(f32[64,2176]{1,0:T(8,128)S(1)} %get-tuple-element.86), channel_id=1, source_target_pairs={{0,128},{8,136},{16,144},{24,152},{32,160},{40,168},{48,176},{56,1... | collective-permute-start | bytes 1671176 | tf_op jit(solution)/shard_map/sum_x/ppermute | solution.py:343
  25.7 1.2 collective-permute-start.9
  26.9 10.4 %collective-permute-done.7.p1_ref = f32[64,2176]{1,0:T(8,128)S(1)} collective-permute-done((f32[64,2176]{1,0:T(8,128)S(1)}, f32[64,2176]{1,0:T(8,128)S(1)}, u32[]{:S(2)}, u32[]{:S(2)}) %collective-permute-start.7) | collective-permute-done | bytes 557088 | tf_op jit(solution)/shard_map/sum_x/ppermute | solution.py:343
  37.3 12.9 %collective-permute-done.8.p2_ref = f32[64,2176]{1,0:T(8,128)S(1)} collective-permute-done((f32[64,2176]{1,0:T(8,128)S(1)}, f32[64,2176]{1,0:T(8,128)S(1)}, u32[]{:S(2)}, u32[]{:S(2)}) %collective-permute-start.8) | collective-permute-done | bytes 557088 | tf_op jit(solution)/shard_map/sum_x/ppermute | solution.py:343
  50.2 0.1 sum_x.1
  50.4 34.1 %all-reduce.2 = (f32[16,128]{1,0:T(8,128)S(1)}, f32[16,128]{1,0:T(8,128)S(1)}, f32[16,128]{1,0:T(8,128)S(1)}, f32[16,128]{1,0:T(8,128)S(1)}, f32[16,128]{1,0:T(8...) all-reduce(f32[16,128]{1,0:T(8,128)S(1)} %get-tuple-element.88, ...), channel_id=1, replica_groups={{0,8,16,24,32,40,48,56},{64,72,80,88,96,104,112,120},{128,136,144,152,1..., use_global_device_ids=true, to_apply=%region_0.1 | all-reduce | flops 139264 | bytes 1114112 | tf_op jit(solution)/shard_map/sum_z/psum | solution.py:358
  84.5 0.1 sum_z.1
  84.6 1.7 %collective-permute-start.12 = (f32[64,128]{1,0:T(8,128)S(1)}, f32[64,128]{1,0:T(8,128)S(1)}, u32[]{:S(2)}, u32[]{:S(2)}) collective-permute-start(f32[64,128]{1,0:T(8,128)S(1)} %get-tuple-element.156), channel_id=1, source_target_pairs={{0,192},{8,200},{16,208},{24,216},{32,224},{40,232},{48,240},{56,2... | collective-permute-start | bytes 98312 | tf_op jit(solution)/shard_map/gather_gram/ppermute | solution.py:343
  86.3 1.1 collective-permute-start.11
  87.4 0.5 collective-permute-start.10
  87.9 2.2 %collective-permute-start.16 = (f32[64,2048]{1,0:T(8,128)S(1)}, f32[64,2048]{1,0:T(8,128)S(1)}, u32[]{:S(2)}, u32[]{:S(2)}) collective-permute-start(f32[64,2048]{1,0:T(8,128)S(1)} %get-tuple-element.159.a0_ref), channel_id=1, source_target_pairs={{0,192},{8,200},{16,208},{24,216},{32,224},{40,232},{48,240},{56,2... | collective-permute-start | bytes 1572872 | tf_op jit(solution)/shard_map/gather_x/ppermute | solution.py:343
  90.1 0.7 collective-permute-start.15
  90.8 0.7 collective-permute-done.10
  91.5 10.2 %collective-permute-start.13 = (f32[4,64,128]{2,1,0:T(8,128)S(1)}, f32[4,64,128]{2,1,0:T(8,128)S(1)}, u32[]{:S(2)}, u32[]{:S(2)}) collective-permute-start(f32[4,64,128]{2,1,0:T(8,128)S(1)} %pad_maximum_fusion.mine_ref), channel_id=1, source_target_pairs={{0,1},{1,0},{2,3},{3,2},{4,5},{5,4},{6,7},{7,6},{8,9},{9,8},{10,11... | collective-permute-start | bytes 393224 | tf_op jit(solution)/shard_map/gather_gram/ppermute | solution.py:361
  101.8 1.0 collective-permute-done.13.other_ref
  102.8 1.2 copy-done.1
  104.0 14.0 %factor.1 = (f32[256,256]{1,0:T(8,128)}, bf16[512,256]{1,0:T(8,128)(2,1)S(1)}, bf16[1024,256]{1,0:T(8,128)(2,1)S(1)}, bf16[1024,2048]{1,0:T(8,128)(2,1)S(1)}) custom-call(s32[3]{0:T(128)S(1)} %pad_add_fusion.ids_ref, f32[4,64,128]{2,1,0:T(8,128)S(1)} %pad_maximum_fusion.mine_ref, f32[4,64,128]{2,1,0:T(8,128)S(1)} %collective-permute-done.13.other_ref, ...), custom_call_target="tpu_custom_call" | custom-call | flops 3500000000 | bytes 1000 | tf_op jit(solution)/shard_map/factor/pallas_call | solution.py:273
  118.0 4.6 %update.1 = (f32[256,2048]{1,0:T(8,128)}, bf16[1024,2048]{1,0:T(8,128)(2,1)}) custom-call(s32[3]{0:T(128)S(1)} %pad_add_fusion.ids_ref, f32[64,2048]{1,0:T(8,128)S(1)} %get-tuple-element.159.a0_ref, f32[64,2048]{1,0:T(8,128)S(1)} %collective-permute-done.14.a1_ref, f32[64,2048]{1,0:T(8,128)S(1)} %collective-permute-done.15.a2_ref, ...), custom_call_target="tpu_custom_call" | custom-call | flops 3000000000 | bytes 12000000 | tf_op jit(solution)/shard_map/update/pallas_call | solution.py:291
  (15 shorter events, 0.0 us)
Async XLA Ops:
  0.6 7.6 %collective-permute-start.2 = (f32[32,1024]{1,0:T(8,128)}, f32[32,1024]{1,0:T(8,128)S(1)}, u32[]{:S(2)}, u32[]{:S(2)}) collective-permute-start(f32[32,1024]{1,0:T(8,128)} %bitcast.8), channel_id=1, source_target_pairs={{0,6},{1,7},{2,0},{3,1},{4,2},{5,3},{6,4},{7,5},{8,14},{9,15},{10,... | collective-permute-start | bytes 393224 | tf_op jit(solution)/shard_map/gather_panel/ppermute | solution.py:343
  4.3 6.9 %collective-permute-start.1 = (f32[32,1024]{1,0:T(8,128)}, f32[32,1024]{1,0:T(8,128)S(1)}, u32[]{:S(2)}, u32[]{:S(2)}) collective-permute-start(f32[32,1024]{1,0:T(8,128)} %bitcast.9), channel_id=1, source_target_pairs={{0,4},{1,5},{2,6},{3,7},{4,0},{5,1},{6,2},{7,3},{8,12},{9,13},{10,... | collective-permute-start | bytes 393224 | tf_op jit(solution)/shard_map/gather_panel/ppermute | solution.py:343
  4.6 9.5 %collective-permute-start = (f32[32,1024]{1,0:T(8,128)}, f32[32,1024]{1,0:T(8,128)S(1)}, u32[]{:S(2)}, u32[]{:S(2)}) collective-permute-start(f32[32,1024]{1,0:T(8,128)} %bitcast.10), channel_id=1, source_target_pairs={{0,2},{1,3},{2,4},{3,5},{4,6},{5,7},{6,0},{7,1},{8,10},{9,11},{10,... | collective-permute-start | bytes 393224 | tf_op jit(solution)/shard_map/gather_panel/ppermute | solution.py:343
  5.3 10.5 %collective-permute-start.3 = (f32[32,1024]{1,0:T(8,128)}, f32[32,1024]{1,0:T(8,128)S(1)}, u32[]{:S(2)}, u32[]{:S(2)}) collective-permute-start(f32[32,1024]{1,0:T(8,128)} %bitcast.11), channel_id=1, source_target_pairs={{0,1},{1,0},{2,3},{3,2},{4,5},{5,4},{6,7},{7,6},{8,9},{9,8},{10,11... | collective-permute-start | bytes 393224 | tf_op jit(solution)/shard_map/gather_panel/ppermute | solution.py:351
  8.2 7.7 %collective-permute-start.6 = (f32[32,1024]{1,0:T(8,128)S(1)}, f32[32,1024]{1,0:T(8,128)S(1)}, u32[]{:S(2)}, u32[]{:S(2)}) collective-permute-start(f32[32,1024]{1,0:T(8,128)S(1)} %collective-permute-done.2.refs_3_), channel_id=1, source_target_pairs={{0,1},{1,0},{2,3},{3,2},{4,5},{5,4},{6,7},{7,6},{8,9},{9,8},{10,11... | collective-permute-start | bytes 393224 | tf_op jit(solution)/shard_map/gather_panel/ppermute | solution.py:351
  11.1 4.7 %collective-permute-start.5 = (f32[32,1024]{1,0:T(8,128)S(1)}, f32[32,1024]{1,0:T(8,128)S(1)}, u32[]{:S(2)}, u32[]{:S(2)}) collective-permute-start(f32[32,1024]{1,0:T(8,128)S(1)} %collective-permute-done.1.refs_2_), channel_id=1, source_target_pairs={{0,1},{1,0},{2,3},{3,2},{4,5},{5,4},{6,7},{7,6},{8,9},{9,8},{10,11... | collective-permute-start | bytes 393224 | tf_op jit(solution)/shard_map/gather_panel/ppermute | solution.py:351
  14.1 1.8 %collective-permute-start.4 = (f32[32,1024]{1,0:T(8,128)S(1)}, f32[32,1024]{1,0:T(8,128)S(1)}, u32[]{:S(2)}, u32[]{:S(2)}) collective-permute-start(f32[32,1024]{1,0:T(8,128)S(1)} %collective-permute-done.refs_1_), channel_id=1, source_target_pairs={{0,1},{1,0},{2,3},{3,2},{4,5},{5,4},{6,7},{7,6},{8,9},{9,8},{10,11... | collective-permute-start | bytes 393224 | tf_op jit(solution)/shard_map/gather_panel/ppermute | solution.py:351
  14.7 0.9 copy-start
  22.0 15.3 %collective-permute-start.7 = (f32[64,2176]{1,0:T(8,128)S(1)}, f32[64,2176]{1,0:T(8,128)S(1)}, u32[]{:S(2)}, u32[]{:S(2)}) collective-permute-start(f32[64,2176]{1,0:T(8,128)S(1)} %get-tuple-element.85), channel_id=1, source_target_pairs={{0,64},{8,72},{16,80},{24,88},{32,96},{40,104},{48,112},{56,120},{... | collective-permute-start | bytes 1671176 | tf_op jit(solution)/shard_map/sum_x/ppermute | solution.py:343
  23.3 27.0 %collective-permute-start.8 = (f32[64,2176]{1,0:T(8,128)S(1)}, f32[64,2176]{1,0:T(8,128)S(1)}, u32[]{:S(2)}, u32[]{:S(2)}) collective-permute-start(f32[64,2176]{1,0:T(8,128)S(1)} %get-tuple-element.86), channel_id=1, source_target_pairs={{0,128},{8,136},{16,144},{24,152},{32,160},{40,168},{48,176},{56,1... | collective-permute-start | bytes 1671176 | tf_op jit(solution)/shard_map/sum_x/ppermute | solution.py:343
  25.7 24.5 %collective-permute-start.9 = (f32[64,2176]{1,0:T(8,128)S(1)}, f32[64,2176]{1,0:T(8,128)S(1)}, u32[]{:S(2)}, u32[]{:S(2)}) collective-permute-start(f32[64,2176]{1,0:T(8,128)S(1)} %get-tuple-element.87), channel_id=1, source_target_pairs={{0,192},{8,200},{16,208},{24,216},{32,224},{40,232},{48,240},{56,2... | collective-permute-start | bytes 1671176 | tf_op jit(solution)/shard_map/sum_x/ppermute | solution.py:343
  84.6 6.2 %collective-permute-start.12 = (f32[64,128]{1,0:T(8,128)S(1)}, f32[64,128]{1,0:T(8,128)S(1)}, u32[]{:S(2)}, u32[]{:S(2)}) collective-permute-start(f32[64,128]{1,0:T(8,128)S(1)} %get-tuple-element.156), channel_id=1, source_target_pairs={{0,192},{8,200},{16,208},{24,216},{32,224},{40,232},{48,240},{56,2... | collective-permute-start | bytes 98312 | tf_op jit(solution)/shard_map/gather_gram/ppermute | solution.py:343
  86.3 4.4 %collective-permute-start.11 = (f32[64,128]{1,0:T(8,128)S(1)}, f32[64,128]{1,0:T(8,128)S(1)}, u32[]{:S(2)}, u32[]{:S(2)}) collective-permute-start(f32[64,128]{1,0:T(8,128)S(1)} %get-tuple-element.156), channel_id=1, source_target_pairs={{0,128},{8,136},{16,144},{24,152},{32,160},{40,168},{48,176},{56,1... | collective-permute-start | bytes 98312 | tf_op jit(solution)/shard_map/gather_gram/ppermute | solution.py:343
  87.4 4.1 %collective-permute-start.10 = (f32[64,128]{1,0:T(8,128)S(1)}, f32[64,128]{1,0:T(8,128)S(1)}, u32[]{:S(2)}, u32[]{:S(2)}) collective-permute-start(f32[64,128]{1,0:T(8,128)S(1)} %get-tuple-element.156), channel_id=1, source_target_pairs={{0,64},{8,72},{16,80},{24,88},{32,96},{40,104},{48,112},{56,120},{... | collective-permute-start | bytes 98312 | tf_op jit(solution)/shard_map/gather_gram/ppermute | solution.py:343
  87.9 30.1 %collective-permute-start.16 = (f32[64,2048]{1,0:T(8,128)S(1)}, f32[64,2048]{1,0:T(8,128)S(1)}, u32[]{:S(2)}, u32[]{:S(2)}) collective-permute-start(f32[64,2048]{1,0:T(8,128)S(1)} %get-tuple-element.159.a0_ref), channel_id=1, source_target_pairs={{0,192},{8,200},{16,208},{24,216},{32,224},{40,232},{48,240},{56,2... | collective-permute-start | bytes 1572872 | tf_op jit(solution)/shard_map/gather_x/ppermute | solution.py:343
  90.1 27.9 %collective-permute-start.15 = (f32[64,2048]{1,0:T(8,128)S(1)}, f32[64,2048]{1,0:T(8,128)S(1)}, u32[]{:S(2)}, u32[]{:S(2)}) collective-permute-start(f32[64,2048]{1,0:T(8,128)S(1)} %get-tuple-element.159.a0_ref), channel_id=1, source_target_pairs={{0,128},{8,136},{16,144},{24,152},{32,160},{40,168},{48,176},{56,1... | collective-permute-start | bytes 1572872 | tf_op jit(solution)/shard_map/gather_x/ppermute | solution.py:343
  90.8 27.2 %collective-permute-start.14 = (f32[64,2048]{1,0:T(8,128)S(1)}, f32[64,2048]{1,0:T(8,128)S(1)}, u32[]{:S(2)}, u32[]{:S(2)}) collective-permute-start(f32[64,2048]{1,0:T(8,128)S(1)} %get-tuple-element.159.a0_ref), channel_id=1, source_target_pairs={{0,64},{8,72},{16,80},{24,88},{32,96},{40,104},{48,112},{56,120},{... | collective-permute-start | bytes 1572872 | tf_op jit(solution)/shard_map/gather_x/ppermute | solution.py:343
  91.5 11.2 %collective-permute-start.13 = (f32[4,64,128]{2,1,0:T(8,128)S(1)}, f32[4,64,128]{2,1,0:T(8,128)S(1)}, u32[]{:S(2)}, u32[]{:S(2)}) collective-permute-start(f32[4,64,128]{2,1,0:T(8,128)S(1)} %pad_maximum_fusion.mine_ref), channel_id=1, source_target_pairs={{0,1},{1,0},{2,3},{3,2},{4,5},{5,4},{6,7},{7,6},{8,9},{9,8},{10,11... | collective-permute-start | bytes 393224 | tf_op jit(solution)/shard_map/gather_gram/ppermute | solution.py:361
  102.8 1.2 copy-start.1

commit v9 on v8

--- a/solution.py
+++ b/solution.py
@@ -12,7 +12,7 @@
 HIGHEST = lax.Precision.HIGHEST
 NX, NZ = 4, 8
 B, ROWS, COLS, HALF, TILE = 256, 1024, 2048, 128, 256
-WIDE = 4
+WIDE = 2
 
 Z_GROUPS = [[x * NZ + z for z in range(NZ)] for x in range(NX)]
 SIBLING = [(c, c ^ 1) for c in range(8)]

time: 123 us -> 123 us (level)
  no operation moved by 1% of the time
where the time goes in v9:
time: 123 us
  blocking collectives  34.1 us (28%)
  starting transfers between devices  33.2 us (27%)
  waiting for transfers between devices  27.3 us (22%)
  Pallas kernels  24.8 us (20%)
  local copies, waits for them, and re-layouts  2.13 us (2%)
    psum x1, blocking collectives, local(): lax.psum(tuple(blocks), 'row', axis_index_groups=Z_GROUPS)  34.1 us
    ppermute x12, waiting for transfers between devices, shift(): lax.ppermute(pieces[k], axis, routes[k])  26.3 us
    ppermute x12, starting transfers between devices, shift(): lax.ppermute(pieces[k], axis, routes[k])  15.8 us
    pallas_call x1, Pallas kernels, factor(): pl.pallas_call(factor_kernel, out_shape=(array(B, B), array(2 * B, B, dty...  14 us
    ppermute x1, starting transfers between devices, local(): gram_other = lax.ppermute(gram_mine, 'col', SIBLING)  10.2 us
    ppermute x4, starting transfers between devices, local(): other = [lax.ppermute(piece, 'col', SIBLING) for piece in mine]  7.23 us
    pallas_call x1, Pallas kernels, product(): pl.pallas_call(product_kernel, out_shape=(array(2 * B, ROWS, dtype=BF16),...  6.09 us
    pallas_call x1, Pallas kernels, update(): pl.pallas_call(update_kernel, out_shape=(array(B, COLS), array(ROWS, COLS...  4.4 us
  transfers between devices with their start and end apart: 17, of which 6 were waited for; matrix products, arithmetic and copies ran while one was open for 0% of the time, Pallas kernels for 12%

profile of v9, /device:TPU:1, one launch (start us, length us, event | category | flops | bytes accessed | tf_op | source)
XLA Modules:
  0.0 122.6 jit_solution(9984166034553919408)
XLA Ops:
  0.6 3.6 %collective-permute-start.2 = (f32[32,1024]{1,0:T(8,128)}, f32[32,1024]{1,0:T(8,128)S(1)}, u32[]{:S(2)}, u32[]{:S(2)}) collective-permute-start(f32[32,1024]{1,0:T(8,128)} %bitcast.8), channel_id=1, source_target_pairs={{0,6},{1,7},{2,0},{3,1},{4,2},{5,3},{6,4},{7,5},{8,14},{9,15},{10,... | collective-permute-start | bytes 393224 | tf_op jit(solution)/shard_map/gather_panel/ppermute | solution.py:343
  4.3 0.3 collective-permute-start.1
  4.6 0.7 collective-permute-start
  5.3 1.5 %collective-permute-start.3 = (f32[32,1024]{1,0:T(8,128)}, f32[32,1024]{1,0:T(8,128)S(1)}, u32[]{:S(2)}, u32[]{:S(2)}) collective-permute-start(f32[32,1024]{1,0:T(8,128)} %bitcast.11), channel_id=1, source_target_pairs={{0,1},{1,0},{2,3},{3,2},{4,5},{5,4},{6,7},{7,6},{8,9},{9,8},{10,11... | collective-permute-start | bytes 393224 | tf_op jit(solution)/shard_map/gather_panel/ppermute | solution.py:351
  6.8 1.4 %collective-permute-done.2.refs_3_ = f32[32,1024]{1,0:T(8,128)S(1)} collective-permute-done((f32[32,1024]{1,0:T(8,128)}, f32[32,1024]{1,0:T(8,128)S(1)}, u32[]{:S(2)}, u32[]{:S(2)}) %collective-permute-start.2) | collective-permute-done | bytes 131104 | tf_op jit(solution)/shard_map/gather_panel/ppermute | solution.py:343
  8.2 2.9 %collective-permute-start.6 = (f32[32,1024]{1,0:T(8,128)S(1)}, f32[32,1024]{1,0:T(8,128)S(1)}, u32[]{:S(2)}, u32[]{:S(2)}) collective-permute-start(f32[32,1024]{1,0:T(8,128)S(1)} %collective-permute-done.2.refs_3_), channel_id=1, source_target_pairs={{0,1},{1,0},{2,3},{3,2},{4,5},{5,4},{6,7},{7,6},{8,9},{9,8},{10,11... | collective-permute-start | bytes 393224 | tf_op jit(solution)/shard_map/gather_panel/ppermute | solution.py:351
  11.1 2.2 %collective-permute-start.5 = (f32[32,1024]{1,0:T(8,128)S(1)}, f32[32,1024]{1,0:T(8,128)S(1)}, u32[]{:S(2)}, u32[]{:S(2)}) collective-permute-start(f32[32,1024]{1,0:T(8,128)S(1)} %collective-permute-done.1.refs_2_), channel_id=1, source_target_pairs={{0,1},{1,0},{2,3},{3,2},{4,5},{5,4},{6,7},{7,6},{8,9},{9,8},{10,11... | collective-permute-start | bytes 393224 | tf_op jit(solution)/shard_map/gather_panel/ppermute | solution.py:351
  13.3 0.8 collective-permute-done.refs_1_
  14.1 0.6 collective-permute-start.4
  14.7 0.9 copy-done
  15.6 0.1 gather_panel.1.refs_0_
  15.8 0.1 pad_add_fusion.ids_ref
  15.9 6.1 %product.1 = (bf16[512,1024]{1,0:T(8,128)(2,1)}, f32[64,2176]{1,0:T(8,128)S(1)}, f32[64,2176]{1,0:T(8,128)S(1)}, f32[64,2176]{1,0:T(8,128)S(1)}, f32[64,2176]{1,0:T(8,128)S(1)}) custom-call(s32[3]{0:T(128)S(1)} %pad_add_fusion.ids_ref, f32[32,1024]{1,0:T(8,128)S(1)} %gather_panel.1.refs_0_, f32[32,1024]{1,0:T(8,128)S(1)} %collective-permute-done.refs_1_, ...), custom_call_target="tpu_custom_call" | custom-call | flops 3600000000 | bytes 8000000 | tf_op jit(solution)/shard_map/product/pallas_call | solution.py:255
  22.0 1.3 %collective-permute-start.7 = (f32[64,2176]{1,0:T(8,128)S(1)}, f32[64,2176]{1,0:T(8,128)S(1)}, u32[]{:S(2)}, u32[]{:S(2)}) collective-permute-start(f32[64,2176]{1,0:T(8,128)S(1)} %get-tuple-element.85), channel_id=1, source_target_pairs={{0,64},{8,72},{16,80},{24,88},{32,96},{40,104},{48,112},{56,120},{... | collective-permute-start | bytes 1671176 | tf_op jit(solution)/shard_map/sum_x/ppermute | solution.py:343
  23.3 2.5 %collective-permute-start.8 = (f32[64,2176]{1,0:T(8,128)S(1)}, f32[64,2176]{1,0:T(8,128)S(1)}, u32[]{:S(2)}, u32[]{:S(2)}) collective-permute-start(f32[64,2176]{1,0:T(8,128)S(1)} %get-tuple-element.86), channel_id=1, source_target_pairs={{0,128},{8,136},{16,144},{24,152},{32,160},{40,168},{48,176},{56,1... | collective-permute-start | bytes 1671176 | tf_op jit(solution)/shard_map/sum_x/ppermute | solution.py:343
  25.7 1.2 collective-permute-start.9
  26.9 10.4 %collective-permute-done.7.p1_ref = f32[64,2176]{1,0:T(8,128)S(1)} collective-permute-done((f32[64,2176]{1,0:T(8,128)S(1)}, f32[64,2176]{1,0:T(8,128)S(1)}, u32[]{:S(2)}, u32[]{:S(2)}) %collective-permute-start.7) | collective-permute-done | bytes 557088 | tf_op jit(solution)/shard_map/sum_x/ppermute | solution.py:343
  37.3 12.9 %collective-permute-done.8.p2_ref = f32[64,2176]{1,0:T(8,128)S(1)} collective-permute-done((f32[64,2176]{1,0:T(8,128)S(1)}, f32[64,2176]{1,0:T(8,128)S(1)}, u32[]{:S(2)}, u32[]{:S(2)}) %collective-permute-start.8) | collective-permute-done | bytes 557088 | tf_op jit(solution)/shard_map/sum_x/ppermute | solution.py:343
  50.2 0.1 sum_x.1
  50.4 34.1 %all-reduce.2 = (f32[16,128]{1,0:T(8,128)S(1)}, f32[16,128]{1,0:T(8,128)S(1)}, f32[16,128]{1,0:T(8,128)S(1)}, f32[16,128]{1,0:T(8,128)S(1)}, f32[16,128]{1,0:T(8...) all-reduce(f32[16,128]{1,0:T(8,128)S(1)} %get-tuple-element.88, ...), channel_id=1, replica_groups={{0,8,16,24,32,40,48,56},{64,72,80,88,96,104,112,120},{128,136,144,152,1..., use_global_device_ids=true, to_apply=%region_0.1 | all-reduce | flops 139264 | bytes 1114112 | tf_op jit(solution)/shard_map/sum_z/psum | solution.py:358
  84.5 0.1 sum_z.1
  84.6 1.7 %collective-permute-start.12 = (f32[64,128]{1,0:T(8,128)S(1)}, f32[64,128]{1,0:T(8,128)S(1)}, u32[]{:S(2)}, u32[]{:S(2)}) collective-permute-start(f32[64,128]{1,0:T(8,128)S(1)} %get-tuple-element.156), channel_id=1, source_target_pairs={{0,192},{8,200},{16,208},{24,216},{32,224},{40,232},{48,240},{56,2... | collective-permute-start | bytes 98312 | tf_op jit(solution)/shard_map/gather_gram/ppermute | solution.py:343
  86.3 1.1 collective-permute-start.11
  87.4 0.5 collective-permute-start.10
  87.9 2.2 %collective-permute-start.16 = (f32[64,2048]{1,0:T(8,128)S(1)}, f32[64,2048]{1,0:T(8,128)S(1)}, u32[]{:S(2)}, u32[]{:S(2)}) collective-permute-start(f32[64,2048]{1,0:T(8,128)S(1)} %get-tuple-element.159.a0_ref), channel_id=1, source_target_pairs={{0,192},{8,200},{16,208},{24,216},{32,224},{40,232},{48,240},{56,2... | collective-permute-start | bytes 1572872 | tf_op jit(solution)/shard_map/gather_x/ppermute | solution.py:343
  90.1 0.7 collective-permute-start.15
  90.8 0.7 collective-permute-done.10
  91.5 10.2 %collective-permute-start.13 = (f32[4,64,128]{2,1,0:T(8,128)S(1)}, f32[4,64,128]{2,1,0:T(8,128)S(1)}, u32[]{:S(2)}, u32[]{:S(2)}) collective-permute-start(f32[4,64,128]{2,1,0:T(8,128)S(1)} %pad_maximum_fusion.mine_ref), channel_id=1, source_target_pairs={{0,1},{1,0},{2,3},{3,2},{4,5},{5,4},{6,7},{7,6},{8,9},{9,8},{10,11... | collective-permute-start | bytes 393224 | tf_op jit(solution)/shard_map/gather_gram/ppermute | solution.py:361
  101.8 1.0 collective-permute-done.13.other_ref
  102.8 1.2 copy-done.1
  104.0 14.0 %factor.1 = (f32[256,256]{1,0:T(8,128)}, bf16[512,256]{1,0:T(8,128)(2,1)S(1)}, bf16[1024,256]{1,0:T(8,128)(2,1)S(1)}, bf16[1024,2048]{1,0:T(8,128)(2,1)S(1)}) custom-call(s32[3]{0:T(128)S(1)} %pad_add_fusion.ids_ref, f32[4,64,128]{2,1,0:T(8,128)S(1)} %pad_maximum_fusion.mine_ref, f32[4,64,128]{2,1,0:T(8,128)S(1)} %collective-permute-done.13.other_ref, ...), custom_call_target="tpu_custom_call" | custom-call | flops 3500000000 | bytes 1000 | tf_op jit(solution)/shard_map/factor/pallas_call | solution.py:273
  118.0 4.4 %update.1 = (f32[256,2048]{1,0:T(8,128)}, bf16[1024,2048]{1,0:T(8,128)(2,1)}) custom-call(s32[3]{0:T(128)S(1)} %pad_add_fusion.ids_ref, f32[64,2048]{1,0:T(8,128)S(1)} %get-tuple-element.159.a0_ref, f32[64,2048]{1,0:T(8,128)S(1)} %collective-permute-done.14.a1_ref, f32[64,2048]{1,0:T(8,128)S(1)} %collective-permute-done.15.a2_ref, ...), custom_call_target="tpu_custom_call" | custom-call | flops 3000000000 | bytes 12000000 | tf_op jit(solution)/shard_map/update/pallas_call | solution.py:291
  (15 shorter events, 0.0 us)
Async XLA Ops:
  0.6 7.6 %collective-permute-start.2 = (f32[32,1024]{1,0:T(8,128)}, f32[32,1024]{1,0:T(8,128)S(1)}, u32[]{:S(2)}, u32[]{:S(2)}) collective-permute-start(f32[32,1024]{1,0:T(8,128)} %bitcast.8), channel_id=1, source_target_pairs={{0,6},{1,7},{2,0},{3,1},{4,2},{5,3},{6,4},{7,5},{8,14},{9,15},{10,... | collective-permute-start | bytes 393224 | tf_op jit(solution)/shard_map/gather_panel/ppermute | solution.py:343
  4.3 6.9 %collective-permute-start.1 = (f32[32,1024]{1,0:T(8,128)}, f32[32,1024]{1,0:T(8,128)S(1)}, u32[]{:S(2)}, u32[]{:S(2)}) collective-permute-start(f32[32,1024]{1,0:T(8,128)} %bitcast.9), channel_id=1, source_target_pairs={{0,4},{1,5},{2,6},{3,7},{4,0},{5,1},{6,2},{7,3},{8,12},{9,13},{10,... | collective-permute-start | bytes 393224 | tf_op jit(solution)/shard_map/gather_panel/ppermute | solution.py:343
  4.6 9.5 %collective-permute-start = (f32[32,1024]{1,0:T(8,128)}, f32[32,1024]{1,0:T(8,128)S(1)}, u32[]{:S(2)}, u32[]{:S(2)}) collective-permute-start(f32[32,1024]{1,0:T(8,128)} %bitcast.10), channel_id=1, source_target_pairs={{0,2},{1,3},{2,4},{3,5},{4,6},{5,7},{6,0},{7,1},{8,10},{9,11},{10,... | collective-permute-start | bytes 393224 | tf_op jit(solution)/shard_map/gather_panel/ppermute | solution.py:343
  5.3 10.5 %collective-permute-start.3 = (f32[32,1024]{1,0:T(8,128)}, f32[32,1024]{1,0:T(8,128)S(1)}, u32[]{:S(2)}, u32[]{:S(2)}) collective-permute-start(f32[32,1024]{1,0:T(8,128)} %bitcast.11), channel_id=1, source_target_pairs={{0,1},{1,0},{2,3},{3,2},{4,5},{5,4},{6,7},{7,6},{8,9},{9,8},{10,11... | collective-permute-start | bytes 393224 | tf_op jit(solution)/shard_map/gather_panel/ppermute | solution.py:351
  8.2 7.7 %collective-permute-start.6 = (f32[32,1024]{1,0:T(8,128)S(1)}, f32[32,1024]{1,0:T(8,128)S(1)}, u32[]{:S(2)}, u32[]{:S(2)}) collective-permute-start(f32[32,1024]{1,0:T(8,128)S(1)} %collective-permute-done.2.refs_3_), channel_id=1, source_target_pairs={{0,1},{1,0},{2,3},{3,2},{4,5},{5,4},{6,7},{7,6},{8,9},{9,8},{10,11... | collective-permute-start | bytes 393224 | tf_op jit(solution)/shard_map/gather_panel/ppermute | solution.py:351
  11.1 4.7 %collective-permute-start.5 = (f32[32,1024]{1,0:T(8,128)S(1)}, f32[32,1024]{1,0:T(8,128)S(1)}, u32[]{:S(2)}, u32[]{:S(2)}) collective-permute-start(f32[32,1024]{1,0:T(8,128)S(1)} %collective-permute-done.1.refs_2_), channel_id=1, source_target_pairs={{0,1},{1,0},{2,3},{3,2},{4,5},{5,4},{6,7},{7,6},{8,9},{9,8},{10,11... | collective-permute-start | bytes 393224 | tf_op jit(solution)/shard_map/gather_panel/ppermute | solution.py:351
  14.1 1.8 %collective-permute-start.4 = (f32[32,1024]{1,0:T(8,128)S(1)}, f32[32,1024]{1,0:T(8,128)S(1)}, u32[]{:S(2)}, u32[]{:S(2)}) collective-permute-start(f32[32,1024]{1,0:T(8,128)S(1)} %collective-permute-done.refs_1_), channel_id=1, source_target_pairs={{0,1},{1,0},{2,3},{3,2},{4,5},{5,4},{6,7},{7,6},{8,9},{9,8},{10,11... | collective-permute-start | bytes 393224 | tf_op jit(solution)/shard_map/gather_panel/ppermute | solution.py:351
  14.7 0.9 copy-start
  22.0 15.3 %collective-permute-start.7 = (f32[64,2176]{1,0:T(8,128)S(1)}, f32[64,2176]{1,0:T(8,128)S(1)}, u32[]{:S(2)}, u32[]{:S(2)}) collective-permute-start(f32[64,2176]{1,0:T(8,128)S(1)} %get-tuple-element.85), channel_id=1, source_target_pairs={{0,64},{8,72},{16,80},{24,88},{32,96},{40,104},{48,112},{56,120},{... | collective-permute-start | bytes 1671176 | tf_op jit(solution)/shard_map/sum_x/ppermute | solution.py:343
  23.3 27.0 %collective-permute-start.8 = (f32[64,2176]{1,0:T(8,128)S(1)}, f32[64,2176]{1,0:T(8,128)S(1)}, u32[]{:S(2)}, u32[]{:S(2)}) collective-permute-start(f32[64,2176]{1,0:T(8,128)S(1)} %get-tuple-element.86), channel_id=1, source_target_pairs={{0,128},{8,136},{16,144},{24,152},{32,160},{40,168},{48,176},{56,1... | collective-permute-start | bytes 1671176 | tf_op jit(solution)/shard_map/sum_x/ppermute | solution.py:343
  25.7 24.5 %collective-permute-start.9 = (f32[64,2176]{1,0:T(8,128)S(1)}, f32[64,2176]{1,0:T(8,128)S(1)}, u32[]{:S(2)}, u32[]{:S(2)}) collective-permute-start(f32[64,2176]{1,0:T(8,128)S(1)} %get-tuple-element.87), channel_id=1, source_target_pairs={{0,192},{8,200},{16,208},{24,216},{32,224},{40,232},{48,240},{56,2... | collective-permute-start | bytes 1671176 | tf_op jit(solution)/shard_map/sum_x/ppermute | solution.py:343
  84.6 6.2 %collective-permute-start.12 = (f32[64,128]{1,0:T(8,128)S(1)}, f32[64,128]{1,0:T(8,128)S(1)}, u32[]{:S(2)}, u32[]{:S(2)}) collective-permute-start(f32[64,128]{1,0:T(8,128)S(1)} %get-tuple-element.156), channel_id=1, source_target_pairs={{0,192},{8,200},{16,208},{24,216},{32,224},{40,232},{48,240},{56,2... | collective-permute-start | bytes 98312 | tf_op jit(solution)/shard_map/gather_gram/ppermute | solution.py:343
  86.3 4.4 %collective-permute-start.11 = (f32[64,128]{1,0:T(8,128)S(1)}, f32[64,128]{1,0:T(8,128)S(1)}, u32[]{:S(2)}, u32[]{:S(2)}) collective-permute-start(f32[64,128]{1,0:T(8,128)S(1)} %get-tuple-element.156), channel_id=1, source_target_pairs={{0,128},{8,136},{16,144},{24,152},{32,160},{40,168},{48,176},{56,1... | collective-permute-start | bytes 98312 | tf_op jit(solution)/shard_map/gather_gram/ppermute | solution.py:343
  87.4 4.1 %collective-permute-start.10 = (f32[64,128]{1,0:T(8,128)S(1)}, f32[64,128]{1,0:T(8,128)S(1)}, u32[]{:S(2)}, u32[]{:S(2)}) collective-permute-start(f32[64,128]{1,0:T(8,128)S(1)} %get-tuple-element.156), channel_id=1, source_target_pairs={{0,64},{8,72},{16,80},{24,88},{32,96},{40,104},{48,112},{56,120},{... | collective-permute-start | bytes 98312 | tf_op jit(solution)/shard_map/gather_gram/ppermute | solution.py:343
  87.9 30.1 %collective-permute-start.16 = (f32[64,2048]{1,0:T(8,128)S(1)}, f32[64,2048]{1,0:T(8,128)S(1)}, u32[]{:S(2)}, u32[]{:S(2)}) collective-permute-start(f32[64,2048]{1,0:T(8,128)S(1)} %get-tuple-element.159.a0_ref), channel_id=1, source_target_pairs={{0,192},{8,200},{16,208},{24,216},{32,224},{40,232},{48,240},{56,2... | collective-permute-start | bytes 1572872 | tf_op jit(solution)/shard_map/gather_x/ppermute | solution.py:343
  90.1 27.9 %collective-permute-start.15 = (f32[64,2048]{1,0:T(8,128)S(1)}, f32[64,2048]{1,0:T(8,128)S(1)}, u32[]{:S(2)}, u32[]{:S(2)}) collective-permute-start(f32[64,2048]{1,0:T(8,128)S(1)} %get-tuple-element.159.a0_ref), channel_id=1, source_target_pairs={{0,128},{8,136},{16,144},{24,152},{32,160},{40,168},{48,176},{56,1... | collective-permute-start | bytes 1572872 | tf_op jit(solution)/shard_map/gather_x/ppermute | solution.py:343
  90.8 27.2 %collective-permute-start.14 = (f32[64,2048]{1,0:T(8,128)S(1)}, f32[64,2048]{1,0:T(8,128)S(1)}, u32[]{:S(2)}, u32[]{:S(2)}) collective-permute-start(f32[64,2048]{1,0:T(8,128)S(1)} %get-tuple-element.159.a0_ref), channel_id=1, source_target_pairs={{0,64},{8,72},{16,80},{24,88},{32,96},{40,104},{48,112},{56,120},{... | collective-permute-start | bytes 1572872 | tf_op jit(solution)/shard_map/gather_x/ppermute | solution.py:343
  91.5 11.2 %collective-permute-start.13 = (f32[4,64,128]{2,1,0:T(8,128)S(1)}, f32[4,64,128]{2,1,0:T(8,128)S(1)}, u32[]{:S(2)}, u32[]{:S(2)}) collective-permute-start(f32[4,64,128]{2,1,0:T(8,128)S(1)} %pad_maximum_fusion.mine_ref), channel_id=1, source_target_pairs={{0,1},{1,0},{2,3},{3,2},{4,5},{5,4},{6,7},{7,6},{8,9},{9,8},{10,11... | collective-permute-start | bytes 393224 | tf_op jit(solution)/shard_map/gather_gram/ppermute | solution.py:361
  102.8 1.2 copy-start.1
